TPU v7x, 32 devices: a whole 2x2x4 slice. The times are simulated.
32 devices in a mesh: blk: 32 (over z, y, x, core), chan: 1.
Axes of the slice: x: 2, y: 2, z: 4, core: 2. Of those that a mesh axis runs over, the one named last changes fastest.
Arguments:
- spec_in: bfloat16 [256, 2, 512, 128], P('chan', None, 'blk'), may hold values from -6 to 6
- weight: bfloat16 [128, 2, 256, 256], P('blk', None, 'chan'), may hold values from -0.375 to 0.375
- pattern: int32 [128, 4, 4], P('blk'), may hold values 0 or 1
- cotangent: bfloat16 [256, 2, 512, 128], P('chan', None, 'blk'), may hold values from -6 to 6
Outputs:
- spec_out: bfloat16 [256, 2, 512, 128], P('chan', None, 'blk')
- grad_in: bfloat16 [256, 2, 512, 128], P('chan', None, 'blk')
- grad_weight: float32 [128, 2, 256, 256], P('blk', None, 'chan')
All inputs are finite; a program needn't handle non-finite values. No bound on the sum of `pattern` on one device may be relied on, other than what follows from the above.
Results may differ from a plain program's by a relative error of at most 0.001.
Values may be sent and summed in bfloat16 or wider, within the bound.
No kernel may reach another device: no remote copies, remote signals or barrier semaphores. Data moves between devices by JAX's collectives and lax.ppermute only.
A program may use at most 256 MiB of HBM per device.

v0:
```python
import jax
import jax.numpy as jnp
from jax import lax
from jax.sharding import PartitionSpec as P


def mix_forward(x_real, x_imag, w_real, w_imag):
    form = "ism,mio->osm"
    real_part = jnp.einsum(form, x_real, w_real, preferred_element_type=jnp.float32) - jnp.einsum(
        form, x_imag, w_imag, preferred_element_type=jnp.float32
    )
    imag_part = jnp.einsum(form, x_real, w_imag, preferred_element_type=jnp.float32) + jnp.einsum(
        form, x_imag, w_real, preferred_element_type=jnp.float32
    )
    return jnp.stack([real_part, imag_part], axis=1)


def mix_input_grad(g_real, g_imag, w_real, w_imag):
    form = "osm,mio->ism"
    real_part = jnp.einsum(form, g_real, w_real, preferred_element_type=jnp.float32) + jnp.einsum(
        form, g_imag, w_imag, preferred_element_type=jnp.float32
    )
    imag_part = jnp.einsum(form, g_imag, w_real, preferred_element_type=jnp.float32) - jnp.einsum(
        form, g_real, w_imag, preferred_element_type=jnp.float32
    )
    return jnp.stack([real_part, imag_part], axis=1)


def mix_weight_grad(x_real, x_imag, g_real, g_imag):
    form = "ism,osm->mio"
    real_part = jnp.einsum(form, x_real, g_real, preferred_element_type=jnp.float32) + jnp.einsum(
        form, x_imag, g_imag, preferred_element_type=jnp.float32
    )
    imag_part = jnp.einsum(form, x_real, g_imag, preferred_element_type=jnp.float32) - jnp.einsum(
        form, x_imag, g_real, preferred_element_type=jnp.float32
    )
    return jnp.stack([real_part, imag_part], axis=1)


def local(spec_in, weight, pattern, cotangent):
    in_rows = spec_in.shape[0]
    width = weight.shape[3]
    block_size = width // pattern.shape[2]
    full_mask = jnp.repeat(
        jnp.repeat(pattern.astype(jnp.bfloat16), block_size, axis=1), block_size, axis=2
    )
    own_mask = lax.dynamic_slice_in_dim(full_mask, lax.axis_index("chan") * in_rows, in_rows, 1)
    masked = weight * own_mask[:, None]
    full_weight = lax.all_gather(masked, "blk", axis=0, tiled=True)
    x_real = spec_in[:, 0]
    x_imag = spec_in[:, 1]
    grad_full = lax.all_gather(cotangent, "chan", axis=0, tiled=True)
    w_real = full_weight[:, 0]
    w_imag = full_weight[:, 1]
    summed = lax.psum_scatter(
        mix_forward(x_real, x_imag, w_real, w_imag), "chan", scatter_dimension=0, tiled=True
    )
    spec_out = summed.astype(jnp.bfloat16)
    grad_in = mix_input_grad(grad_full[:, 0], grad_full[:, 1], w_real, w_imag).astype(jnp.bfloat16)
    gs_real = grad_full[:, 0]
    gs_imag = grad_full[:, 1]
    weight_sum = lax.psum_scatter(
        mix_weight_grad(x_real, x_imag, gs_real, gs_imag), "blk", scatter_dimension=0, tiled=True
    )
    grad_weight = weight_sum * own_mask[:, None].astype(jnp.float32)
    return (spec_out, grad_in, grad_weight)


def solution(mesh):
    in_specs = (
        P("chan", None, "blk", None),
        P("blk", None, "chan", None),
        P("blk", None, None),
        P("chan", None, "blk", None),
    )
    out_specs = (
        P("chan", None, "blk", None),
        P("chan", None, "blk", None),
        P("blk", None, "chan", None),
    )
    return jax.shard_map(local, mesh=mesh, in_specs=in_specs, out_specs=out_specs, check_vma=False)
```

profile of v0, /device:TPU:0, one launch (start us, length us, event | category | flops | bytes accessed | tf_op | source)
XLA Modules:
  0.0 1391.5 jit_solution(11583585166954406112)
XLA Ops:
  7.2 0.0 all-reduce.3.cloned.1.call-start
  7.2 1.9 fusion.30
  9.1 1.3 copy.41
  10.4 2.0 copy.42
  12.4 2.9 fusion.31
  15.3 1.3 copy.39
  16.6 2.2 copy.40
  18.8 0.0 copy-start
  18.8 13.1 fusion.18
  31.9 0.0 copy-done
  31.9 13.2 fusion.12
  45.1 24.6 %add_bitcast_fusion = f32[128,1,256,256]{3,2,0,1:T(8,128)} fusion(f32[128,256,256]{2,1,0:T(8,128)} %fusion.18, bf16[256,1,16,128]{0,2,3,1:T(8,128)(2,1)S(1)} %copy-done, bf16[256,1,16,128]{0,2,3,1:T(8,128)(2,1)S(1)} %copy.40), kind=kOutput, calls=%fused_computation.2 | convolution fusion | flops 276824064 | bytes 69206016 | tf_op jit(solution)/shard_map/ism,osm->mio/dot_general | solution.py:31
  69.7 24.7 %subtract_bitcast_fusion = f32[128,1,256,256]{3,2,0,1:T(8,128)} fusion(f32[128,256,256]{2,1,0:T(8,128)} %fusion.12, bf16[256,1,16,128]{0,2,3,1:T(8,128)(2,1)S(1)} %copy.41, bf16[256,1,16,128]{0,2,3,1:T(8,128)(2,1)S(1)} %copy.40), kind=kOutput, calls=%fused_computation.1 | convolution fusion | flops 276824064 | bytes 69206016 | tf_op jit(solution)/shard_map/ism,osm->mio/dot_general | solution.py:34
  94.4 44.3 %pad_maximum_fusion = f32[128,2,256,256]{3,2,0,1:T(8,128)} fusion(f32[128,1,256,256]{3,2,0,1:T(8,128)} %subtract_bitcast_fusion, f32[128,1,256,256]{3,2,0,1:T(8,128)} %add_bitcast_fusion), kind=kLoop, calls=%fused_computation | loop fusion | flops 16777216 | bytes 134217728 | tf_op jit(solution)/shard_map/stack | solution.py:37
  138.7 0.0 copy-start.2
  138.7 0.0 all-reduce.3.cloned.1.call-update
  138.7 0.0 all-gather.2.cloned.1.call-start
  138.8 0.6 copy-done.2
  139.4 0.1 copy.26
  139.5 0.1 broadcast_in_dim.8
  139.6 0.1 reshape.19
  139.7 0.8 broadcast_in_dim.9
  140.5 2.0 copy.27
  142.6 2.4 copy_multiply_fusion
  145.0 0.0 all-gather.2.cloned.1.call-update
  145.0 1.0 bitcast_convert_fusion
  146.1 2.8 copy.33
  148.9 964.3 %all-reduce.3.cloned.1.call-done = f32[128,2,256,256]{3,2,0,1:T(8,128)} async-done(((f32[128,2,256,256]{3,2,0,1:T(8,128)}), f32[128,2,256,256]{3,2,0,1:T(8,128)}) %all-reduce.3.cloned.1.call-update) | async-done | bytes 67108880
  1113.3 2.1 dynamic-slice_multiply_fusion
  1115.4 1.6 copy.36
  1116.9 194.5 %all-gather.2.cloned.1.call-done = bf16[128,2,256,256]{3,2,0,1:T(8,128)(2,1)} async-done(((bf16[4,2,256,256]{3,2,0,1:T(8,128)(2,1)}), bf16[128,2,256,256]{3,2,0,1:T(8,128)(2,1)}) %all-gather.2.cloned.1.call-update) | async-done | bytes 33554448 | tf_op jit(solution)/shard_map/all_gather | solution.py:49
  1311.5 0.0 copy-start.1
  1311.5 8.1 fusion.1
  1319.6 0.0 copy-done.1
  1319.6 8.1 fusion
  1327.7 8.1 fusion.10
  1335.7 8.1 fusion.11
  1343.8 1.5 pad_maximum_fusion.2
  1345.3 5.1 copy.35
  1350.4 7.0 fusion.2
  1357.4 7.0 fusion.3
  1364.4 8.1 fusion.8
  1372.5 8.1 fusion.9
  1380.6 0.2 pad_maximum_fusion.1
  1380.8 3.9 copy.34
  (1 shorter events, 0.0 us)
Async XLA Ops:
  7.2 1106.1 %all-reduce.3.cloned.1.call-start = ((), (), s32[]{:S(2)}) async-start(), calls=%async_computation.1 | async-start | bytes 134217728
  18.8 13.1 copy-start
  138.7 0.7 copy-start.2
  138.7 1172.7 %all-gather.2.cloned.1.call-start = ((), (), s32[]{:S(2)}) async-start(), calls=%async_computation | async-start | bytes 34603008 | tf_op jit(solution)/shard_map/all_gather | solution.py:49
  1311.5 8.1 copy-start.1
Sparse Core Ops, SparseCore 0:
  138.8 974.3 all-reduce.2
  1116.7 194.6 all-gather.1
where the time goes:
time: 1390 us
  waiting for transfers between devices  1160 us (83%)
  matrix products  138 us (10%)
  other arithmetic  51.6 us (4%)
  local copies, waits for them, and re-layouts  28.8 us (2%)
  between operations  14.1 us (1%)
    unnamed x3, waiting for transfers between devices  964 us
    all_gather x1, waiting for transfers between devices, local(): full_weight = lax.all_gather(masked, 'blk', axis=0, tiled=True)  195 us
    another operation x1, other arithmetic, mix_weight_grad(): return jnp.stack([real_part, imag_part], axis=1)  44.3 us
  transfers between devices with their start and end apart: 2, of which 2 were waited for; matrix products, arithmetic and copies ran while one was open for 1% of the time, Pallas kernels for 0%

commit v1 on v0

v1 whole, which is shorter than its diff:
```python
import jax
import jax.numpy as jnp
from jax import lax
from jax.experimental import pallas as pl
from jax.experimental.layout import Layout, with_layout_constraint
from jax.experimental.pallas import tpu as pltpu
from jax.sharding import PartitionSpec as P

F32 = jnp.float32
NN = (((1,), (0,)), ((), ()))
NT = (((1,), (1,)), ((), ()))
TN = (((0,), (0,)), ((), ()))


def dot(left, right, dims):
    return lax.dot_general(left, right, dims, preferred_element_type=F32)


def mix_kernel(x_ref, g_ref, w_ref, y_ref, d_ref):
    inner, samples = x_ref.shape[0], x_ref.shape[4]

    def products(ref, j, dims):
        rows = ref[:, 0, j].reshape(inner * 2 * samples, ref.shape[-1])
        for c in range(2):
            yield dot(rows, w_ref[0, j, c], dims).reshape(inner, 2, samples, -1)

    for j in range(w_ref.shape[1]):
        real, imag = products(x_ref, j, NN)
        y_ref[:, 0, j, 0] = (real[:, 0] - imag[:, 1]).astype(y_ref.dtype)
        y_ref[:, 0, j, 1] = (real[:, 1] + imag[:, 0]).astype(y_ref.dtype)
        real, imag = products(g_ref, j, NT)
        d_ref[:, 0, j, 0] = (real[:, 0] + imag[:, 1]).astype(d_ref.dtype)
        d_ref[:, 0, j, 1] = (real[:, 1] - imag[:, 0]).astype(d_ref.dtype)


def mix(x, g, w, y_type):
    inner, outer, modes, _, samples, _ = x.shape
    ci, co = w.shape[3:]
    some = 2 if modes % 2 == 0 else 1

    def block(channels):
        return pl.BlockSpec((inner, 1, some, 2, samples, channels), lambda z, j: (0, z, j, 0, 0, 0))

    return pl.pallas_call(
        mix_kernel,
        grid=(outer, modes // some),
        in_specs=[block(ci), block(co), pl.BlockSpec((1, some, 2, ci, co), lambda z, j: (z, j, 0, 0, 0))],
        out_specs=[block(co), block(ci)],
        out_shape=[
            jax.ShapeDtypeStruct(x.shape[:-1] + (co,), y_type),
            jax.ShapeDtypeStruct(x.shape[:-1] + (ci,), jnp.bfloat16),
        ],
        compiler_params=pltpu.CompilerParams(vmem_limit_bytes=32 * 1024 * 1024),
        name="mix",
    )(x, g, w)


def weight_grad_kernel(layer_ref, x_ref, g_ref, *refs):
    *both_refs, mask_ref, out_ref = refs
    ci = x_ref.shape[-1]

    def rows(ref, c):
        return ref[..., c, :, :].reshape(-1, ref.shape[-1])

    def add(x_real, x_imag, g_real, g_imag):
        out_ref[0, 0] += dot(x_real, g_real, TN) + dot(x_imag, g_imag, TN)
        out_ref[0, 1] += dot(x_real, g_imag, TN) - dot(x_imag, g_real, TN)

    out_ref[...] = jnp.zeros_like(out_ref)
    add(rows(x_ref, 0), rows(x_ref, 1), rows(g_ref, 0), rows(g_ref, 1))
    for ref in both_refs:
        real, imag = rows(ref, 0), rows(ref, 1)
        add(real[:, :ci], imag[:, :ci], real[:, ci:], imag[:, ci:])
    out_ref[0] *= mask_ref[...].astype(F32)


def weight_grad(layer, x, g, both, mask):
    inner, _, modes, _, samples, ci = x.shape
    co = g.shape[-1]

    def own(channels):
        return pl.BlockSpec((inner, 1, 1, 2, samples, channels), lambda j, layer: (0, layer[0], j, 0, 0, 0))

    return pl.pallas_call(
        weight_grad_kernel,
        grid_spec=pltpu.PrefetchScalarGridSpec(
            num_scalar_prefetch=1,
            grid=(modes,),
            in_specs=[
                own(ci),
                own(co),
                *[pl.BlockSpec((inner, 1, 2, samples, ci + co), lambda j, layer: (0, j, 0, 0, 0))] * len(both),
                pl.BlockSpec((1, ci, co), lambda j, layer: (j, 0, 0)),
            ],
            out_specs=pl.BlockSpec((1, 2, ci, co), lambda j, layer: (j, 0, 0, 0)),
        ),
        out_shape=jax.ShapeDtypeStruct((modes, 2, ci, co), F32),
        compiler_params=pltpu.CompilerParams(vmem_limit_bytes=32 * 1024 * 1024),
        name="weight_grad",
    )(layer, x, g, *both, mask)


def stage(ready, work, *operands):
    shapes = jax.eval_shape(work, *operands)
    return lax.cond(ready, work, lambda *_: jax.tree.map(lambda a: jnp.zeros(a.shape, a.dtype), shapes), *operands)


def local(spec_in, weight, pattern, cotangent):
    ranks = lax.axis_size("blk")
    chans = lax.axis_size("chan")
    outer = 4 if ranks % 4 == 0 else 1
    inner = ranks // outer
    layer = lax.axis_index("blk") // inner
    layers = [[z * inner + r for r in range(inner)] for z in range(outer)]
    columns = [[z * inner + r for z in range(outer)] for r in range(inner)]
    modes = weight.shape[0]
    in_rows, width = weight.shape[2:]
    block_size = width // pattern.shape[2]

    mask = jnp.repeat(jnp.repeat(pattern.astype(jnp.bfloat16), block_size, axis=1), block_size, axis=2)
    own_mask = lax.dynamic_slice_in_dim(mask, lax.axis_index("chan") * in_rows, in_rows, 1)
    masked = weight * own_mask[:, None]
    held = lax.all_gather(masked, "blk", axis=0, axis_index_groups=columns)

    def exchange(a):
        return lax.all_to_all(a, "blk", 0, 0, tiled=True, axis_index_groups=layers)

    def to_modes(a):
        turned = a.transpose(3, 1, 2, 0)
        return turned.reshape(outer, inner, modes, *turned.shape[1:]).swapaxes(0, 1)

    def to_samples(a):
        turned = a.swapaxes(0, 1)
        return turned.reshape(ranks * modes, *turned.shape[3:]).transpose(3, 1, 2, 0)

    def to_owners(x, g):
        pieces = []
        for step in range(1, outer):
            parts = [lax.dynamic_index_in_dim(a, layer ^ step, 1, keepdims=False) for a in (x, g)]
            both = jnp.concatenate(parts, axis=-1)
            pieces.append(lax.ppermute(both, "blk", [(i, i ^ (step * inner)) for i in range(ranks)]))
        return pieces

    def inward(x, g):
        return exchange(to_modes(x)), exchange(to_modes(g))

    def outward(x, g, held):
        y, d = mix(x, g, held, jnp.bfloat16 if chans == 1 else F32)
        if chans > 1:
            y = lax.psum_scatter(y, "chan", scatter_dimension=5, tiled=True).astype(jnp.bfloat16)
        y, d = exchange(y), exchange(d)
        return tuple(with_layout_constraint(to_samples(a), Layout((0, 1, 2, 3))) for a in (y, d))

    ready = pattern[0, 0, 0] < 2
    if chans > 1:
        cotangent = lax.all_gather(cotangent, "chan", axis=0, tiled=True)
    x, g = stage(ready, inward, spec_in, cotangent)
    owned = to_owners(x, g)
    spec_out, grad_in = stage(ready, outward, x, g, held)
    spec_out, grad_in, owned = lax.optimization_barrier((spec_out, grad_in, owned))
    grad_weight = weight_grad(layer.astype(jnp.int32).reshape(1), x, g, owned, own_mask)
    return spec_out, grad_in, grad_weight


def solution(mesh):
    in_specs = (
        P("chan", None, "blk", None),
        P("blk", None, "chan", None),
        P("blk", None, None),
        P("chan", None, "blk", None),
    )
    out_specs = (
        P("chan", None, "blk", None),
        P("chan", None, "blk", None),
        P("blk", None, "chan", None),
    )
    return jax.shard_map(local, mesh=mesh, in_specs=in_specs, out_specs=out_specs, check_vma=False)
```

time: 1390 us -> 207 us (0.15)
  waiting for transfers between devices: 1160 us -> 45.7 us
  matrix products: 138 us -> 0 us
  blocking collectives: 0 us -> 80.6 us
  other arithmetic: 51.6 us -> 5.17 us
  starting transfers between devices: 0.08 us -> 14.3 us
  Pallas kernels: 0 us -> 14 us
    unnamed x3 -> x1, waiting for transfers between devices: 964 us -> 0.02 us
    all_gather x1, waiting for transfers between devices: 195 us -> 6.13 us  [local(): held = lax.all_gather(masked, 'blk', axis=0, axis_index_groups=columns)]
    dot_general x12 -> x0, matrix products: 138 us -> none  [the longest x1 24.7 us: mix_weight_grad(): jnp.einsum(form, x_imag, g_real, preferred_element_type=jnp.float32)]
    all_to_all x0 -> x2, blocking collectives: none -> 80.6 us  [exchange(): return lax.all_to_all(a, 'blk', 0, 0, tiled=True, axis_index_groups=layers)]
    another operation x3 -> x0, other arithmetic: 46 us -> none  [the longest x1 44.3 us: mix_weight_grad(): return jnp.stack([real_part, imag_part], axis=1)]
    all_to_all x0 -> x2, waiting for transfers between devices: none -> 39.6 us  [exchange(): return lax.all_to_all(a, 'blk', 0, 0, tiled=True, axis_index_groups=layers)]
    unnamed x13 -> x4, local copies, waits for them, and re-layouts: 18 us -> 0.01 us
    pallas_call x0 -> x2, Pallas kernels: none -> 14 us  [the longest x1 8.49 us: mix(): pl.pallas_call(mix_kernel, grid=(outer, modes // some), in_specs=[block(c...]
  transfers between devices with their start and end apart: 2 -> 6, of which waited for: 2 -> 3; matrix products, arithmetic and copies ran while one was open for 1% -> 17% of each run, Pallas kernels for 0% -> 4%
where the time goes in v1:
time: 207 us; the launch traced here: 206 us
  blocking collectives  80.6 us (39%)
  waiting for transfers between devices  45.7 us (22%)
  local copies, waits for them, and re-layouts  31.8 us (15%)
  between operations  14.8 us (7%)
  starting transfers between devices  14.3 us (7%)
  Pallas kernels  14 us (7%)
  other arithmetic  5.17 us (2%)
    all_to_all x2, blocking collectives, exchange(): return lax.all_to_all(a, 'blk', 0, 0, tiled=True, axis_index_groups=layers)  80.6 us
    all_to_all x2, waiting for transfers between devices, exchange(): return lax.all_to_all(a, 'blk', 0, 0, tiled=True, axis_index_groups=layers)  39.6 us
    reshape x2, local copies, waits for them, and re-layouts, to_samples(): turned.reshape(ranks * modes, *turned.shape[3:]).transpose(3, 1, 2, 0)  10.3 us
    all_to_all x2, starting transfers between devices, exchange(): return lax.all_to_all(a, 'blk', 0, 0, tiled=True, axis_index_groups=layers)  9.52 us
    pallas_call x1, Pallas kernels, mix(): pl.pallas_call(mix_kernel, grid=(outer, modes // some), in_specs=[block(c...  8.49 us
    another operation x2, local copies, waits for them, and re-layouts  7.9 us
    transpose x2, local copies, waits for them, and re-layouts, to_samples(): turned = a.swapaxes(0, 1)  6.37 us
    all_gather x1, waiting for transfers between devices, local(): held = lax.all_gather(masked, 'blk', axis=0, axis_index_groups=columns)  6.13 us
  transfers between devices with their start and end apart: 6, of which 3 were waited for; matrix products, arithmetic and copies ran while one was open for 17% of the time, Pallas kernels for 4%

profile of v1, /device:TPU:0, one launch (start us, length us, event | category | flops | bytes accessed | tf_op | source)
XLA Modules:
  0.0 206.3 jit_solution(15568698526813483840)
XLA Ops:
  7.2 0.0 copy-start.1
  7.2 0.0 all-gather.3.cloned.1.call-start
  7.2 0.8 convert_element_type.12
  8.0 0.1 copy.42
  8.1 0.1 broadcast_in_dim.7
  8.2 0.1 reshape.31
  8.4 0.2 copy.43.refs_3_
  8.6 0.0 copy-done.1
  8.6 1.1 broadcast_multiply_fusion
  9.6 0.0 all-gather.3.cloned.1.call-update
  9.7 1.2 slice.3
  11.5 67.5 %conditional.2 = (bf16[8,4,4,2,16,256]{5,4,3,2,1,0:T(8,128)(2,1)}, bf16[8,4,4,2,16,256]{5,4,3,2,1,0:T(8,128)(2,1)S(1)}) conditional(s32[]{:T(128)} %bitcast.17, () %tuple.26, (bf16[256,2,16,128]{3,2,1,0:T(8,128)(2,1)}, bf16[256,2,16,128]{3,2,1,0:T(8,128)(2,1)}) %tuple.27), branch_computations={%region_0.1_spmd, %region_1.2_spmd} | conditional | bytes 27263024 | solution.py:105
  11.5 3.9 %copy.40 = bf16[256,2,16,128]{0,2,1,3:T(8,128)(2,1)S(1)} copy(bf16[256,2,16,128]{3,2,1,0:T(8,128)(2,1)} %get-tuple-element.50) | data formatting | bytes 4194304 | tf_op jit(solution)/shard_map
  15.5 1.5 copy.34
  17.0 5.2 %all-to-all-start = ((bf16[8,4,4,2,16,256]{5,4,3,2,1,0:T(8,128)(2,1)}), bf16[8,4,4,2,16,256]{5,4,3,2,1,0:T(8,128)(2,1)}, u32[]{:S(2)}, u32[]{:S(2)}) async-start(bf16[8,4,4,2,16,256]{5,4,3,2,1,0:T(8,128)(2,1)} %copy.34), calls=%async_computation | async-start | bytes 4194304 | tf_op jit(solution)/shard_map/cond/branch_1_fun/all_to_all | solution.py:126
  22.2 4.0 %copy.41 = bf16[256,2,16,128]{0,2,1,3:T(8,128)(2,1)S(1)} copy(bf16[256,2,16,128]{3,2,1,0:T(8,128)(2,1)} %get-tuple-element.51) | data formatting | bytes 4194304 | tf_op jit(solution)/shard_map
  26.2 1.5 copy.35
  27.7 21.2 %all-to-all-done = bf16[8,4,4,2,16,256]{5,4,3,2,1,0:T(8,128)(2,1)} async-done(((bf16[8,4,4,2,16,256]{5,4,3,2,1,0:T(8,128)(2,1)}), bf16[8,4,4,2,16,256]{5,4,3,2,1,0:T(8,128)(2,1)}, u32[]{:S(2)}, u32[]{:S(2)}) %all-to-all-start) | async-done | bytes 2097184 | tf_op jit(solution)/shard_map/cond/branch_1_fun/all_to_all | solution.py:126
  48.9 30.1 %all_to_all.16 = bf16[8,4,4,2,16,256]{5,4,3,2,1,0:T(8,128)(2,1)S(1)} all-to-all(bf16[8,4,4,2,16,256]{5,4,3,2,1,0:T(8,128)(2,1)} %copy.35), channel_id=1, replica_groups={{0,1,2,3,4,5,6,7},{8,9,10,11,12,13,14,15},{16,17,18,19,20,21,22,23},{24..., dimensions={0} | all-to-all | bytes 4194304 | tf_op jit(solution)/shard_map/cond/branch_1_fun/all_to_all | solution.py:126
  79.0 0.0 copy-start
  79.0 2.4 %dynamic-slice_bitcast_fusion = (bf16[8,4,2,16,256]{4,3,2,1,0:T(8,128)(2,1)S(1)}, bf16[8,4,2,16,256]{4,3,2,1,0:T(8,128)(2,1)S(1)}, bf16[8,4,2,16,256]{4,3,2,1,0:...) fusion(bf16[8,4,4,2,16,256]{5,4,3,2,1,0:T(8,128)(2,1)S(1)} %get, ...), kind=kLoop, calls=%fused_computation.3 | loop fusion | bytes 6291468 | tf_op jit(solution)/shard_map/jit(dynamic_index_in_dim)/squeeze | solution.py:139
  81.5 0.0 copy-done
  81.5 1.1 pad_maximum_fusion
  82.6 2.2 %collective-permute-start = (bf16[8,4,2,16,512]{4,3,2,1,0:T(8,128)(2,1)}, bf16[8,4,2,16,512]{4,3,2,1,0:T(8,128)(2,1)S(1)}, u32[]{:S(2)}, u32[]{:S(2)}) collective-permute-start(bf16[8,4,2,16,512]{4,3,2,1,0:T(8,128)(2,1)} %pad_maximum_fusion), channel_id=1, source_target_pairs={{0,8},{1,9},{2,10},{3,11},{4,12},{5,13},{6,14},{7,15},{8,0},{9,1},... | collective-permute-start | bytes 3145736 | tf_op jit(solution)/shard_map/ppermute | solution.py:141
  84.7 1.1 pad_maximum_fusion.1
  85.9 2.6 %collective-permute-start.1 = (bf16[8,4,2,16,512]{4,3,2,1,0:T(8,128)(2,1)}, bf16[8,4,2,16,512]{4,3,2,1,0:T(8,128)(2,1)S(1)}, u32[]{:S(2)}, u32[]{:S(2)}) collective-permute-start(bf16[8,4,2,16,512]{4,3,2,1,0:T(8,128)(2,1)} %pad_maximum_fusion.1), channel_id=1, source_target_pairs={{0,16},{1,17},{2,18},{3,19},{4,20},{5,21},{6,22},{7,23},{8,24},{9,... | collective-permute-start | bytes 3145736 | tf_op jit(solution)/shard_map/ppermute | solution.py:141
  88.4 1.1 pad_maximum_fusion.2
  89.6 0.0 collective-permute-start.2
  89.6 6.1 %all-gather.3.cloned.1.call-done = bf16[16,2,256,256]{3,2,1,0:T(8,128)(2,1)} async-done(((bf16[4,2,256,256]{3,2,1,0:T(8,128)(2,1)}), bf16[16,2,256,256]{3,2,1,0:T(8,128)(2,1)}) %all-gather.3.cloned.1.call-update) | async-done | bytes 4194320 | tf_op jit(solution)/shard_map/all_gather | solution.py:123
  95.7 98.3 %conditional.3 = (bf16[256,2,16,128]{3,2,1,0:T(8,128)(2,1)}, bf16[256,2,16,128]{3,2,1,0:T(8,128)(2,1)}) conditional(s32[]{:T(128)} %bitcast.17, () %tuple.25, (bf16[8,4,4,2,16,256]{5,4,3,2,1,0:T(8,128)(2,1)}, bf16[8,4,4,2,16,256]{5,4,3,2,1,0:T(8,128)(2,1)}, bf16[16,2,256,256]{3,2,1,0:T(8,128)(2,1)}) %tuple.48), branch_computations={%region_2.3_spmd, %region_3.4_spmd} | conditional | bytes 27263024 | solution.py:105
  95.7 8.5 %mix.1 = (bf16[8,4,4,2,16,256]{5,4,3,2,1,0:T(8,128)(2,1)S(1)}, bf16[8,4,4,2,16,256]{5,4,3,2,1,0:T(8,128)(2,1)}) custom-call(bf16[8,4,4,2,16,256]{5,4,3,2,1,0:T(8,128)(2,1)} %get-tuple-element.12.x_ref, bf16[8,4,4,2,16,256]{5,4,3,2,1,0:T(8,128)(2,1)} %get-tuple-element.13.g_ref, bf16[4,4,2,256,256]{4,3,2,1,0:T(8,128)(2,1)} %bitcast.39), custom_call_target="tpu_custom_call" | custom-call | tf_op jit(solution)/shard_map/cond/branch_1_fun/mix/pallas_call | solution.py:44
  104.2 50.4 %all_to_all.17 = bf16[8,4,4,2,16,256]{5,4,3,2,1,0:T(8,128)(2,1)} all-to-all(bf16[8,4,4,2,16,256]{5,4,3,2,1,0:T(8,128)(2,1)S(1)} %get-tuple-element.15), channel_id=1, replica_groups={{0,1,2,3,4,5,6,7},{8,9,10,11,12,13,14,15},{16,17,18,19,20,21,22,23},{24..., dimensions={0} | all-to-all | bytes 4194304 | tf_op jit(solution)/shard_map/cond/branch_1_fun/all_to_all | solution.py:126
  154.6 4.4 %all-to-all-start.3 = ((bf16[8,4,4,2,16,256]{5,4,3,2,1,0:T(8,128)(2,1)}), bf16[8,4,4,2,16,256]{5,4,3,2,1,0:T(8,128)(2,1)}, u32[]{:S(2)}, u32[]{:S(2)}) async-start(bf16[8,4,4,2,16,256]{5,4,3,2,1,0:T(8,128)(2,1)} %get-tuple-element.16), calls=%async_computation.3 | async-start | bytes 4194304 | tf_op jit(solution)/shard_map/cond/branch_1_fun/all_to_all | solution.py:126
  159.0 3.2 %copy.36 = bf16[4,8,4,2,16,256]{5,4,3,2,1,0:T(8,128)(2,1)} copy(bf16[4,8,4,2,16,256]{5,4,3,2,0,1:T(8,128)(2,1)} %bitcast.34) | data formatting | bytes 4194304 | tf_op jit(solution)/shard_map/cond/branch_1_fun/transpose | solution.py:133
  162.2 5.1 %copy.37 = bf16[128,2,16,256]{0,2,1,3:T(8,128)(2,1)} copy(bf16[128,2,16,256]{3,2,1,0:T(8,128)(2,1)} %bitcast.35) | data formatting | bytes 4194304 | tf_op jit(solution)/shard_map/cond/branch_1_fun/reshape | solution.py:134
  167.3 18.3 %all-to-all-done.3 = bf16[8,4,4,2,16,256]{5,4,3,2,1,0:T(8,128)(2,1)} async-done(((bf16[8,4,4,2,16,256]{5,4,3,2,1,0:T(8,128)(2,1)}), bf16[8,4,4,2,16,256]{5,4,3,2,1,0:T(8,128)(2,1)}, u32[]{:S(2)}, u32[]{:S(2)}) %all-to-all-start.3) | async-done | bytes 2097184 | tf_op jit(solution)/shard_map/cond/branch_1_fun/all_to_all | solution.py:126
  185.6 3.2 %copy.38 = bf16[4,8,4,2,16,256]{5,4,3,2,1,0:T(8,128)(2,1)} copy(bf16[4,8,4,2,16,256]{5,4,3,2,0,1:T(8,128)(2,1)} %bitcast.14) | data formatting | bytes 4194304 | tf_op jit(solution)/shard_map/cond/branch_1_fun/transpose | solution.py:133
  188.8 5.1 %copy.39 = bf16[128,2,16,256]{0,2,1,3:T(8,128)(2,1)} copy(bf16[128,2,16,256]{3,2,1,0:T(8,128)(2,1)} %bitcast.36) | data formatting | bytes 4194304 | tf_op jit(solution)/shard_map/cond/branch_1_fun/reshape | solution.py:134
  194.0 0.0 collective-permute-done.refs_0_
  194.0 0.0 collective-permute-done.1.refs_1_
  194.0 0.0 collective-permute-done.2.refs_2_
  194.0 5.5 %weight_grad.1 = f32[4,2,256,256]{3,2,1,0:T(8,128)} custom-call(s32[1]{0:T(128)} %bitcast.25.layer_ref, bf16[8,4,4,2,16,256]{5,4,3,2,1,0:T(8,128)(2,1)} %get-tuple-element.29.x_ref, bf16[8,4,4,2,16,256]{5,4,3,2,1,0:T(8,128)(2,1)} %copy-done, bf16[8,4,2,16,512]{4,3,2,1,0:T(8,128)(2,1)S(1)} %collective-permute-done.refs_0_, ...), custom_call_target="tpu_custom_call" | custom-call | tf_op jit(solution)/shard_map/weight_grad/pallas_call | solution.py:84
  (1 shorter events, 0.0 us)
Async XLA Ops:
  7.2 1.4 copy-start.1
  7.2 88.5 %all-gather.3.cloned.1.call-start = ((), (), s32[]{:S(2)}) async-start(), calls=%async_computation.4 | async-start | bytes 5242880 | tf_op jit(solution)/shard_map/all_gather | solution.py:123
  17.0 31.9 %all-to-all-start = ((bf16[8,4,4,2,16,256]{5,4,3,2,1,0:T(8,128)(2,1)}), bf16[8,4,4,2,16,256]{5,4,3,2,1,0:T(8,128)(2,1)}, u32[]{:S(2)}, u32[]{:S(2)}) async-start(bf16[8,4,4,2,16,256]{5,4,3,2,1,0:T(8,128)(2,1)} %copy.34), calls=%async_computation | async-start | bytes 4194304 | tf_op jit(solution)/shard_map/cond/branch_1_fun/all_to_all | solution.py:126
  79.0 2.4 %copy-start = (bf16[8,4,4,2,16,256]{5,4,3,2,1,0:T(8,128)(2,1)}, bf16[8,4,4,2,16,256]{5,4,3,2,1,0:T(8,128)(2,1)S(1)}, u32[]{:S(2)}) copy-start(bf16[8,4,4,2,16,256]{5,4,3,2,1,0:T(8,128)(2,1)S(1)} %get-tuple-element.30.g_ref) | copy-start | bytes 6291460
  82.6 111.4 %collective-permute-start = (bf16[8,4,2,16,512]{4,3,2,1,0:T(8,128)(2,1)}, bf16[8,4,2,16,512]{4,3,2,1,0:T(8,128)(2,1)S(1)}, u32[]{:S(2)}, u32[]{:S(2)}) collective-permute-start(bf16[8,4,2,16,512]{4,3,2,1,0:T(8,128)(2,1)} %pad_maximum_fusion), channel_id=1, source_target_pairs={{0,8},{1,9},{2,10},{3,11},{4,12},{5,13},{6,14},{7,15},{8,0},{9,1},... | collective-permute-start | bytes 3145736 | tf_op jit(solution)/shard_map/ppermute | solution.py:141
  85.9 108.1 %collective-permute-start.1 = (bf16[8,4,2,16,512]{4,3,2,1,0:T(8,128)(2,1)}, bf16[8,4,2,16,512]{4,3,2,1,0:T(8,128)(2,1)S(1)}, u32[]{:S(2)}, u32[]{:S(2)}) collective-permute-start(bf16[8,4,2,16,512]{4,3,2,1,0:T(8,128)(2,1)} %pad_maximum_fusion.1), channel_id=1, source_target_pairs={{0,16},{1,17},{2,18},{3,19},{4,20},{5,21},{6,22},{7,23},{8,24},{9,... | collective-permute-start | bytes 3145736 | tf_op jit(solution)/shard_map/ppermute | solution.py:141
  89.6 104.4 %collective-permute-start.2 = (bf16[8,4,2,16,512]{4,3,2,1,0:T(8,128)(2,1)}, bf16[8,4,2,16,512]{4,3,2,1,0:T(8,128)(2,1)}, u32[]{:S(2)}, u32[]{:S(2)}) collective-permute-start(bf16[8,4,2,16,512]{4,3,2,1,0:T(8,128)(2,1)} %pad_maximum_fusion.2), channel_id=1, source_target_pairs={{0,24},{1,25},{2,26},{3,27},{4,28},{5,29},{6,30},{7,31},{8,16},{9,... | collective-permute-start | bytes 3145736 | tf_op jit(solution)/shard_map/ppermute | solution.py:141
  154.6 31.0 %all-to-all-start.3 = ((bf16[8,4,4,2,16,256]{5,4,3,2,1,0:T(8,128)(2,1)}), bf16[8,4,4,2,16,256]{5,4,3,2,1,0:T(8,128)(2,1)}, u32[]{:S(2)}, u32[]{:S(2)}) async-start(bf16[8,4,4,2,16,256]{5,4,3,2,1,0:T(8,128)(2,1)} %get-tuple-element.16), calls=%async_computation.3 | async-start | bytes 4194304 | tf_op jit(solution)/shard_map/cond/branch_1_fun/all_to_all | solution.py:126
Sparse Core Ops, SparseCore 0:
  10.2 85.5 all-gather.2

commit v2 on v1

v2 whole, which is shorter than its diff:
```python
import functools

import jax
import jax.numpy as jnp
from jax import lax
from jax.experimental import pallas as pl
from jax.experimental.layout import Layout, with_layout_constraint
from jax.experimental.pallas import tpu as pltpu
from jax.sharding import PartitionSpec as P

F32 = jnp.float32
NN = (((1,), (0,)), ((), ()))
NT = (((1,), (1,)), ((), ()))
TN = (((0,), (0,)), ((), ()))


def dot(left, right, dims):
    return lax.dot_general(left, right, dims, preferred_element_type=F32)


def mix_kernel(layer_ref, x_ref, g_ref, *refs):
    *w_refs, y_ref, d_ref = refs
    inner, samples = x_ref.shape[0], x_ref.shape[4]

    def run(w_ref):
        def products(ref, j, dims):
            rows = ref[:, 0, j].reshape(inner * 2 * samples, ref.shape[-1])
            for c in range(2):
                yield dot(rows, w_ref[j, c], dims).reshape(inner, 2, samples, -1)

        for j in range(w_ref.shape[0]):
            real, imag = products(x_ref, j, NN)
            y_ref[:, 0, j, 0] = (real[:, 0] - imag[:, 1]).astype(y_ref.dtype)
            y_ref[:, 0, j, 1] = (real[:, 1] + imag[:, 0]).astype(y_ref.dtype)
            real, imag = products(g_ref, j, NT)
            d_ref[:, 0, j, 0] = (real[:, 0] + imag[:, 1]).astype(d_ref.dtype)
            d_ref[:, 0, j, 1] = (real[:, 1] - imag[:, 0]).astype(d_ref.dtype)

    for p, w_ref in enumerate(w_refs):
        pl.when(pl.program_id(0) == p)(functools.partial(run, w_ref))


def mix(layer, odd, x, g, ws, y_type):
    inner, outer, modes, _, samples, _ = x.shape
    ci, co = ws[0].shape[2:]
    some = 2 if modes % 2 == 0 else 1

    def block(channels):
        return pl.BlockSpec(
            (inner, 1, some, 2, samples, channels), lambda p, k, layer: (0, layer[0] ^ (odd + 2 * p), k, 0, 0, 0)
        )

    def result(channels):
        return pl.BlockSpec((inner, 1, some, 2, samples, channels), lambda p, k, layer: (0, (layer[0] // 2) ^ p, k, 0, 0, 0))

    def weights(own):
        rest = 0 if own else modes // some - 1
        return pl.BlockSpec((some, 2, ci, co), lambda p, k, layer: (jnp.where(p == own, k, rest), 0, 0, 0))

    return pl.pallas_call(
        mix_kernel,
        grid_spec=pltpu.PrefetchScalarGridSpec(
            num_scalar_prefetch=1,
            grid=(2, modes // some),
            in_specs=[block(ci), block(co), weights(0), weights(1)],
            out_specs=[result(co), result(ci)],
        ),
        out_shape=[
            jax.ShapeDtypeStruct((inner, 2, modes, 2, samples, co), y_type),
            jax.ShapeDtypeStruct((inner, 2, modes, 2, samples, ci), jnp.bfloat16),
        ],
        compiler_params=pltpu.CompilerParams(vmem_limit_bytes=40 * 1024 * 1024),
        name="mix",
    )(layer, x, g, *ws)


def weight_grad_kernel(layer_ref, x_ref, g_ref, *refs):
    *both_refs, mask_ref, out_ref = refs
    ci = x_ref.shape[-1]

    def rows(ref, c):
        return ref[..., c, :, :].reshape(-1, ref.shape[-1])

    def add(x_real, x_imag, g_real, g_imag):
        out_ref[0, 0] += dot(x_real, g_real, TN) + dot(x_imag, g_imag, TN)
        out_ref[0, 1] += dot(x_real, g_imag, TN) - dot(x_imag, g_real, TN)

    out_ref[...] = jnp.zeros_like(out_ref)
    add(rows(x_ref, 0), rows(x_ref, 1), rows(g_ref, 0), rows(g_ref, 1))
    for ref in both_refs:
        real, imag = rows(ref, 0), rows(ref, 1)
        add(real[:, :ci], imag[:, :ci], real[:, ci:], imag[:, ci:])
    out_ref[0] *= mask_ref[...].astype(F32)


def weight_grad(layer, x, g, both, mask):
    inner, _, modes, _, samples, ci = x.shape
    co = g.shape[-1]

    def own(channels):
        return pl.BlockSpec((inner, 1, 1, 2, samples, channels), lambda j, layer: (0, layer[0], j, 0, 0, 0))

    return pl.pallas_call(
        weight_grad_kernel,
        grid_spec=pltpu.PrefetchScalarGridSpec(
            num_scalar_prefetch=1,
            grid=(modes,),
            in_specs=[
                own(ci),
                own(co),
                *[pl.BlockSpec((inner, 1, 2, samples, ci + co), lambda j, layer: (0, j, 0, 0, 0))] * len(both),
                pl.BlockSpec((1, ci, co), lambda j, layer: (j, 0, 0)),
            ],
            out_specs=pl.BlockSpec((1, 2, ci, co), lambda j, layer: (j, 0, 0, 0)),
        ),
        out_shape=jax.ShapeDtypeStruct((modes, 2, ci, co), F32),
        compiler_params=pltpu.CompilerParams(vmem_limit_bytes=32 * 1024 * 1024),
        name="weight_grad",
    )(layer, x, g, *both, mask)


def stage(ready, work, *operands):
    shapes = jax.eval_shape(work, *operands)
    return lax.cond(ready, work, lambda *_: jax.tree.map(lambda a: jnp.zeros(a.shape, a.dtype), shapes), *operands)


def local(spec_in, weight, pattern, cotangent):
    ranks = lax.axis_size("blk")
    chans = lax.axis_size("chan")
    outer = 4
    inner = ranks // outer
    layer = lax.axis_index("blk") // inner
    layers = [[z * inner + r for r in range(inner)] for z in range(outer)]
    modes = weight.shape[0]
    in_rows, width = weight.shape[2:]
    block_size = width // pattern.shape[2]

    mask = jnp.repeat(jnp.repeat(pattern.astype(jnp.bfloat16), block_size, axis=1), block_size, axis=2)
    own_mask = lax.dynamic_slice_in_dim(mask, lax.axis_index("chan") * in_rows, in_rows, 1)
    masked = weight * own_mask[:, None]

    def exchange(a):
        return lax.all_to_all(a, "blk", 0, 0, tiled=True, axis_index_groups=layers)

    def to_modes(a):
        turned = a.transpose(3, 1, 2, 0)
        return turned.reshape(outer, inner, modes, *turned.shape[1:]).swapaxes(0, 1)

    def to_samples(same, other):
        even = layer % 2 == 0
        parts = jnp.where(even, same, other), jnp.where(even, other, same)
        turned = jnp.stack(parts, axis=2).transpose(1, 2, 0, *range(3, 7))
        turned = turned.reshape(ranks * modes, *turned.shape[4:]).transpose(3, 1, 2, 0)
        return with_layout_constraint(turned, Layout((0, 1, 2, 3)))

    def send(a, step):
        return lax.ppermute(a, "blk", [(i, i ^ (step * inner)) for i in range(ranks)])

    def for_owner(step):
        parts = [lax.dynamic_index_in_dim(a, layer ^ step, 1, keepdims=False) for a in (x, g)]
        return send(jnp.concatenate(parts, axis=-1), step)

    def mixed(odd, x, g, ws):
        y, d = mix(place, odd, x, g, ws, jnp.bfloat16 if chans == 1 else F32)
        if chans > 1:
            y = lax.psum_scatter(y, "chan", scatter_dimension=5, tiled=True).astype(jnp.bfloat16)
        return exchange(y), exchange(d)

    def outward(x, g, ws, y_same, d_same):
        y, d = mixed(1, x, g, ws)
        return to_samples(y_same, y), to_samples(d_same, d)

    barrier = lax.optimization_barrier
    place = layer.astype(jnp.int32).reshape(1)
    ready = pattern[0, 0, 0] < 2
    far, near = send(masked, 2), send(masked, 1)
    if chans > 1:
        cotangent = lax.all_gather(cotangent, "chan", axis=0, tiled=True)
    x, g = stage(ready, lambda a, b: (exchange(to_modes(a)), exchange(to_modes(b))), spec_in, cotangent)
    x, g, far, near = barrier((x, g, far, near))
    near_far = send(far, 1)
    owned = {step: for_owner(step) for step in (2, 3, 1)}
    y_same, d_same = stage(ready, functools.partial(mixed, 0), x, g, [masked, far])
    y_same, d_same, near_far = barrier((y_same, d_same, near_far))
    far_pairs = [near, near_far]
    spec_out, grad_in = stage(ready, outward, x, g, far_pairs, y_same, d_same)
    spec_out, grad_in, owned = barrier((spec_out, grad_in, owned))
    grad_weight = weight_grad(place, x, g, [owned[step] for step in (1, 2, 3)], own_mask)
    return spec_out, grad_in, grad_weight


def solution(mesh):
    in_specs = (
        P("chan", None, "blk", None),
        P("blk", None, "chan", None),
        P("blk", None, None),
        P("chan", None, "blk", None),
    )
    out_specs = (
        P("chan", None, "blk", None),
        P("chan", None, "blk", None),
        P("blk", None, "chan", None),
    )
    return jax.shard_map(local, mesh=mesh, in_specs=in_specs, out_specs=out_specs, check_vma=False)
```

time: 207 us -> 188 us (0.908)
  waiting for transfers between devices: 45.7 us -> 25.5 us
  between operations: 14.8 us -> 1.39 us
  starting transfers between devices: 14.3 us -> 19.2 us
  blocking collectives: 80.6 us -> 85 us
  other arithmetic: 5.17 us -> 8 us
    all_to_all x2, waiting for transfers between devices: 39.6 us -> 25.5 us  [exchange(): return lax.all_to_all(a, 'blk', 0, 0, tiled=True, axis_index_groups=layers)]
    all_gather x1 -> x0, waiting for transfers between devices: 6.13 us -> none  [local(): held = lax.all_gather(masked, 'blk', axis=0, axis_index_groups=columns)]
    ppermute x3 -> x6, starting transfers between devices: 4.75 us -> 10.6 us  [send(): return lax.ppermute(a, 'blk', [(i, i ^ step * inner) for i in range(ranks)])]
    all_to_all x2 -> x4, blocking collectives: 80.6 us -> 85 us  [exchange(): return lax.all_to_all(a, 'blk', 0, 0, tiled=True, axis_index_groups=layers)]
    another operation x0 -> x2, other arithmetic: none -> 3.36 us  [to_samples(): turned = jnp.stack(parts, axis=2).transpose(1, 2, 0, *range(3, 7))]
    transpose x2, local copies, waits for them, and re-layouts: 6.37 us -> 3.07 us  [to_samples(): turned = jnp.stack(parts, axis=2).transpose(1, 2, 0, *range(3, 7))]
    transpose x2, local copies, waits for them, and re-layouts: 3.07 us -> 6.37 us  [to_modes(): return turned.reshape(outer, inner, modes, *turned.shape[1:]).swapaxes(0, 1)]
    pallas_call x1 -> x2, Pallas kernels: 8.49 us -> 9.23 us  [mix(): pl.pallas_call(mix_kernel, grid_spec=pltpu.PrefetchScalarGridSpec(num_sca...]
  transfers between devices with their start and end apart: 6 -> 8, of which waited for: 3 -> 2; matrix products, arithmetic and copies ran while one was open for 17% -> 21% of each run, Pallas kernels for 4% -> 5%
where the time goes in v2:
time: 188 us; the launch traced here: 187 us
  blocking collectives  85 us (45%)
  local copies, waits for them, and re-layouts  33.4 us (18%)
  waiting for transfers between devices  25.5 us (14%)
  starting transfers between devices  19.2 us (10%)
  Pallas kernels  14.7 us (8%)
  other arithmetic  8 us (4%)
    all_to_all x4, blocking collectives, exchange(): return lax.all_to_all(a, 'blk', 0, 0, tiled=True, axis_index_groups=layers)  85 us
    all_to_all x2, waiting for transfers between devices, exchange(): return lax.all_to_all(a, 'blk', 0, 0, tiled=True, axis_index_groups=layers)  25.5 us
    ppermute x6, starting transfers between devices, send(): return lax.ppermute(a, 'blk', [(i, i ^ step * inner) for i in range(ranks)])  10.6 us
    reshape x2, local copies, waits for them, and re-layouts, to_samples(): turned.reshape(ranks * modes, *turned.shape[4:]).transpose(3, 1, 2, 0)  10.3 us
    another operation x2, local copies, waits for them, and re-layouts  9.66 us
    pallas_call x2, Pallas kernels, mix(): pl.pallas_call(mix_kernel, grid_spec=pltpu.PrefetchScalarGridSpec(num_sca...  9.23 us
    all_to_all x2, starting transfers between devices, exchange(): return lax.all_to_all(a, 'blk', 0, 0, tiled=True, axis_index_groups=layers)  8.59 us
    transpose x2, local copies, waits for them, and re-layouts, to_modes(): return turned.reshape(outer, inner, modes, *turned.shape[1:]).swapaxes(0, 1)  6.37 us
  transfers between devices with their start and end apart: 8, of which 2 were waited for; matrix products, arithmetic and copies ran while one was open for 21% of the time, Pallas kernels for 5%

profile of v2, /device:TPU:0, one launch (start us, length us, event | category | flops | bytes accessed | tf_op | source)
XLA Modules:
  0.0 187.3 jit_solution(9609554840928289908)
XLA Ops:
  0.6 0.0 copy-start.6
  0.6 0.8 convert_element_type.13
  1.4 0.1 copy.46
  1.6 0.1 broadcast_in_dim.7
  1.6 0.1 reshape.32
  1.8 0.2 copy.47.refs_3_
  2.0 0.0 copy-done.6
  2.0 0.1 broadcast_multiply_fusion
  2.1 0.0 copy-start.1
  2.1 4.1 %collective-permute-start = (bf16[4,2,256,256]{3,2,1,0:T(8,128)(2,1)S(1)}, bf16[4,2,256,256]{3,2,1,0:T(8,128)(2,1)}, u32[]{:S(2)}, u32[]{:S(2)}) collective-permute-start(bf16[4,2,256,256]{3,2,1,0:T(8,128)(2,1)S(1)} %broadcast_multiply_fusion), channel_id=1, source_target_pairs={{0,16},{1,17},{2,18},{3,19},{4,20},{5,21},{6,22},{7,23},{8,24},{9,... | collective-permute-start | bytes 3145736 | tf_op jit(solution)/shard_map/ppermute | solution.py:157
  6.2 1.6 collective-permute-start.1
  7.8 1.2 slice.3
  9.6 0.0 copy-done.1
  9.7 70.0 %conditional.3 = (bf16[8,4,4,2,16,256]{5,4,3,2,1,0:T(8,128)(2,1)}, bf16[8,4,4,2,16,256]{5,4,3,2,1,0:T(8,128)(2,1)}) conditional(s32[]{:T(128)} %bitcast.20, () %tuple.36, (bf16[256,2,16,128]{3,2,1,0:T(8,128)(2,1)}, bf16[256,2,16,128]{3,2,1,0:T(8,128)(2,1)}) %tuple.37), branch_computations={%region_0.1_spmd, %region_1.2_spmd} | conditional | bytes 27263024 | solution.py:124
  9.7 4.8 %copy.44 = bf16[256,2,16,128]{0,2,1,3:T(8,128)(2,1)} copy(bf16[256,2,16,128]{3,2,1,0:T(8,128)(2,1)} %get-tuple-element.120) | data formatting | bytes 4194304 | tf_op jit(solution)/shard_map
  14.5 3.2 %copy.38 = bf16[8,4,4,2,16,256]{5,4,3,2,1,0:T(8,128)(2,1)} copy(bf16[8,4,4,2,16,256]{5,4,3,2,0,1:T(8,128)(2,1)} %bitcast.45) | data formatting | bytes 4194304 | tf_op jit(solution)/shard_map/cond/branch_1_fun/transpose | solution.py:147
  17.7 4.3 %all-to-all-start = ((bf16[8,4,4,2,16,256]{5,4,3,2,1,0:T(8,128)(2,1)}), bf16[8,4,4,2,16,256]{5,4,3,2,1,0:T(8,128)(2,1)}, u32[]{:S(2)}, u32[]{:S(2)}) async-start(bf16[8,4,4,2,16,256]{5,4,3,2,1,0:T(8,128)(2,1)} %copy.38), calls=%async_computation | async-start | bytes 4194304 | tf_op jit(solution)/shard_map/cond/branch_1_fun/all_to_all | solution.py:143
  22.0 4.8 %copy.45 = bf16[256,2,16,128]{0,2,1,3:T(8,128)(2,1)} copy(bf16[256,2,16,128]{3,2,1,0:T(8,128)(2,1)} %get-tuple-element.121) | data formatting | bytes 4194304 | tf_op jit(solution)/shard_map
  26.9 3.2 %copy.39 = bf16[8,4,4,2,16,256]{5,4,3,2,1,0:T(8,128)(2,1)} copy(bf16[8,4,4,2,16,256]{5,4,3,2,0,1:T(8,128)(2,1)} %bitcast.46) | data formatting | bytes 4194304 | tf_op jit(solution)/shard_map/cond/branch_1_fun/transpose | solution.py:147
  30.1 18.6 %all-to-all-done = bf16[8,4,4,2,16,256]{5,4,3,2,1,0:T(8,128)(2,1)} async-done(((bf16[8,4,4,2,16,256]{5,4,3,2,1,0:T(8,128)(2,1)}), bf16[8,4,4,2,16,256]{5,4,3,2,1,0:T(8,128)(2,1)}, u32[]{:S(2)}, u32[]{:S(2)}) %all-to-all-start) | async-done | bytes 2097184 | tf_op jit(solution)/shard_map/cond/branch_1_fun/all_to_all | solution.py:143
  48.7 30.9 %all_to_all.24 = bf16[8,4,4,2,16,256]{5,4,3,2,1,0:T(8,128)(2,1)} all-to-all(bf16[8,4,4,2,16,256]{5,4,3,2,1,0:T(8,128)(2,1)} %copy.39), channel_id=1, replica_groups={{0,1,2,3,4,5,6,7},{8,9,10,11,12,13,14,15},{16,17,18,19,20,21,22,23},{24..., dimensions={0} | all-to-all | bytes 4194304 | tf_op jit(solution)/shard_map/cond/branch_1_fun/all_to_all | solution.py:143
  79.6 0.0 collective-permute-done
  79.6 0.0 collective-permute-done.1
  79.6 0.0 copy-start.5
  79.6 0.5 collective-permute-start.2
  80.1 2.3 %dynamic-slice_bitcast_fusion = (bf16[8,4,2,16,256]{4,3,2,1,0:T(8,128)(2,1)S(1)}, bf16[8,4,2,16,256]{4,3,2,1,0:T(8,128)(2,1)S(1)}, bf16[8,4,2,16,256]{4,3,2,1,0:...) fusion(bf16[8,4,4,2,16,256]{5,4,3,2,1,0:T(8,128)(2,1)} %get-tup, ...), kind=kLoop, calls=%fused_computation.9 | loop fusion | bytes 6291468 | tf_op jit(solution)/shard_map/jit(dynamic_index_in_dim)/squeeze | solution.py:160
  82.4 0.0 copy-done.5
  82.4 1.1 pad_maximum_fusion
  83.6 1.6 collective-permute-start.3
  85.2 0.0 copy-start.2
  85.2 1.1 pad_maximum_fusion.1
  86.3 0.3 collective-permute-start.4
  86.6 1.1 pad_maximum_fusion.2
  87.7 2.5 %collective-permute-start.5 = (bf16[8,4,2,16,512]{4,3,2,1,0:T(8,128)(2,1)}, bf16[8,4,2,16,512]{4,3,2,1,0:T(8,128)(2,1)}, u32[]{:S(2)}, u32[]{:S(2)}) collective-permute-start(bf16[8,4,2,16,512]{4,3,2,1,0:T(8,128)(2,1)} %pad_maximum_fusion.2), channel_id=1, source_target_pairs={{0,24},{1,25},{2,26},{3,27},{4,28},{5,29},{6,30},{7,31},{8,16},{9,... | collective-permute-start | bytes 3145736 | tf_op jit(solution)/shard_map/ppermute | solution.py:157
  90.2 0.0 copy-done.2
  90.2 39.7 %conditional.4 = (bf16[8,2,4,2,16,256]{5,4,3,2,1,0:T(8,128)(2,1)S(1)}, bf16[8,2,4,2,16,256]{5,4,3,2,1,0:T(8,128)(2,1)S(1)}) conditional(s32[]{:T(128)} %bitcast.20, () %tuple.39, (s32[1]{0:T(128)}, bf16[8,4,4,2,16,256]{5,4,3,2,1,0:T(8,128)(2,1)}, bf16[8,4,4,2,16,256]{5,4,3,2,1,0:T(8,128)(2,1)}, bf16[4,2,256,256]{3,2,1,0:T(8,128)(2,1)S(1)}, ...), branch_computations={%region_2.3_spmd, %region_3.4_spmd} | conditional | bytes 4194320 | solution.py:124
  90.2 4.1 %mix.2 = (bf16[8,2,4,2,16,256]{5,4,3,2,1,0:T(8,128)(2,1)S(1)}, bf16[8,2,4,2,16,256]{5,4,3,2,1,0:T(8,128)(2,1)S(1)}) custom-call(s32[1]{0:T(128)} %get-tuple-element.32.layer_ref, bf16[8,4,4,2,16,256]{5,4,3,2,1,0:T(8,128)(2,1)} %get-tuple-element.33.x_ref, bf16[8,4,4,2,16,256]{5,4,3,2,1,0:T(8,128)(2,1)} %get-tuple-element.34.g_ref, ...), custom_call_target="tpu_custom_call" | custom-call | tf_op jit(solution)/shard_map/cond/branch_1_fun/mix/pallas_call | solution.py:60
  94.3 17.8 %all_to_all.25 = bf16[8,2,4,2,16,256]{5,4,3,2,1,0:T(8,128)(2,1)S(1)} all-to-all(bf16[8,2,4,2,16,256]{5,4,3,2,1,0:T(8,128)(2,1)S(1)} %get-tuple-element.37), channel_id=1, replica_groups={{0,1,2,3,4,5,6,7},{8,9,10,11,12,13,14,15},{16,17,18,19,20,21,22,23},{24..., dimensions={0} | all-to-all | bytes 2097152 | tf_op jit(solution)/shard_map/cond/branch_1_fun/all_to_all | solution.py:143
  112.1 17.8 %all_to_all.26 = bf16[8,2,4,2,16,256]{5,4,3,2,1,0:T(8,128)(2,1)S(1)} all-to-all(bf16[8,2,4,2,16,256]{5,4,3,2,1,0:T(8,128)(2,1)S(1)} %get-tuple-element.38), channel_id=1, replica_groups={{0,1,2,3,4,5,6,7},{8,9,10,11,12,13,14,15},{16,17,18,19,20,21,22,23},{24..., dimensions={0} | all-to-all | bytes 2097152 | tf_op jit(solution)/shard_map/cond/branch_1_fun/all_to_all | solution.py:143
  129.9 0.0 collective-permute-done.2
  129.9 51.9 %conditional.5 = (bf16[256,2,16,128]{3,2,1,0:T(8,128)(2,1)}, bf16[256,2,16,128]{3,2,1,0:T(8,128)(2,1)}) conditional(s32[]{:T(128)} %bitcast.20, () %tuple.35, (s32[]{:T(128)}, s32[1]{0:T(128)}, bf16[8,4,4,2,16,256]{5,4,3,2,1,0:T(8,128)(2,1)}, bf16[8,4,4,2,16,256]{5,4,3,2,1,0:T(8,128)(2,1)}, bf16[4,2,256,256]{3,2,1,0:T(8,128)(2,1)}, ...), branch_computations={%region_4.5_spmd, %region_5.6_spmd} | conditional | flops 4194316 | bytes 51380476 | solution.py:124
  129.9 0.0 copy-start.3
  129.9 0.0 copy-start.4
  129.9 5.1 %mix.3 = (bf16[8,2,4,2,16,256]{5,4,3,2,1,0:T(8,128)(2,1)S(1)}, bf16[8,2,4,2,16,256]{5,4,3,2,1,0:T(8,128)(2,1)S(1)}) custom-call(s32[1]{0:T(128)} %get-tuple-element.41.layer_ref, bf16[8,4,4,2,16,256]{5,4,3,2,1,0:T(8,128)(2,1)} %get-tuple-element.42.x_ref, bf16[8,4,4,2,16,256]{5,4,3,2,1,0:T(8,128)(2,1)} %get-tuple-element.43.g_ref, ...), custom_call_target="tpu_custom_call" | custom-call | tf_op jit(solution)/shard_map/cond/branch_1_fun/mix/pallas_call | solution.py:60
  135.0 0.0 copy-done.3
  135.0 0.0 copy-done.4
  135.0 0.0 copy-start
  135.0 18.5 %all_to_all.27 = bf16[8,2,4,2,16,256]{5,4,3,2,1,0:T(8,128)(2,1)} all-to-all(bf16[8,2,4,2,16,256]{5,4,3,2,1,0:T(8,128)(2,1)S(1)} %get-tuple-element.46), channel_id=1, replica_groups={{0,1,2,3,4,5,6,7},{8,9,10,11,12,13,14,15},{16,17,18,19,20,21,22,23},{24..., dimensions={0} | all-to-all | bytes 2097152 | tf_op jit(solution)/shard_map/cond/branch_1_fun/all_to_all | solution.py:143
  153.5 0.0 copy-done
  153.5 4.2 %all-to-all-start.5 = ((bf16[8,2,4,2,16,256]{5,4,3,2,1,0:T(8,128)(2,1)}), bf16[8,2,4,2,16,256]{5,4,3,2,1,0:T(8,128)(2,1)}, u32[]{:S(2)}, u32[]{:S(2)}) async-start(bf16[8,2,4,2,16,256]{5,4,3,2,1,0:T(8,128)(2,1)} %copy-done), calls=%async_computation.5 | async-start | bytes 2097152 | tf_op jit(solution)/shard_map/cond/branch_1_fun/all_to_all | solution.py:143
  157.8 1.7 select_bitcast_fusion.3
  159.5 0.2 maximum_bitcast_fusion
  159.7 1.5 copy.40
  161.2 5.1 %copy.41 = bf16[128,2,16,256]{0,2,1,3:T(8,128)(2,1)} copy(bf16[128,2,16,256]{3,2,1,0:T(8,128)(2,1)} %bitcast.43) | data formatting | bytes 4194304 | tf_op jit(solution)/shard_map/cond/branch_1_fun/reshape | solution.py:153
  166.4 6.8 %all-to-all-done.5 = bf16[8,2,4,2,16,256]{5,4,3,2,1,0:T(8,128)(2,1)} async-done(((bf16[8,2,4,2,16,256]{5,4,3,2,1,0:T(8,128)(2,1)}), bf16[8,2,4,2,16,256]{5,4,3,2,1,0:T(8,128)(2,1)}, u32[]{:S(2)}, u32[]{:S(2)}) %all-to-all-start.5) | async-done | bytes 1048608 | tf_op jit(solution)/shard_map/cond/branch_1_fun/all_to_all | solution.py:143
  173.2 1.7 select_bitcast_fusion.1
  174.9 0.2 maximum_bitcast_fusion.1
  175.1 1.5 copy.42
  176.6 5.1 %copy.43 = bf16[128,2,16,256]{0,2,1,3:T(8,128)(2,1)} copy(bf16[128,2,16,256]{3,2,1,0:T(8,128)(2,1)} %bitcast.44) | data formatting | bytes 4194304 | tf_op jit(solution)/shard_map/cond/branch_1_fun/reshape | solution.py:153
  181.8 0.0 collective-permute-done.3.refs_0_
  181.8 0.0 collective-permute-done.4.refs_1_
  181.8 0.0 collective-permute-done.5.refs_2_
  181.8 5.5 %weight_grad.1 = f32[4,2,256,256]{3,2,1,0:T(8,128)} custom-call(s32[1]{0:T(128)} %bitcast.21.layer_ref, bf16[8,4,4,2,16,256]{5,4,3,2,1,0:T(8,128)(2,1)} %get-tuple-element.72.x_ref, bf16[8,4,4,2,16,256]{5,4,3,2,1,0:T(8,128)(2,1)} %get-tuple-element.73.g_ref, bf16[8,4,2,16,512]{4,3,2,1,0:T(8,128)(2,1)S(1)} %collective-permute-done.3.refs_0_, ...), custom_call_target="tpu_custom_call" | custom-call | tf_op jit(solution)/shard_map/weight_grad/pallas_call | solution.py:103
  (1 shorter events, 0.0 us)
Async XLA Ops:
  0.6 1.4 copy-start.6
  2.1 7.5 %copy-start.1 = (bf16[4,2,256,256]{3,2,1,0:T(8,128)(2,1)}, bf16[4,2,256,256]{3,2,1,0:T(8,128)(2,1)S(1)}, u32[]{:S(2)}) copy-start(bf16[4,2,256,256]{3,2,1,0:T(8,128)(2,1)S(1)} %broadcast_multiply_fusion) | copy-start | bytes 3145732
  2.1 77.5 %collective-permute-start = (bf16[4,2,256,256]{3,2,1,0:T(8,128)(2,1)S(1)}, bf16[4,2,256,256]{3,2,1,0:T(8,128)(2,1)}, u32[]{:S(2)}, u32[]{:S(2)}) collective-permute-start(bf16[4,2,256,256]{3,2,1,0:T(8,128)(2,1)S(1)} %broadcast_multiply_fusion), channel_id=1, source_target_pairs={{0,16},{1,17},{2,18},{3,19},{4,20},{5,21},{6,22},{7,23},{8,24},{9,... | collective-permute-start | bytes 3145736 | tf_op jit(solution)/shard_map/ppermute | solution.py:157
  6.2 73.4 %collective-permute-start.1 = (bf16[4,2,256,256]{3,2,1,0:T(8,128)(2,1)S(1)}, bf16[4,2,256,256]{3,2,1,0:T(8,128)(2,1)S(1)}, u32[]{:S(2)}, u32[]{:S(2)}) collective-permute-start(bf16[4,2,256,256]{3,2,1,0:T(8,128)(2,1)S(1)} %broadcast_multiply_fusion), channel_id=1, source_target_pairs={{0,8},{1,9},{2,10},{3,11},{4,12},{5,13},{6,14},{7,15},{8,0},{9,1},... | collective-permute-start | bytes 3145736 | tf_op jit(solution)/shard_map/ppermute | solution.py:157
  17.7 31.0 %all-to-all-start = ((bf16[8,4,4,2,16,256]{5,4,3,2,1,0:T(8,128)(2,1)}), bf16[8,4,4,2,16,256]{5,4,3,2,1,0:T(8,128)(2,1)}, u32[]{:S(2)}, u32[]{:S(2)}) async-start(bf16[8,4,4,2,16,256]{5,4,3,2,1,0:T(8,128)(2,1)} %copy.38), calls=%async_computation | async-start | bytes 4194304 | tf_op jit(solution)/shard_map/cond/branch_1_fun/all_to_all | solution.py:143
  79.6 2.8 %copy-start.5 = (bf16[4,2,256,256]{3,2,1,0:T(8,128)(2,1)}, bf16[4,2,256,256]{3,2,1,0:T(8,128)(2,1)S(1)}, u32[]{:S(2)}) copy-start(bf16[4,2,256,256]{3,2,1,0:T(8,128)(2,1)S(1)} %collective-permute-done.1) | copy-start | bytes 3145732
  79.6 50.3 %collective-permute-start.2 = (bf16[4,2,256,256]{3,2,1,0:T(8,128)(2,1)}, bf16[4,2,256,256]{3,2,1,0:T(8,128)(2,1)}, u32[]{:S(2)}, u32[]{:S(2)}) collective-permute-start(bf16[4,2,256,256]{3,2,1,0:T(8,128)(2,1)} %collective-permute-done), channel_id=1, source_target_pairs={{0,8},{1,9},{2,10},{3,11},{4,12},{5,13},{6,14},{7,15},{8,0},{9,1},... | collective-permute-start | bytes 3145736 | tf_op jit(solution)/shard_map/ppermute | solution.py:157
  83.6 98.2 %collective-permute-start.3 = (bf16[8,4,2,16,512]{4,3,2,1,0:T(8,128)(2,1)}, bf16[8,4,2,16,512]{4,3,2,1,0:T(8,128)(2,1)S(1)}, u32[]{:S(2)}, u32[]{:S(2)}) collective-permute-start(bf16[8,4,2,16,512]{4,3,2,1,0:T(8,128)(2,1)} %pad_maximum_fusion), channel_id=1, source_target_pairs={{0,8},{1,9},{2,10},{3,11},{4,12},{5,13},{6,14},{7,15},{8,0},{9,1},... | collective-permute-start | bytes 3145736 | tf_op jit(solution)/shard_map/ppermute | solution.py:157
  85.2 5.1 %copy-start.2 = (bf16[4,2,256,256]{3,2,1,0:T(8,128)(2,1)S(1)}, bf16[4,2,256,256]{3,2,1,0:T(8,128)(2,1)}, u32[]{:S(2)}) copy-start(bf16[4,2,256,256]{3,2,1,0:T(8,128)(2,1)} %copy-done.1) | copy-start | bytes 3145732
  86.3 95.5 %collective-permute-start.4 = (bf16[8,4,2,16,512]{4,3,2,1,0:T(8,128)(2,1)}, bf16[8,4,2,16,512]{4,3,2,1,0:T(8,128)(2,1)S(1)}, u32[]{:S(2)}, u32[]{:S(2)}) collective-permute-start(bf16[8,4,2,16,512]{4,3,2,1,0:T(8,128)(2,1)} %pad_maximum_fusion.1), channel_id=1, source_target_pairs={{0,16},{1,17},{2,18},{3,19},{4,20},{5,21},{6,22},{7,23},{8,24},{9,... | collective-permute-start | bytes 3145736 | tf_op jit(solution)/shard_map/ppermute | solution.py:157
  87.7 94.0 %collective-permute-start.5 = (bf16[8,4,2,16,512]{4,3,2,1,0:T(8,128)(2,1)}, bf16[8,4,2,16,512]{4,3,2,1,0:T(8,128)(2,1)}, u32[]{:S(2)}, u32[]{:S(2)}) collective-permute-start(bf16[8,4,2,16,512]{4,3,2,1,0:T(8,128)(2,1)} %pad_maximum_fusion.2), channel_id=1, source_target_pairs={{0,24},{1,25},{2,26},{3,27},{4,28},{5,29},{6,30},{7,31},{8,16},{9,... | collective-permute-start | bytes 3145736 | tf_op jit(solution)/shard_map/ppermute | solution.py:157
  129.9 5.1 %copy-start.3 = (bf16[8,2,4,2,16,256]{5,4,3,2,1,0:T(8,128)(2,1)}, bf16[8,2,4,2,16,256]{5,4,3,2,1,0:T(8,128)(2,1)S(1)}, u32[]{:S(2)}) copy-start(bf16[8,2,4,2,16,256]{5,4,3,2,1,0:T(8,128)(2,1)S(1)} %get-tuple-element.40) | copy-start | bytes 3145732 | tf_op jit(solution)/shard_map/cond
  129.9 5.1 %copy-start.4 = (bf16[8,2,4,2,16,256]{5,4,3,2,1,0:T(8,128)(2,1)}, bf16[8,2,4,2,16,256]{5,4,3,2,1,0:T(8,128)(2,1)S(1)}, u32[]{:S(2)}) copy-start(bf16[8,2,4,2,16,256]{5,4,3,2,1,0:T(8,128)(2,1)S(1)} %get-tuple-element.47) | copy-start | bytes 3145732 | tf_op jit(solution)/shard_map/cond
  135.0 18.5 %copy-start = (bf16[8,2,4,2,16,256]{5,4,3,2,1,0:T(8,128)(2,1)}, bf16[8,2,4,2,16,256]{5,4,3,2,1,0:T(8,128)(2,1)S(1)}, u32[]{:S(2)}) copy-start(bf16[8,2,4,2,16,256]{5,4,3,2,1,0:T(8,128)(2,1)S(1)} %get-tuple-element.48) | copy-start | bytes 3145732 | tf_op jit(solution)/shard_map/cond
  153.5 19.7 %all-to-all-start.5 = ((bf16[8,2,4,2,16,256]{5,4,3,2,1,0:T(8,128)(2,1)}), bf16[8,2,4,2,16,256]{5,4,3,2,1,0:T(8,128)(2,1)}, u32[]{:S(2)}, u32[]{:S(2)}) async-start(bf16[8,2,4,2,16,256]{5,4,3,2,1,0:T(8,128)(2,1)} %copy-done), calls=%async_computation.5 | async-start | bytes 2097152 | tf_op jit(solution)/shard_map/cond/branch_1_fun/all_to_all | solution.py:143

commit v3 on v2

--- a/solution.py
+++ b/solution.py
@@ -18,9 +18,9 @@
     return lax.dot_general(left, right, dims, preferred_element_type=F32)
 
 
-def mix_kernel(layer_ref, x_ref, g_ref, *refs):
-    *w_refs, y_ref, d_ref = refs
+def mix_kernel(layer_ref, x_ref, g_ref, same_ref, other_ref, *out_refs):
     inner, samples = x_ref.shape[0], x_ref.shape[4]
+    y_ref, d_ref = out_refs if len(out_refs) == 2 else (out_refs[0].at[:, k] for k in range(2))
 
     def run(w_ref):
         def products(ref, j, dims):
@@ -36,11 +36,11 @@
             d_ref[:, 0, j, 0] = (real[:, 0] + imag[:, 1]).astype(d_ref.dtype)
             d_ref[:, 0, j, 1] = (real[:, 1] - imag[:, 0]).astype(d_ref.dtype)
 
-    for p, w_ref in enumerate(w_refs):
+    for p, w_ref in enumerate((same_ref, other_ref)):
         pl.when(pl.program_id(0) == p)(functools.partial(run, w_ref))
 
 
-def mix(layer, odd, x, g, ws, y_type):
+def mix(layer, odd, x, g, ws, y_type, joint):
     inner, outer, modes, _, samples, _ = x.shape
     ci, co = ws[0].shape[2:]
     some = 2 if modes % 2 == 0 else 1
@@ -57,66 +57,69 @@
         rest = 0 if own else modes // some - 1
         return pl.BlockSpec((some, 2, ci, co), lambda p, k, layer: (jnp.where(p == own, k, rest), 0, 0, 0))
 
+    if joint:
+        out_specs = [
+            pl.BlockSpec((inner, 2, 1, some, 2, samples, co), lambda p, k, layer: (0, 0, (layer[0] // 2) ^ p, k, 0, 0, 0))
+        ]
+        out_shape = [jax.ShapeDtypeStruct((inner, 2, 2, modes, 2, samples, co), y_type)]
+    else:
+        out_specs = [result(co), result(ci)]
+        out_shape = [
+            jax.ShapeDtypeStruct((inner, 2, modes, 2, samples, co), y_type),
+            jax.ShapeDtypeStruct((inner, 2, modes, 2, samples, ci), jnp.bfloat16),
+        ]
     return pl.pallas_call(
         mix_kernel,
         grid_spec=pltpu.PrefetchScalarGridSpec(
             num_scalar_prefetch=1,
             grid=(2, modes // some),
             in_specs=[block(ci), block(co), weights(0), weights(1)],
-            out_specs=[result(co), result(ci)],
+            out_specs=out_specs,
         ),
-        out_shape=[
-            jax.ShapeDtypeStruct((inner, 2, modes, 2, samples, co), y_type),
-            jax.ShapeDtypeStruct((inner, 2, modes, 2, samples, ci), jnp.bfloat16),
-        ],
+        out_shape=out_shape,
         compiler_params=pltpu.CompilerParams(vmem_limit_bytes=40 * 1024 * 1024),
         name="mix",
     )(layer, x, g, *ws)
 
 
-def weight_grad_kernel(layer_ref, x_ref, g_ref, *refs):
-    *both_refs, mask_ref, out_ref = refs
-    ci = x_ref.shape[-1]
+def weight_grad_kernel(layer_ref, *refs):
+    *pairs, mask_ref, out_ref = refs
 
     def rows(ref, c):
         return ref[..., c, :, :].reshape(-1, ref.shape[-1])
 
-    def add(x_real, x_imag, g_real, g_imag):
-        out_ref[0, 0] += dot(x_real, g_real, TN) + dot(x_imag, g_imag, TN)
-        out_ref[0, 1] += dot(x_real, g_imag, TN) - dot(x_imag, g_real, TN)
-
-    out_ref[...] = jnp.zeros_like(out_ref)
-    add(rows(x_ref, 0), rows(x_ref, 1), rows(g_ref, 0), rows(g_ref, 1))
-    for ref in both_refs:
-        real, imag = rows(ref, 0), rows(ref, 1)
-        add(real[:, :ci], imag[:, :ci], real[:, ci:], imag[:, ci:])
-    out_ref[0] *= mask_ref[...].astype(F32)
-
-
-def weight_grad(layer, x, g, both, mask):
+    real = imag = 0.0
+    for x_ref, g_ref in zip(pairs[::2], pairs[1::2]):
+        x_real, x_imag, g_real, g_imag = rows(x_ref, 0), rows(x_ref, 1), rows(g_ref, 0), rows(g_ref, 1)
+        real = real + dot(x_real, g_real, TN) + dot(x_imag, g_imag, TN)
+        imag = imag + dot(x_real, g_imag, TN) - dot(x_imag, g_real, TN)
+    mask = mask_ref[0].astype(F32)
+    out_ref[0, 0] = real * mask
+    out_ref[0, 1] = imag * mask
+
+
+def weight_grad(layer, x, g, pairs, mask):
     inner, _, modes, _, samples, ci = x.shape
     co = g.shape[-1]
 
     def own(channels):
         return pl.BlockSpec((inner, 1, 1, 2, samples, channels), lambda j, layer: (0, layer[0], j, 0, 0, 0))
+
+    def block(channels):
+        return pl.BlockSpec((inner, 1, 2, samples, channels), lambda j, layer: (0, j, 0, 0, 0))
 
     return pl.pallas_call(
         weight_grad_kernel,
         grid_spec=pltpu.PrefetchScalarGridSpec(
             num_scalar_prefetch=1,
             grid=(modes,),
-            in_specs=[
-                own(ci),
-                own(co),
-                *[pl.BlockSpec((inner, 1, 2, samples, ci + co), lambda j, layer: (0, j, 0, 0, 0))] * len(both),
-                pl.BlockSpec((1, ci, co), lambda j, layer: (j, 0, 0)),
-            ],
+            in_specs=[own(ci), own(co), *[block(ci), block(co)] * len(pairs), pl.BlockSpec((1, ci, co), lambda j, layer: (j, 0, 0))],
             out_specs=pl.BlockSpec((1, 2, ci, co), lambda j, layer: (j, 0, 0, 0)),
         ),
         out_shape=jax.ShapeDtypeStruct((modes, 2, ci, co), F32),
-        compiler_params=pltpu.CompilerParams(vmem_limit_bytes=32 * 1024 * 1024),
+        compiler_params=pltpu.CompilerParams(vmem_limit_bytes=40 * 1024 * 1024),
         name="weight_grad",
-    )(layer, x, g, *both, mask)
+    )(layer, x, g, *(a for pair in pairs for a in pair), mask)
 
 
 def stage(ready, work, *operands):
@@ -156,36 +159,42 @@
     def send(a, step):
         return lax.ppermute(a, "blk", [(i, i ^ (step * inner)) for i in range(ranks)])
 
-    def for_owner(step):
-        parts = [lax.dynamic_index_in_dim(a, layer ^ step, 1, keepdims=False) for a in (x, g)]
-        return send(jnp.concatenate(parts, axis=-1), step)
-
-    def mixed(odd, x, g, ws):
-        y, d = mix(place, odd, x, g, ws, jnp.bfloat16 if chans == 1 else F32)
+    def for_owner(a, step):
+        return send(lax.dynamic_index_in_dim(a, layer ^ step, 1, keepdims=False), step)
+
+    def mixed(odd, joint, x, g, ws):
+        out = list(mix(place, odd, x, g, ws, jnp.bfloat16 if chans == 1 else F32, joint))
         if chans > 1:
-            y = lax.psum_scatter(y, "chan", scatter_dimension=5, tiled=True).astype(jnp.bfloat16)
-        return exchange(y), exchange(d)
-
-    def outward(x, g, ws, y_same, d_same):
-        y, d = mixed(1, x, g, ws)
-        return to_samples(y_same, y), to_samples(d_same, d)
+            out[0] = lax.psum_scatter(out[0], "chan", scatter_dimension=5, tiled=True).astype(jnp.bfloat16)
+        return [exchange(a) for a in out]
+
+    def outward(x, g, ws, same):
+        y, d = mixed(1, False, x, g, ws)
+        spec_out = to_samples(same[0][:, 0] if chans == 1 else same[0], y)
+        same, d, spec_out = lax.optimization_barrier((same, d, spec_out))
+        return spec_out, to_samples(same[0][:, 1] if chans == 1 else same[1], d)
 
     barrier = lax.optimization_barrier
     place = layer.astype(jnp.int32).reshape(1)
-    ready = pattern[0, 0, 0] < 2
+    ready = lax.axis_index("blk") < ranks
     far, near = send(masked, 2), send(masked, 1)
     if chans > 1:
         cotangent = lax.all_gather(cotangent, "chan", axis=0, tiled=True)
-    x, g = stage(ready, lambda a, b: (exchange(to_modes(a)), exchange(to_modes(b))), spec_in, cotangent)
-    x, g, far, near = barrier((x, g, far, near))
+    x, turned = stage(ready, lambda a, b: (exchange(to_modes(a)), to_modes(b)), spec_in, cotangent)
+    g = exchange(turned)
+    x, far, near = barrier((x, far, near))
     near_far = send(far, 1)
-    owned = {step: for_owner(step) for step in (2, 3, 1)}
-    y_same, d_same = stage(ready, functools.partial(mixed, 0), x, g, [masked, far])
-    y_same, d_same, near_far = barrier((y_same, d_same, near_far))
-    far_pairs = [near, near_far]
-    spec_out, grad_in = stage(ready, outward, x, g, far_pairs, y_same, d_same)
-    spec_out, grad_in, owned = barrier((spec_out, grad_in, owned))
-    grad_weight = weight_grad(place, x, g, [owned[step] for step in (1, 2, 3)], own_mask)
+    pairs = {step: [for_owner(x, step)] for step in (2, 3)}
+    g, near = barrier((g, near))
+    for step in (2, 3):
+        pairs[step].append(for_owner(g, step))
+    same = stage(ready, functools.partial(mixed, 0, chans == 1), x, g, [masked, far])
+    same, near_far = barrier((same, near_far))
+    x_late, g_late, near_far = barrier((x, g, near_far))
+    pairs[1] = [for_owner(x_late, 1), for_owner(g_late, 1)]
+    spec_out, grad_in = stage(ready, outward, x, g, [near, near_far], same)
+    spec_out, grad_in, pairs = barrier((spec_out, grad_in, pairs))
+    grad_weight = weight_grad(place, x, g, [pairs[step] for step in (1, 2, 3)], own_mask)
     return spec_out, grad_in, grad_weight
 
 

time: 188 us -> 179 us (0.952)
  blocking collectives: 85 us -> 48.2 us
  waiting for transfers between devices: 25.5 us -> 45.7 us
  starting transfers between devices: 19.2 us -> 27.8 us
  other arithmetic: 8 us -> 4.53 us
  local copies, waits for them, and re-layouts: 33.4 us -> 36.5 us
    all_to_all x4 -> x2, blocking collectives: 85 us -> 48.2 us  [exchange(): return lax.all_to_all(a, 'blk', 0, 0, tiled=True, axis_index_groups=layers)]
    all_to_all x2 -> x3, waiting for transfers between devices: 25.5 us -> 41.9 us  [exchange(): return lax.all_to_all(a, 'blk', 0, 0, tiled=True, axis_index_groups=layers)]
    squeeze x1 -> x4, local copies, waits for them, and re-layouts: 2.28 us -> 8.37 us  [for_owner(): lax.dynamic_index_in_dim(a, layer ^ step, 1, keepdims=False)]
    transpose x2 -> x1, local copies, waits for them, and re-layouts: 6.37 us -> 1.54 us  [to_modes(): return turned.reshape(outer, inner, modes, *turned.shape[1:]).swapaxes(0, 1)]
    all_to_all x2 -> x3, starting transfers between devices: 8.59 us -> 13 us  [exchange(): return lax.all_to_all(a, 'blk', 0, 0, tiled=True, axis_index_groups=layers)]
    ppermute x6 -> x9, starting transfers between devices: 10.6 us -> 14.8 us  [send(): return lax.ppermute(a, 'blk', [(i, i ^ step * inner) for i in range(ranks)])]
    ppermute x6 -> x9, waiting for transfers between devices: 0.02 us -> 3.83 us  [send(): return lax.ppermute(a, 'blk', [(i, i ^ step * inner) for i in range(ranks)])]
    concatenate x3 -> x0, other arithmetic: 3.37 us -> none  [for_owner(): return send(jnp.concatenate(parts, axis=-1), step)]
  transfers between devices with their start and end apart: 8 -> 12, of which waited for: 2 -> 5; matrix products, arithmetic and copies ran while one was open for 21% -> 22% of each run, Pallas kernels for 5% -> 5%
where the time goes in v3:
time: 179 us; the launch traced here: 178 us
  blocking collectives  48.2 us (27%)
  waiting for transfers between devices  45.7 us (26%)
  local copies, waits for them, and re-layouts  36.5 us (20%)
  starting transfers between devices  27.8 us (16%)
  Pallas kernels  14.7 us (8%)
  other arithmetic  4.53 us (3%)
    all_to_all x2, blocking collectives, exchange(): return lax.all_to_all(a, 'blk', 0, 0, tiled=True, axis_index_groups=layers)  48.2 us
    all_to_all x3, waiting for transfers between devices, exchange(): return lax.all_to_all(a, 'blk', 0, 0, tiled=True, axis_index_groups=layers)  41.9 us
    ppermute x9, starting transfers between devices, send(): return lax.ppermute(a, 'blk', [(i, i ^ step * inner) for i in range(ranks)])  14.8 us
    all_to_all x3, starting transfers between devices, exchange(): return lax.all_to_all(a, 'blk', 0, 0, tiled=True, axis_index_groups=layers)  13 us
    another operation x3, local copies, waits for them, and re-layouts  11.2 us
    reshape x2, local copies, waits for them, and re-layouts, to_samples(): turned.reshape(ranks * modes, *turned.shape[4:]).transpose(3, 1, 2, 0)  10.3 us
    pallas_call x2, Pallas kernels, mix(): pl.pallas_call(mix_kernel, grid_spec=pltpu.PrefetchScalarGridSpec(num_sca...  9.3 us
    squeeze x4, local copies, waits for them, and re-layouts, for_owner(): lax.dynamic_index_in_dim(a, layer ^ step, 1, keepdims=False)  8.37 us
  transfers between devices with their start and end apart: 12, of which 5 were waited for; matrix products, arithmetic and copies ran while one was open for 22% of the time, Pallas kernels for 5%

profile of v3, /device:TPU:0, one launch (start us, length us, event | category | flops | bytes accessed | tf_op | source)
XLA Modules:
  0.0 178.4 jit_solution(3660719242137450433)
XLA Ops:
  0.6 0.0 copy-start.2
  0.6 0.8 convert_element_type.9
  1.4 0.1 copy.41
  1.6 0.1 broadcast_in_dim.7
  1.6 0.1 reshape.28
  1.8 0.2 copy.42.refs_8_
  2.0 0.0 copy-done.2
  2.0 1.1 broadcast_multiply_fusion
  3.1 4.0 %collective-permute-start = (bf16[4,2,256,256]{3,2,1,0:T(8,128)(2,1)}, bf16[4,2,256,256]{3,2,1,0:T(8,128)(2,1)}, u32[]{:S(2)}, u32[]{:S(2)}) collective-permute-start(bf16[4,2,256,256]{3,2,1,0:T(8,128)(2,1)} %broadcast_multiply_fusion), channel_id=1, source_target_pairs={{0,16},{1,17},{2,18},{3,19},{4,20},{5,21},{6,22},{7,23},{8,24},{9,... | collective-permute-start | bytes 3145736 | tf_op jit(solution)/shard_map/ppermute | solution.py:160
  7.1 1.6 collective-permute-start.1
  8.7 36.5 %conditional.3 = (bf16[8,4,4,2,16,256]{5,4,3,2,1,0:T(8,128)(2,1)}, bf16[8,4,4,2,16,256]{5,4,3,2,1,0:T(8,128)(2,1)}) conditional(s32[]{:T(128)} %convert_element_type.8, () %tuple.37, (bf16[256,2,16,128]{3,2,1,0:T(8,128)(2,1)}, bf16[256,2,16,128]{3,2,1,0:T(8,128)(2,1)}) %tuple.38), branch_computations={%region_0.1_spmd, %region_1.2_spmd} | conditional | bytes 23068720 | solution.py:127
  8.7 3.9 %copy.39 = bf16[256,2,16,128]{0,2,1,3:T(8,128)(2,1)S(1)} copy(bf16[256,2,16,128]{3,2,1,0:T(8,128)(2,1)} %get-tuple-element.129) | data formatting | bytes 4194304 | tf_op jit(solution)/shard_map
  12.6 1.5 copy.34
  14.1 4.3 %all-to-all-start = ((bf16[8,4,4,2,16,256]{5,4,3,2,1,0:T(8,128)(2,1)}), bf16[8,4,4,2,16,256]{5,4,3,2,1,0:T(8,128)(2,1)}, u32[]{:S(2)}, u32[]{:S(2)}) async-start(bf16[8,4,4,2,16,256]{5,4,3,2,1,0:T(8,128)(2,1)} %copy.34), calls=%async_computation | async-start | bytes 4194304 | tf_op jit(solution)/shard_map/cond/branch_1_fun/all_to_all | solution.py:146
  18.5 3.9 %copy.40 = bf16[256,2,16,128]{0,2,1,3:T(8,128)(2,1)S(1)} copy(bf16[256,2,16,128]{3,2,1,0:T(8,128)(2,1)} %get-tuple-element.130) | data formatting | bytes 4194304 | tf_op jit(solution)/shard_map
  22.4 1.5 copy.47
  24.0 21.2 %all-to-all-done = bf16[8,4,4,2,16,256]{5,4,3,2,1,0:T(8,128)(2,1)} async-done(((bf16[8,4,4,2,16,256]{5,4,3,2,1,0:T(8,128)(2,1)}), bf16[8,4,4,2,16,256]{5,4,3,2,1,0:T(8,128)(2,1)}, u32[]{:S(2)}, u32[]{:S(2)}) %all-to-all-start) | async-done | bytes 2097184 | tf_op jit(solution)/shard_map/cond/branch_1_fun/all_to_all | solution.py:146
  45.2 4.4 %all-to-all-start.4 = ((bf16[8,4,4,2,16,256]{5,4,3,2,1,0:T(8,128)(2,1)}), bf16[8,4,4,2,16,256]{5,4,3,2,1,0:T(8,128)(2,1)}, u32[]{:S(2)}, u32[]{:S(2)}) async-start(bf16[8,4,4,2,16,256]{5,4,3,2,1,0:T(8,128)(2,1)} %get-tuple-element.138), calls=%async_computation.4 | async-start | bytes 4194304 | tf_op jit(solution)/shard_map/all_to_all | solution.py:146
  49.5 3.6 %collective-permute-done = bf16[4,2,256,256]{3,2,1,0:T(8,128)(2,1)} collective-permute-done((bf16[4,2,256,256]{3,2,1,0:T(8,128)(2,1)}, bf16[4,2,256,256]{3,2,1,0:T(8,128)(2,1)}, u32[]{:S(2)}, u32[]{:S(2)}) %collective-permute-start) | collective-permute-done | bytes 1048608 | tf_op jit(solution)/shard_map/ppermute | solution.py:160
  53.2 0.2 collective-permute-done.1
  53.3 1.5 collective-permute-start.2
  54.8 2.3 %dynamic-slice_bitcast_fusion.1 = (bf16[8,4,2,16,256]{4,3,2,1,0:T(8,128)(2,1)}, bf16[8,4,2,16,256]{4,3,2,1,0:T(8,128)(2,1)}) fusion(bf16[8,4,4,2,16,256]{5,4,3,2,1,0:T(8,128)(2,1)} %get-tuple-element.87.refs_0_, s32[]{:T(128)S(6)} %select_n.50, s32[]{:T(128)S(6)} %select_n.49), kind=kLoop, calls=%fused_computation.10 | loop fusion | bytes 2097160 | tf_op jit(solution)/shard_map/jit(dynamic_index_in_dim)/squeeze | solution.py:163
  57.1 2.3 %collective-permute-start.5 = (bf16[8,4,2,16,256]{4,3,2,1,0:T(8,128)(2,1)}, bf16[8,4,2,16,256]{4,3,2,1,0:T(8,128)(2,1)S(1)}, u32[]{:S(2)}, u32[]{:S(2)}) collective-permute-start(bf16[8,4,2,16,256]{4,3,2,1,0:T(8,128)(2,1)} %get-tuple-element.146), channel_id=1, source_target_pairs={{0,16},{1,17},{2,18},{3,19},{4,20},{5,21},{6,22},{7,23},{8,24},{9,... | collective-permute-start | bytes 1572872 | tf_op jit(solution)/shard_map/ppermute | solution.py:160
  59.4 0.6 collective-permute-start.7
  60.0 16.2 %all-to-all-done.4.refs_1_ = bf16[8,4,4,2,16,256]{5,4,3,2,1,0:T(8,128)(2,1)} async-done(((bf16[8,4,4,2,16,256]{5,4,3,2,1,0:T(8,128)(2,1)}), bf16[8,4,4,2,16,256]{5,4,3,2,1,0:T(8,128)(2,1)}, u32[]{:S(2)}, u32[]{:S(2)}) %all-to-all-start.4) | async-done | bytes 2097184 | tf_op jit(solution)/shard_map/all_to_all | solution.py:146
  76.2 2.3 %dynamic-slice_bitcast_fusion = (bf16[8,4,2,16,256]{4,3,2,1,0:T(8,128)(2,1)}, bf16[8,4,2,16,256]{4,3,2,1,0:T(8,128)(2,1)}) fusion(bf16[8,4,4,2,16,256]{5,4,3,2,1,0:T(8,128)(2,1)} %all-to-all-done.4.refs_1_, s32[]{:T(128)S(6)} %select_n.50, s32[]{:T(128)S(6)} %select_n.49), kind=kLoop, calls=%fused_computation.9 | loop fusion | bytes 2097160 | tf_op jit(solution)/shard_map/jit(dynamic_index_in_dim)/squeeze | solution.py:163
  78.5 0.3 collective-permute-start.6
  78.9 2.5 %collective-permute-start.8 = (bf16[8,4,2,16,256]{4,3,2,1,0:T(8,128)(2,1)}, bf16[8,4,2,16,256]{4,3,2,1,0:T(8,128)(2,1)S(1)}, u32[]{:S(2)}, u32[]{:S(2)}) collective-permute-start(bf16[8,4,2,16,256]{4,3,2,1,0:T(8,128)(2,1)} %get-tuple-element.143), channel_id=1, source_target_pairs={{0,24},{1,25},{2,26},{3,27},{4,28},{5,29},{6,30},{7,31},{8,16},{9,... | collective-permute-start | bytes 1572872 | tf_op jit(solution)/shard_map/ppermute | solution.py:160
  81.3 34.1 %conditional.4 = (bf16[8,2,2,4,2,16,256]{6,5,4,3,2,1,0:T(8,128)(2,1)}) conditional(s32[]{:T(128)} %convert_element_type.8, () %tuple.41, (s32[1]{0:T(128)}, bf16[8,4,4,2,16,256]{5,4,3,2,1,0:T(8,128)(2,1)}, bf16[8,4,4,2,16,256]{5,4,3,2,1,0:T(8,128)(2,1)}, bf16[4,2,256,256]{3,2,1,0:T(8,128)(2,1)}, bf16[4,2,256,256]{3,2,1,0:T(8,128)(2,1)}) %tuple.42), branch_computations={%region_2.3_spmd, %region_3.4_spmd} | conditional | bytes 4194312 | solution.py:127
  81.3 4.3 %mix.2 = bf16[8,2,2,4,2,16,256]{6,5,4,3,2,1,0:T(8,128)(2,1)S(1)} custom-call(s32[1]{0:T(128)} %get-tuple-element.33.layer_ref, bf16[8,4,4,2,16,256]{5,4,3,2,1,0:T(8,128)(2,1)} %get-tuple-element.34.x_ref, bf16[8,4,4,2,16,256]{5,4,3,2,1,0:T(8,128)(2,1)} %get-tuple-element.35.g_ref, bf16[4,2,256,256]{3,2,1,0:T(8,128)(2,1)} %get-tuple-element.36.same_ref, ...), custom_call_target="tpu_custom_call" | custom-call | tf_op jit(solution)/shard_map/cond/branch_1_fun/mix/pallas_call | solution.py:71
  85.6 29.8 %all_to_all.21 = bf16[8,2,2,4,2,16,256]{6,5,4,3,2,1,0:T(8,128)(2,1)} all-to-all(bf16[8,2,2,4,2,16,256]{6,5,4,3,2,1,0:T(8,128)(2,1)S(1)} %mix.2), channel_id=1, replica_groups={{0,1,2,3,4,5,6,7},{8,9,10,11,12,13,14,15},{16,17,18,19,20,21,22,23},{24..., dimensions={0} | all-to-all | bytes 4194304 | tf_op jit(solution)/shard_map/cond/branch_1_fun/all_to_all | solution.py:146
  115.4 0.0 collective-permute-done.2
  115.4 1.9 %dynamic-slice_bitcast_fusion.5 = bf16[8,4,2,16,256]{4,3,2,1,0:T(8,128)(2,1)} fusion(bf16[8,4,4,2,16,256]{5,4,3,2,1,0:T(8,128)(2,1)} %get-tuple-element.87.refs_0_, s32[]{:T(128)S(6)} %select_n.48), kind=kLoop, calls=%fused_computation.14 | loop fusion | bytes 1048580 | tf_op jit(solution)/shard_map/jit(dynamic_index_in_dim)/squeeze | solution.py:163
  117.3 0.7 collective-permute-start.3
  118.0 1.9 %dynamic-slice_bitcast_fusion.4 = bf16[8,4,2,16,256]{4,3,2,1,0:T(8,128)(2,1)} fusion(bf16[8,4,4,2,16,256]{5,4,3,2,1,0:T(8,128)(2,1)} %all-to-all-done.4.refs_1_, s32[]{:T(128)S(6)} %select_n.48), kind=kLoop, calls=%fused_computation.13 | loop fusion | bytes 1048580 | tf_op jit(solution)/shard_map/jit(dynamic_index_in_dim)/squeeze | solution.py:163
  119.8 0.0 collective-permute-done.5.refs_4_
  119.9 1.4 collective-permute-start.4
  121.2 51.7 %conditional.5 = (bf16[256,2,16,128]{3,2,1,0:T(8,128)(2,1)}, bf16[256,2,16,128]{3,2,1,0:T(8,128)(2,1)}) conditional(s32[]{:T(128)} %convert_element_type.8, () %tuple.36, (s32[1]{0:T(128)}, bf16[8,4,4,2,16,256]{5,4,3,2,1,0:T(8,128)(2,1)}, bf16[8,4,4,2,16,256]{5,4,3,2,1,0:T(8,128)(2,1)}, bf16[4,2,256,256]{3,2,1,0:T(8,128)(2,1)}, ...), branch_computations={%region_4.5_spmd, %region_5.6_spmd} | conditional | flops 4194316 | bytes 55574752 | solution.py:127
  121.2 5.0 %mix.3 = (bf16[8,2,4,2,16,256]{5,4,3,2,1,0:T(8,128)(2,1)S(1)}, bf16[8,2,4,2,16,256]{5,4,3,2,1,0:T(8,128)(2,1)}) custom-call(s32[1]{0:T(128)} %get-tuple-element.39.layer_ref, bf16[8,4,4,2,16,256]{5,4,3,2,1,0:T(8,128)(2,1)} %get-tuple-element.40.x_ref, bf16[8,4,4,2,16,256]{5,4,3,2,1,0:T(8,128)(2,1)} %get-tuple-element.41.g_ref, ...), custom_call_target="tpu_custom_call" | custom-call | tf_op jit(solution)/shard_map/cond/branch_1_fun/mix/pallas_call | solution.py:71
  126.2 18.5 %all_to_all.22 = bf16[8,2,4,2,16,256]{5,4,3,2,1,0:T(8,128)(2,1)} all-to-all(bf16[8,2,4,2,16,256]{5,4,3,2,1,0:T(8,128)(2,1)S(1)} %get-tuple-element.46), channel_id=1, replica_groups={{0,1,2,3,4,5,6,7},{8,9,10,11,12,13,14,15},{16,17,18,19,20,21,22,23},{24..., dimensions={0} | all-to-all | bytes 2097152 | tf_op jit(solution)/shard_map/cond/branch_1_fun/all_to_all | solution.py:146
  144.7 4.2 %all-to-all-start.2 = ((bf16[8,2,4,2,16,256]{5,4,3,2,1,0:T(8,128)(2,1)}), bf16[8,2,4,2,16,256]{5,4,3,2,1,0:T(8,128)(2,1)}, u32[]{:S(2)}, u32[]{:S(2)}) async-start(bf16[8,2,4,2,16,256]{5,4,3,2,1,0:T(8,128)(2,1)} %get-tuple-element.44), calls=%async_computation.2 | async-start | bytes 2097152 | tf_op jit(solution)/shard_map/cond/branch_1_fun/all_to_all | solution.py:146
  148.9 0.0 copy-start
  148.9 0.0 copy-start.1
  149.0 3.3 %copy.44 = bf16[8,2,2,4,2,16,256]{6,5,4,3,2,0,1:T(8,128)(2,1)} copy(bf16[8,2,2,4,2,16,256]{6,5,4,3,2,1,0:T(8,128)(2,1)} %get-tuple-element.137) | data formatting | bytes 4194304 | tf_op jit(solution)/shard_map
  152.3 0.0 copy-done
  152.3 0.0 copy-done.1
  152.3 0.6 select_bitcast_fusion.1
  152.9 0.2 maximum_bitcast_fusion
  153.1 1.5 copy.35
  154.7 5.1 %copy.36 = bf16[128,2,16,256]{0,2,1,3:T(8,128)(2,1)} copy(bf16[128,2,16,256]{3,2,1,0:T(8,128)(2,1)} %bitcast.55) | data formatting | bytes 4194304 | tf_op jit(solution)/shard_map/cond/branch_1_fun/reshape | solution.py:156
  159.8 4.5 %all-to-all-done.2 = bf16[8,2,4,2,16,256]{5,4,3,2,1,0:T(8,128)(2,1)} async-done(((bf16[8,2,4,2,16,256]{5,4,3,2,1,0:T(8,128)(2,1)}), bf16[8,2,4,2,16,256]{5,4,3,2,1,0:T(8,128)(2,1)}, u32[]{:S(2)}, u32[]{:S(2)}) %all-to-all-start.2) | async-done | bytes 1048608 | tf_op jit(solution)/shard_map/cond/branch_1_fun/all_to_all | solution.py:146
  164.3 1.7 fusion
  166.0 0.2 maximum_bitcast_fusion.1
  166.2 1.5 copy.37
  167.8 5.1 %copy.38 = bf16[128,2,16,256]{0,2,1,3:T(8,128)(2,1)} copy(bf16[128,2,16,256]{3,2,1,0:T(8,128)(2,1)} %bitcast.56) | data formatting | bytes 4194304 | tf_op jit(solution)/shard_map/cond/branch_1_fun/reshape | solution.py:156
  172.9 0.0 collective-permute-done.7.refs_6_
  172.9 0.0 collective-permute-done.6.refs_5_
  172.9 0.0 collective-permute-done.8.refs_7_
  172.9 0.0 collective-permute-done.3.refs_2_
  172.9 0.0 collective-permute-done.4.refs_3_
  172.9 5.4 %weight_grad.1 = f32[4,2,256,256]{3,2,1,0:T(8,128)} custom-call(s32[1]{0:T(128)} %bitcast.22.layer_ref, bf16[8,4,4,2,16,256]{5,4,3,2,1,0:T(8,128)(2,1)} %get-tuple-element.87.refs_0_, bf16[8,4,4,2,16,256]{5,4,3,2,1,0:T(8,128)(2,1)} %all-to-all-done.4.refs_1_, bf16[8,4,2,16,256]{4,3,2,1,0:T(8,128)(2,1)S(1)} %collective-permute-done.3.refs_2_, ...), custom_call_target="tpu_custom_call" | custom-call | tf_op jit(solution)/shard_map/weight_grad/pallas_call | solution.py:111
  (1 shorter events, 0.0 us)
Async XLA Ops:
  0.6 1.4 copy-start.2
  3.1 50.1 %collective-permute-start = (bf16[4,2,256,256]{3,2,1,0:T(8,128)(2,1)}, bf16[4,2,256,256]{3,2,1,0:T(8,128)(2,1)}, u32[]{:S(2)}, u32[]{:S(2)}) collective-permute-start(bf16[4,2,256,256]{3,2,1,0:T(8,128)(2,1)} %broadcast_multiply_fusion), channel_id=1, source_target_pairs={{0,16},{1,17},{2,18},{3,19},{4,20},{5,21},{6,22},{7,23},{8,24},{9,... | collective-permute-start | bytes 3145736 | tf_op jit(solution)/shard_map/ppermute | solution.py:160
  7.1 46.2 %collective-permute-start.1 = (bf16[4,2,256,256]{3,2,1,0:T(8,128)(2,1)}, bf16[4,2,256,256]{3,2,1,0:T(8,128)(2,1)}, u32[]{:S(2)}, u32[]{:S(2)}) collective-permute-start(bf16[4,2,256,256]{3,2,1,0:T(8,128)(2,1)} %broadcast_multiply_fusion), channel_id=1, source_target_pairs={{0,8},{1,9},{2,10},{3,11},{4,12},{5,13},{6,14},{7,15},{8,0},{9,1},... | collective-permute-start | bytes 3145736 | tf_op jit(solution)/shard_map/ppermute | solution.py:160
  14.1 31.0 %all-to-all-start = ((bf16[8,4,4,2,16,256]{5,4,3,2,1,0:T(8,128)(2,1)}), bf16[8,4,4,2,16,256]{5,4,3,2,1,0:T(8,128)(2,1)}, u32[]{:S(2)}, u32[]{:S(2)}) async-start(bf16[8,4,4,2,16,256]{5,4,3,2,1,0:T(8,128)(2,1)} %copy.34), calls=%async_computation | async-start | bytes 4194304 | tf_op jit(solution)/shard_map/cond/branch_1_fun/all_to_all | solution.py:146
  45.2 31.0 %all-to-all-start.4 = ((bf16[8,4,4,2,16,256]{5,4,3,2,1,0:T(8,128)(2,1)}), bf16[8,4,4,2,16,256]{5,4,3,2,1,0:T(8,128)(2,1)}, u32[]{:S(2)}, u32[]{:S(2)}) async-start(bf16[8,4,4,2,16,256]{5,4,3,2,1,0:T(8,128)(2,1)} %get-tuple-element.138), calls=%async_computation.4 | async-start | bytes 4194304 | tf_op jit(solution)/shard_map/all_to_all | solution.py:146
  53.3 62.1 %collective-permute-start.2 = (bf16[4,2,256,256]{3,2,1,0:T(8,128)(2,1)}, bf16[4,2,256,256]{3,2,1,0:T(8,128)(2,1)}, u32[]{:S(2)}, u32[]{:S(2)}) collective-permute-start(bf16[4,2,256,256]{3,2,1,0:T(8,128)(2,1)} %collective-permute-done), channel_id=1, source_target_pairs={{0,8},{1,9},{2,10},{3,11},{4,12},{5,13},{6,14},{7,15},{8,0},{9,1},... | collective-permute-start | bytes 3145736 | tf_op jit(solution)/shard_map/ppermute | solution.py:160
  57.1 62.8 %collective-permute-start.5 = (bf16[8,4,2,16,256]{4,3,2,1,0:T(8,128)(2,1)}, bf16[8,4,2,16,256]{4,3,2,1,0:T(8,128)(2,1)S(1)}, u32[]{:S(2)}, u32[]{:S(2)}) collective-permute-start(bf16[8,4,2,16,256]{4,3,2,1,0:T(8,128)(2,1)} %get-tuple-element.146), channel_id=1, source_target_pairs={{0,16},{1,17},{2,18},{3,19},{4,20},{5,21},{6,22},{7,23},{8,24},{9,... | collective-permute-start | bytes 1572872 | tf_op jit(solution)/shard_map/ppermute | solution.py:160
  59.4 113.5 %collective-permute-start.7 = (bf16[8,4,2,16,256]{4,3,2,1,0:T(8,128)(2,1)}, bf16[8,4,2,16,256]{4,3,2,1,0:T(8,128)(2,1)S(1)}, u32[]{:S(2)}, u32[]{:S(2)}) collective-permute-start(bf16[8,4,2,16,256]{4,3,2,1,0:T(8,128)(2,1)} %get-tuple-element.145), channel_id=1, source_target_pairs={{0,24},{1,25},{2,26},{3,27},{4,28},{5,29},{6,30},{7,31},{8,16},{9,... | collective-permute-start | bytes 1572872 | tf_op jit(solution)/shard_map/ppermute | solution.py:160
  78.5 94.4 %collective-permute-start.6 = (bf16[8,4,2,16,256]{4,3,2,1,0:T(8,128)(2,1)}, bf16[8,4,2,16,256]{4,3,2,1,0:T(8,128)(2,1)S(1)}, u32[]{:S(2)}, u32[]{:S(2)}) collective-permute-start(bf16[8,4,2,16,256]{4,3,2,1,0:T(8,128)(2,1)} %get-tuple-element.144), channel_id=1, source_target_pairs={{0,16},{1,17},{2,18},{3,19},{4,20},{5,21},{6,22},{7,23},{8,24},{9,... | collective-permute-start | bytes 1572872 | tf_op jit(solution)/shard_map/ppermute | solution.py:160
  78.9 94.0 %collective-permute-start.8 = (bf16[8,4,2,16,256]{4,3,2,1,0:T(8,128)(2,1)}, bf16[8,4,2,16,256]{4,3,2,1,0:T(8,128)(2,1)S(1)}, u32[]{:S(2)}, u32[]{:S(2)}) collective-permute-start(bf16[8,4,2,16,256]{4,3,2,1,0:T(8,128)(2,1)} %get-tuple-element.143), channel_id=1, source_target_pairs={{0,24},{1,25},{2,26},{3,27},{4,28},{5,29},{6,30},{7,31},{8,16},{9,... | collective-permute-start | bytes 1572872 | tf_op jit(solution)/shard_map/ppermute | solution.py:160
  117.3 55.6 %collective-permute-start.3 = (bf16[8,4,2,16,256]{4,3,2,1,0:T(8,128)(2,1)}, bf16[8,4,2,16,256]{4,3,2,1,0:T(8,128)(2,1)S(1)}, u32[]{:S(2)}, u32[]{:S(2)}) collective-permute-start(bf16[8,4,2,16,256]{4,3,2,1,0:T(8,128)(2,1)} %dynamic-slice_bitcast_fusion.5), channel_id=1, source_target_pairs={{0,8},{1,9},{2,10},{3,11},{4,12},{5,13},{6,14},{7,15},{8,0},{9,1},... | collective-permute-start | bytes 1572872 | tf_op jit(solution)/shard_map/ppermute | solution.py:160
  119.9 53.1 %collective-permute-start.4 = (bf16[8,4,2,16,256]{4,3,2,1,0:T(8,128)(2,1)}, bf16[8,4,2,16,256]{4,3,2,1,0:T(8,128)(2,1)}, u32[]{:S(2)}, u32[]{:S(2)}) collective-permute-start(bf16[8,4,2,16,256]{4,3,2,1,0:T(8,128)(2,1)} %dynamic-slice_bitcast_fusion.4), channel_id=1, source_target_pairs={{0,8},{1,9},{2,10},{3,11},{4,12},{5,13},{6,14},{7,15},{8,0},{9,1},... | collective-permute-start | bytes 1572872 | tf_op jit(solution)/shard_map/ppermute | solution.py:160
  144.7 19.7 %all-to-all-start.2 = ((bf16[8,2,4,2,16,256]{5,4,3,2,1,0:T(8,128)(2,1)}), bf16[8,2,4,2,16,256]{5,4,3,2,1,0:T(8,128)(2,1)}, u32[]{:S(2)}, u32[]{:S(2)}) async-start(bf16[8,2,4,2,16,256]{5,4,3,2,1,0:T(8,128)(2,1)} %get-tuple-element.44), calls=%async_computation.2 | async-start | bytes 2097152 | tf_op jit(solution)/shard_map/cond/branch_1_fun/all_to_all | solution.py:146
  148.9 3.4 %copy-start = (bf16[8,2,2,4,2,16,256]{6,5,4,3,2,1,0:T(8,128)(2,1)S(1)}, bf16[8,2,2,4,2,16,256]{6,5,4,3,2,1,0:T(8,128)(2,1)}, u32[]{:S(2)}) copy-start(bf16[8,2,2,4,2,16,256]{6,5,4,3,2,1,0:T(8,128)(2,1)} %get-tuple-element.137) | copy-start | bytes 6291460 | tf_op jit(solution)/shard_map/cond
  148.9 3.4 %copy-start.1 = (bf16[8,2,4,2,16,256]{5,4,3,2,1,0:T(8,128)(2,1)S(1)}, bf16[8,2,4,2,16,256]{5,4,3,2,1,0:T(8,128)(2,1)}, u32[]{:S(2)}) copy-start(bf16[8,2,4,2,16,256]{5,4,3,2,1,0:T(8,128)(2,1)} %all_to_all.22) | copy-start | bytes 3145732 | tf_op jit(solution)/shard_map/cond

commit v4 on v3

--- a/solution.py
+++ b/solution.py
@@ -159,8 +159,8 @@
     def send(a, step):
         return lax.ppermute(a, "blk", [(i, i ^ (step * inner)) for i in range(ranks)])
 
-    def for_owner(a, step):
-        return send(lax.dynamic_index_in_dim(a, layer ^ step, 1, keepdims=False), step)
+    def of_owner(a, step):
+        return lax.dynamic_index_in_dim(a, layer ^ step, 1, keepdims=False)
 
     def mixed(odd, joint, x, g, ws):
         out = list(mix(place, odd, x, g, ws, jnp.bfloat16 if chans == 1 else F32, joint))
@@ -184,14 +184,15 @@
     g = exchange(turned)
     x, far, near = barrier((x, far, near))
     near_far = send(far, 1)
-    pairs = {step: [for_owner(x, step)] for step in (2, 3)}
+    x_parts = {step: of_owner(x, step) for step in (1, 2, 3)}
+    pairs = {step: [send(x_parts[step], step)] for step in (2, 3)}
     g, near = barrier((g, near))
+    g_parts = {step: of_owner(g, step) for step in (1, 2, 3)}
     for step in (2, 3):
-        pairs[step].append(for_owner(g, step))
+        pairs[step].append(send(g_parts[step], step))
     same = stage(ready, functools.partial(mixed, 0, chans == 1), x, g, [masked, far])
-    same, near_far = barrier((same, near_far))
-    x_late, g_late, near_far = barrier((x, g, near_far))
-    pairs[1] = [for_owner(x_late, 1), for_owner(g_late, 1)]
+    x_parts[1], g_parts[1], near_far, same = barrier((x_parts[1], g_parts[1], near_far, same))
+    pairs[1] = [send(x_parts[1], 1), send(g_parts[1], 1)]
     spec_out, grad_in = stage(ready, outward, x, g, [near, near_far], same)
     spec_out, grad_in, pairs = barrier((spec_out, grad_in, pairs))
     grad_weight = weight_grad(place, x, g, [pairs[step] for step in (1, 2, 3)], own_mask)

time: 179 us -> 175 us (0.978)
  local copies, waits for them, and re-layouts: 36.5 us -> 33.3 us
    squeeze x4 -> x2, local copies, waits for them, and re-layouts: 8.37 us -> 5.12 us  [of_owner(): return lax.dynamic_index_in_dim(a, layer ^ step, 1, keepdims=False)]
  transfers between devices with their start and end apart: 12 -> 12, of which waited for: 5 -> 5; matrix products, arithmetic and copies ran while one was open for 22% -> 20% of each run, Pallas kernels for 5% -> 5%
where the time goes in v4:
time: 175 us; the launch traced here: 174 us
  blocking collectives  48.2 us (28%)
  waiting for transfers between devices  46.4 us (27%)
  local copies, waits for them, and re-layouts  33.3 us (19%)
  starting transfers between devices  26.5 us (15%)
  Pallas kernels  14.7 us (8%)
  other arithmetic  4.53 us (3%)
    all_to_all x2, blocking collectives, exchange(): return lax.all_to_all(a, 'blk', 0, 0, tiled=True, axis_index_groups=layers)  48.2 us
    all_to_all x3, waiting for transfers between devices, exchange(): return lax.all_to_all(a, 'blk', 0, 0, tiled=True, axis_index_groups=layers)  41.4 us
    ppermute x9, starting transfers between devices, send(): return lax.ppermute(a, 'blk', [(i, i ^ step * inner) for i in range(ranks)])  13.6 us
    all_to_all x3, starting transfers between devices, exchange(): return lax.all_to_all(a, 'blk', 0, 0, tiled=True, axis_index_groups=layers)  13 us
    another operation x3, local copies, waits for them, and re-layouts  11.2 us
    reshape x2, local copies, waits for them, and re-layouts, to_samples(): turned.reshape(ranks * modes, *turned.shape[4:]).transpose(3, 1, 2, 0)  10.3 us
    pallas_call x2, Pallas kernels, mix(): pl.pallas_call(mix_kernel, grid_spec=pltpu.PrefetchScalarGridSpec(num_sca...  9.3 us
    pallas_call x1, Pallas kernels, weight_grad(): pl.pallas_call(weight_grad_kernel, grid_spec=pltpu.PrefetchScalarGridSpec...  5.43 us
  transfers between devices with their start and end apart: 12, of which 5 were waited for; matrix products, arithmetic and copies ran while one was open for 20% of the time, Pallas kernels for 5%

profile of v4, /device:TPU:0, one launch (start us, length us, event | category | flops | bytes accessed | tf_op | source)
XLA Modules:
  0.0 174.5 jit_solution(6053416186650873204)
XLA Ops:
  0.6 0.0 copy-start.2
  0.6 0.8 convert_element_type.9
  1.4 0.1 copy.41
  1.6 0.1 broadcast_in_dim.7
  1.6 0.1 reshape.28
  1.8 0.2 copy.42.refs_8_
  2.0 0.0 copy-done.2
  2.0 1.1 broadcast_multiply_fusion
  3.1 3.0 %collective-permute-start.1 = (bf16[4,2,256,256]{3,2,1,0:T(8,128)(2,1)}, bf16[4,2,256,256]{3,2,1,0:T(8,128)(2,1)}, u32[]{:S(2)}, u32[]{:S(2)}) collective-permute-start(bf16[4,2,256,256]{3,2,1,0:T(8,128)(2,1)} %broadcast_multiply_fusion), channel_id=1, source_target_pairs={{0,8},{1,9},{2,10},{3,11},{4,12},{5,13},{6,14},{7,15},{8,0},{9,1},... | collective-permute-start | bytes 3145736 | tf_op jit(solution)/shard_map/ppermute | solution.py:160
  6.1 2.6 %collective-permute-start = (bf16[4,2,256,256]{3,2,1,0:T(8,128)(2,1)}, bf16[4,2,256,256]{3,2,1,0:T(8,128)(2,1)}, u32[]{:S(2)}, u32[]{:S(2)}) collective-permute-start(bf16[4,2,256,256]{3,2,1,0:T(8,128)(2,1)} %broadcast_multiply_fusion), channel_id=1, source_target_pairs={{0,16},{1,17},{2,18},{3,19},{4,20},{5,21},{6,22},{7,23},{8,24},{9,... | collective-permute-start | bytes 3145736 | tf_op jit(solution)/shard_map/ppermute | solution.py:160
  8.7 36.5 %conditional.3 = (bf16[8,4,4,2,16,256]{5,4,3,2,1,0:T(8,128)(2,1)}, bf16[8,4,4,2,16,256]{5,4,3,2,1,0:T(8,128)(2,1)}) conditional(s32[]{:T(128)} %convert_element_type.8, () %tuple.36, (bf16[256,2,16,128]{3,2,1,0:T(8,128)(2,1)}, bf16[256,2,16,128]{3,2,1,0:T(8,128)(2,1)}) %tuple.37), branch_computations={%region_0.1_spmd, %region_1.2_spmd} | conditional | bytes 23068720 | solution.py:127
  8.7 3.9 %copy.39 = bf16[256,2,16,128]{0,2,1,3:T(8,128)(2,1)S(1)} copy(bf16[256,2,16,128]{3,2,1,0:T(8,128)(2,1)} %get-tuple-element.127) | data formatting | bytes 4194304 | tf_op jit(solution)/shard_map
  12.6 1.5 copy.34
  14.1 4.3 %all-to-all-start = ((bf16[8,4,4,2,16,256]{5,4,3,2,1,0:T(8,128)(2,1)}), bf16[8,4,4,2,16,256]{5,4,3,2,1,0:T(8,128)(2,1)}, u32[]{:S(2)}, u32[]{:S(2)}) async-start(bf16[8,4,4,2,16,256]{5,4,3,2,1,0:T(8,128)(2,1)} %copy.34), calls=%async_computation | async-start | bytes 4194304 | tf_op jit(solution)/shard_map/cond/branch_1_fun/all_to_all | solution.py:146
  18.5 3.9 %copy.40 = bf16[256,2,16,128]{0,2,1,3:T(8,128)(2,1)S(1)} copy(bf16[256,2,16,128]{3,2,1,0:T(8,128)(2,1)} %get-tuple-element.128) | data formatting | bytes 4194304 | tf_op jit(solution)/shard_map
  22.4 1.5 copy.47
  24.0 21.2 %all-to-all-done = bf16[8,4,4,2,16,256]{5,4,3,2,1,0:T(8,128)(2,1)} async-done(((bf16[8,4,4,2,16,256]{5,4,3,2,1,0:T(8,128)(2,1)}), bf16[8,4,4,2,16,256]{5,4,3,2,1,0:T(8,128)(2,1)}, u32[]{:S(2)}, u32[]{:S(2)}) %all-to-all-start) | async-done | bytes 2097184 | tf_op jit(solution)/shard_map/cond/branch_1_fun/all_to_all | solution.py:146
  45.2 4.4 %all-to-all-start.4 = ((bf16[8,4,4,2,16,256]{5,4,3,2,1,0:T(8,128)(2,1)}), bf16[8,4,4,2,16,256]{5,4,3,2,1,0:T(8,128)(2,1)}, u32[]{:S(2)}, u32[]{:S(2)}) async-start(bf16[8,4,4,2,16,256]{5,4,3,2,1,0:T(8,128)(2,1)} %get-tuple-element.136), calls=%async_computation.4 | async-start | bytes 4194304 | tf_op jit(solution)/shard_map/all_to_all | solution.py:146
  49.5 2.4 %collective-permute-done.1 = bf16[4,2,256,256]{3,2,1,0:T(8,128)(2,1)} collective-permute-done((bf16[4,2,256,256]{3,2,1,0:T(8,128)(2,1)}, bf16[4,2,256,256]{3,2,1,0:T(8,128)(2,1)}, u32[]{:S(2)}, u32[]{:S(2)}) %collective-permute-start.1) | collective-permute-done | bytes 1048608 | tf_op jit(solution)/shard_map/ppermute | solution.py:160
  51.9 2.6 %collective-permute-done = bf16[4,2,256,256]{3,2,1,0:T(8,128)(2,1)} collective-permute-done((bf16[4,2,256,256]{3,2,1,0:T(8,128)(2,1)}, bf16[4,2,256,256]{3,2,1,0:T(8,128)(2,1)}, u32[]{:S(2)}, u32[]{:S(2)}) %collective-permute-start) | collective-permute-done | bytes 1048608 | tf_op jit(solution)/shard_map/ppermute | solution.py:160
  54.5 0.4 collective-permute-start.2
  54.9 2.5 %dynamic-slice_bitcast_fusion.1 = (bf16[8,4,2,16,256]{4,3,2,1,0:T(8,128)(2,1)}, bf16[8,4,2,16,256]{4,3,2,1,0:T(8,128)(2,1)}, bf16[8,4,2,16,256]{4,3,2,1,0:T(8,128)(2,1)}) fusion(bf16[8,4,4,2,16,256]{5,4,3,2,1,0:T(8,128)(2,1)} %get-tuple-element.75.refs_0_, s32[]{:T(128)S(6)} %select_n.50, s32[]{:T(128)S(6)} %select_n.49, s32[]{:T(128)S(6)} %select_n.48), kind=kLoop, calls=%fused_computation.10 | loop fusion | bytes 3145740 | tf_op jit(solution)/shard_map/jit(dynamic_index_in_dim)/squeeze | solution.py:163
  57.4 2.1 %collective-permute-start.7 = (bf16[8,4,2,16,256]{4,3,2,1,0:T(8,128)(2,1)}, bf16[8,4,2,16,256]{4,3,2,1,0:T(8,128)(2,1)S(1)}, u32[]{:S(2)}, u32[]{:S(2)}) collective-permute-start(bf16[8,4,2,16,256]{4,3,2,1,0:T(8,128)(2,1)} %get-tuple-element.144), channel_id=1, source_target_pairs={{0,24},{1,25},{2,26},{3,27},{4,28},{5,29},{6,30},{7,31},{8,16},{9,... | collective-permute-start | bytes 1572872 | tf_op jit(solution)/shard_map/ppermute | solution.py:160
  59.5 1.0 collective-permute-start.5
  60.5 15.7 %all-to-all-done.4.refs_1_ = bf16[8,4,4,2,16,256]{5,4,3,2,1,0:T(8,128)(2,1)} async-done(((bf16[8,4,4,2,16,256]{5,4,3,2,1,0:T(8,128)(2,1)}), bf16[8,4,4,2,16,256]{5,4,3,2,1,0:T(8,128)(2,1)}, u32[]{:S(2)}, u32[]{:S(2)}) %all-to-all-start.4) | async-done | bytes 2097184 | tf_op jit(solution)/shard_map/all_to_all | solution.py:146
  76.2 2.6 %dynamic-slice_bitcast_fusion = (bf16[8,4,2,16,256]{4,3,2,1,0:T(8,128)(2,1)}, bf16[8,4,2,16,256]{4,3,2,1,0:T(8,128)(2,1)}, bf16[8,4,2,16,256]{4,3,2,1,0:T(8,128)(2,1)}) fusion(bf16[8,4,4,2,16,256]{5,4,3,2,1,0:T(8,128)(2,1)} %all-to-all-done.4.refs_1_, s32[]{:T(128)S(6)} %select_n.50, s32[]{:T(128)S(6)} %select_n.49, s32[]{:T(128)S(6)} %select_n.48), kind=kLoop, calls=%fused_computation.9 | loop fusion | bytes 3145740 | tf_op jit(solution)/shard_map/jit(dynamic_index_in_dim)/squeeze | solution.py:163
  78.8 0.0 collective-permute-start.8
  78.8 1.9 %collective-permute-start.6 = (bf16[8,4,2,16,256]{4,3,2,1,0:T(8,128)(2,1)}, bf16[8,4,2,16,256]{4,3,2,1,0:T(8,128)(2,1)S(1)}, u32[]{:S(2)}, u32[]{:S(2)}) collective-permute-start(bf16[8,4,2,16,256]{4,3,2,1,0:T(8,128)(2,1)} %get-tuple-element.142), channel_id=1, source_target_pairs={{0,16},{1,17},{2,18},{3,19},{4,20},{5,21},{6,22},{7,23},{8,24},{9,... | collective-permute-start | bytes 1572872 | tf_op jit(solution)/shard_map/ppermute | solution.py:160
  80.7 34.1 %conditional.4 = (bf16[8,2,2,4,2,16,256]{6,5,4,3,2,1,0:T(8,128)(2,1)}) conditional(s32[]{:T(128)} %convert_element_type.8, () %tuple.40, (s32[1]{0:T(128)}, bf16[8,4,4,2,16,256]{5,4,3,2,1,0:T(8,128)(2,1)}, bf16[8,4,4,2,16,256]{5,4,3,2,1,0:T(8,128)(2,1)}, bf16[4,2,256,256]{3,2,1,0:T(8,128)(2,1)}, bf16[4,2,256,256]{3,2,1,0:T(8,128)(2,1)}) %tuple.41), branch_computations={%region_2.3_spmd, %region_3.4_spmd} | conditional | bytes 4194312 | solution.py:127
  80.7 4.3 %mix.2 = bf16[8,2,2,4,2,16,256]{6,5,4,3,2,1,0:T(8,128)(2,1)S(1)} custom-call(s32[1]{0:T(128)} %get-tuple-element.33.layer_ref, bf16[8,4,4,2,16,256]{5,4,3,2,1,0:T(8,128)(2,1)} %get-tuple-element.34.x_ref, bf16[8,4,4,2,16,256]{5,4,3,2,1,0:T(8,128)(2,1)} %get-tuple-element.35.g_ref, bf16[4,2,256,256]{3,2,1,0:T(8,128)(2,1)} %get-tuple-element.36.same_ref, ...), custom_call_target="tpu_custom_call" | custom-call | tf_op jit(solution)/shard_map/cond/branch_1_fun/mix/pallas_call | solution.py:71
  85.0 29.8 %all_to_all.21 = bf16[8,2,2,4,2,16,256]{6,5,4,3,2,1,0:T(8,128)(2,1)} all-to-all(bf16[8,2,2,4,2,16,256]{6,5,4,3,2,1,0:T(8,128)(2,1)S(1)} %mix.2), channel_id=1, replica_groups={{0,1,2,3,4,5,6,7},{8,9,10,11,12,13,14,15},{16,17,18,19,20,21,22,23},{24..., dimensions={0} | all-to-all | bytes 4194304 | tf_op jit(solution)/shard_map/cond/branch_1_fun/all_to_all | solution.py:146
  114.7 0.0 collective-permute-done.2
  114.8 2.5 %collective-permute-start.3 = (bf16[8,4,2,16,256]{4,3,2,1,0:T(8,128)(2,1)}, bf16[8,4,2,16,256]{4,3,2,1,0:T(8,128)(2,1)S(1)}, u32[]{:S(2)}, u32[]{:S(2)}) collective-permute-start(bf16[8,4,2,16,256]{4,3,2,1,0:T(8,128)(2,1)} %get-tuple-element.85), channel_id=1, source_target_pairs={{0,8},{1,9},{2,10},{3,11},{4,12},{5,13},{6,14},{7,15},{8,0},{9,1},... | collective-permute-start | bytes 1572872 | tf_op jit(solution)/shard_map/ppermute | solution.py:160
  117.2 0.0 collective-permute-done.7.refs_6_
  117.2 0.1 collective-permute-start.4
  117.3 51.7 %conditional.5 = (bf16[256,2,16,128]{3,2,1,0:T(8,128)(2,1)}, bf16[256,2,16,128]{3,2,1,0:T(8,128)(2,1)}) conditional(s32[]{:T(128)} %convert_element_type.8, () %tuple.35, (s32[1]{0:T(128)}, bf16[8,4,4,2,16,256]{5,4,3,2,1,0:T(8,128)(2,1)}, bf16[8,4,4,2,16,256]{5,4,3,2,1,0:T(8,128)(2,1)}, bf16[4,2,256,256]{3,2,1,0:T(8,128)(2,1)}, ...), branch_computations={%region_4.5_spmd, %region_5.6_spmd} | conditional | flops 4194316 | bytes 55574752 | solution.py:127
  117.3 5.0 %mix.3 = (bf16[8,2,4,2,16,256]{5,4,3,2,1,0:T(8,128)(2,1)S(1)}, bf16[8,2,4,2,16,256]{5,4,3,2,1,0:T(8,128)(2,1)}) custom-call(s32[1]{0:T(128)} %get-tuple-element.39.layer_ref, bf16[8,4,4,2,16,256]{5,4,3,2,1,0:T(8,128)(2,1)} %get-tuple-element.40.x_ref, bf16[8,4,4,2,16,256]{5,4,3,2,1,0:T(8,128)(2,1)} %get-tuple-element.41.g_ref, ...), custom_call_target="tpu_custom_call" | custom-call | tf_op jit(solution)/shard_map/cond/branch_1_fun/mix/pallas_call | solution.py:71
  122.3 18.5 %all_to_all.22 = bf16[8,2,4,2,16,256]{5,4,3,2,1,0:T(8,128)(2,1)} all-to-all(bf16[8,2,4,2,16,256]{5,4,3,2,1,0:T(8,128)(2,1)S(1)} %get-tuple-element.46), channel_id=1, replica_groups={{0,1,2,3,4,5,6,7},{8,9,10,11,12,13,14,15},{16,17,18,19,20,21,22,23},{24..., dimensions={0} | all-to-all | bytes 2097152 | tf_op jit(solution)/shard_map/cond/branch_1_fun/all_to_all | solution.py:146
  140.8 4.2 %all-to-all-start.2 = ((bf16[8,2,4,2,16,256]{5,4,3,2,1,0:T(8,128)(2,1)}), bf16[8,2,4,2,16,256]{5,4,3,2,1,0:T(8,128)(2,1)}, u32[]{:S(2)}, u32[]{:S(2)}) async-start(bf16[8,2,4,2,16,256]{5,4,3,2,1,0:T(8,128)(2,1)} %get-tuple-element.44), calls=%async_computation.2 | async-start | bytes 2097152 | tf_op jit(solution)/shard_map/cond/branch_1_fun/all_to_all | solution.py:146
  145.0 0.0 copy-start
  145.1 0.0 copy-start.1
  145.1 3.3 %copy.44 = bf16[8,2,2,4,2,16,256]{6,5,4,3,2,0,1:T(8,128)(2,1)} copy(bf16[8,2,2,4,2,16,256]{6,5,4,3,2,1,0:T(8,128)(2,1)} %get-tuple-element.135) | data formatting | bytes 4194304 | tf_op jit(solution)/shard_map
  148.4 0.0 copy-done
  148.4 0.0 copy-done.1
  148.4 0.6 select_bitcast_fusion.1
  149.0 0.2 maximum_bitcast_fusion
  149.2 1.5 copy.35
  150.8 5.1 %copy.36 = bf16[128,2,16,256]{0,2,1,3:T(8,128)(2,1)} copy(bf16[128,2,16,256]{3,2,1,0:T(8,128)(2,1)} %bitcast.55) | data formatting | bytes 4194304 | tf_op jit(solution)/shard_map/cond/branch_1_fun/reshape | solution.py:156
  155.9 4.5 %all-to-all-done.2 = bf16[8,2,4,2,16,256]{5,4,3,2,1,0:T(8,128)(2,1)} async-done(((bf16[8,2,4,2,16,256]{5,4,3,2,1,0:T(8,128)(2,1)}), bf16[8,2,4,2,16,256]{5,4,3,2,1,0:T(8,128)(2,1)}, u32[]{:S(2)}, u32[]{:S(2)}) %all-to-all-start.2) | async-done | bytes 1048608 | tf_op jit(solution)/shard_map/cond/branch_1_fun/all_to_all | solution.py:146
  160.4 1.7 fusion
  162.1 0.2 maximum_bitcast_fusion.1
  162.3 1.5 copy.37
  163.9 5.1 %copy.38 = bf16[128,2,16,256]{0,2,1,3:T(8,128)(2,1)} copy(bf16[128,2,16,256]{3,2,1,0:T(8,128)(2,1)} %bitcast.56) | data formatting | bytes 4194304 | tf_op jit(solution)/shard_map/cond/branch_1_fun/reshape | solution.py:156
  169.0 0.0 collective-permute-done.5.refs_4_
  169.0 0.0 collective-permute-done.8.refs_7_
  169.0 0.0 collective-permute-done.6.refs_5_
  169.0 0.0 collective-permute-done.3.refs_2_
  169.0 0.0 collective-permute-done.4.refs_3_
  169.0 5.4 %weight_grad.1 = f32[4,2,256,256]{3,2,1,0:T(8,128)} custom-call(s32[1]{0:T(128)} %bitcast.22.layer_ref, bf16[8,4,4,2,16,256]{5,4,3,2,1,0:T(8,128)(2,1)} %get-tuple-element.75.refs_0_, bf16[8,4,4,2,16,256]{5,4,3,2,1,0:T(8,128)(2,1)} %all-to-all-done.4.refs_1_, bf16[8,4,2,16,256]{4,3,2,1,0:T(8,128)(2,1)S(1)} %collective-permute-done.3.refs_2_, ...), custom_call_target="tpu_custom_call" | custom-call | tf_op jit(solution)/shard_map/weight_grad/pallas_call | solution.py:111
  (1 shorter events, 0.0 us)
Async XLA Ops:
  0.6 1.4 copy-start.2
  3.1 48.8 %collective-permute-start.1 = (bf16[4,2,256,256]{3,2,1,0:T(8,128)(2,1)}, bf16[4,2,256,256]{3,2,1,0:T(8,128)(2,1)}, u32[]{:S(2)}, u32[]{:S(2)}) collective-permute-start(bf16[4,2,256,256]{3,2,1,0:T(8,128)(2,1)} %broadcast_multiply_fusion), channel_id=1, source_target_pairs={{0,8},{1,9},{2,10},{3,11},{4,12},{5,13},{6,14},{7,15},{8,0},{9,1},... | collective-permute-start | bytes 3145736 | tf_op jit(solution)/shard_map/ppermute | solution.py:160
  6.1 48.4 %collective-permute-start = (bf16[4,2,256,256]{3,2,1,0:T(8,128)(2,1)}, bf16[4,2,256,256]{3,2,1,0:T(8,128)(2,1)}, u32[]{:S(2)}, u32[]{:S(2)}) collective-permute-start(bf16[4,2,256,256]{3,2,1,0:T(8,128)(2,1)} %broadcast_multiply_fusion), channel_id=1, source_target_pairs={{0,16},{1,17},{2,18},{3,19},{4,20},{5,21},{6,22},{7,23},{8,24},{9,... | collective-permute-start | bytes 3145736 | tf_op jit(solution)/shard_map/ppermute | solution.py:160
  14.1 31.0 %all-to-all-start = ((bf16[8,4,4,2,16,256]{5,4,3,2,1,0:T(8,128)(2,1)}), bf16[8,4,4,2,16,256]{5,4,3,2,1,0:T(8,128)(2,1)}, u32[]{:S(2)}, u32[]{:S(2)}) async-start(bf16[8,4,4,2,16,256]{5,4,3,2,1,0:T(8,128)(2,1)} %copy.34), calls=%async_computation | async-start | bytes 4194304 | tf_op jit(solution)/shard_map/cond/branch_1_fun/all_to_all | solution.py:146
  45.2 31.0 %all-to-all-start.4 = ((bf16[8,4,4,2,16,256]{5,4,3,2,1,0:T(8,128)(2,1)}), bf16[8,4,4,2,16,256]{5,4,3,2,1,0:T(8,128)(2,1)}, u32[]{:S(2)}, u32[]{:S(2)}) async-start(bf16[8,4,4,2,16,256]{5,4,3,2,1,0:T(8,128)(2,1)} %get-tuple-element.136), calls=%async_computation.4 | async-start | bytes 4194304 | tf_op jit(solution)/shard_map/all_to_all | solution.py:146
  54.5 60.3 %collective-permute-start.2 = (bf16[4,2,256,256]{3,2,1,0:T(8,128)(2,1)}, bf16[4,2,256,256]{3,2,1,0:T(8,128)(2,1)}, u32[]{:S(2)}, u32[]{:S(2)}) collective-permute-start(bf16[4,2,256,256]{3,2,1,0:T(8,128)(2,1)} %collective-permute-done), channel_id=1, source_target_pairs={{0,8},{1,9},{2,10},{3,11},{4,12},{5,13},{6,14},{7,15},{8,0},{9,1},... | collective-permute-start | bytes 3145736 | tf_op jit(solution)/shard_map/ppermute | solution.py:160
  57.4 59.8 %collective-permute-start.7 = (bf16[8,4,2,16,256]{4,3,2,1,0:T(8,128)(2,1)}, bf16[8,4,2,16,256]{4,3,2,1,0:T(8,128)(2,1)S(1)}, u32[]{:S(2)}, u32[]{:S(2)}) collective-permute-start(bf16[8,4,2,16,256]{4,3,2,1,0:T(8,128)(2,1)} %get-tuple-element.144), channel_id=1, source_target_pairs={{0,24},{1,25},{2,26},{3,27},{4,28},{5,29},{6,30},{7,31},{8,16},{9,... | collective-permute-start | bytes 1572872 | tf_op jit(solution)/shard_map/ppermute | solution.py:160
  59.5 109.5 %collective-permute-start.5 = (bf16[8,4,2,16,256]{4,3,2,1,0:T(8,128)(2,1)}, bf16[8,4,2,16,256]{4,3,2,1,0:T(8,128)(2,1)S(1)}, u32[]{:S(2)}, u32[]{:S(2)}) collective-permute-start(bf16[8,4,2,16,256]{4,3,2,1,0:T(8,128)(2,1)} %get-tuple-element.145), channel_id=1, source_target_pairs={{0,16},{1,17},{2,18},{3,19},{4,20},{5,21},{6,22},{7,23},{8,24},{9,... | collective-permute-start | bytes 1572872 | tf_op jit(solution)/shard_map/ppermute | solution.py:160
  78.8 90.2 %collective-permute-start.8 = (bf16[8,4,2,16,256]{4,3,2,1,0:T(8,128)(2,1)}, bf16[8,4,2,16,256]{4,3,2,1,0:T(8,128)(2,1)S(1)}, u32[]{:S(2)}, u32[]{:S(2)}) collective-permute-start(bf16[8,4,2,16,256]{4,3,2,1,0:T(8,128)(2,1)} %get-tuple-element.141), channel_id=1, source_target_pairs={{0,24},{1,25},{2,26},{3,27},{4,28},{5,29},{6,30},{7,31},{8,16},{9,... | collective-permute-start | bytes 1572872 | tf_op jit(solution)/shard_map/ppermute | solution.py:160
  78.8 90.2 %collective-permute-start.6 = (bf16[8,4,2,16,256]{4,3,2,1,0:T(8,128)(2,1)}, bf16[8,4,2,16,256]{4,3,2,1,0:T(8,128)(2,1)S(1)}, u32[]{:S(2)}, u32[]{:S(2)}) collective-permute-start(bf16[8,4,2,16,256]{4,3,2,1,0:T(8,128)(2,1)} %get-tuple-element.142), channel_id=1, source_target_pairs={{0,16},{1,17},{2,18},{3,19},{4,20},{5,21},{6,22},{7,23},{8,24},{9,... | collective-permute-start | bytes 1572872 | tf_op jit(solution)/shard_map/ppermute | solution.py:160
  114.8 54.3 %collective-permute-start.3 = (bf16[8,4,2,16,256]{4,3,2,1,0:T(8,128)(2,1)}, bf16[8,4,2,16,256]{4,3,2,1,0:T(8,128)(2,1)S(1)}, u32[]{:S(2)}, u32[]{:S(2)}) collective-permute-start(bf16[8,4,2,16,256]{4,3,2,1,0:T(8,128)(2,1)} %get-tuple-element.85), channel_id=1, source_target_pairs={{0,8},{1,9},{2,10},{3,11},{4,12},{5,13},{6,14},{7,15},{8,0},{9,1},... | collective-permute-start | bytes 1572872 | tf_op jit(solution)/shard_map/ppermute | solution.py:160
  117.2 51.8 %collective-permute-start.4 = (bf16[8,4,2,16,256]{4,3,2,1,0:T(8,128)(2,1)}, bf16[8,4,2,16,256]{4,3,2,1,0:T(8,128)(2,1)}, u32[]{:S(2)}, u32[]{:S(2)}) collective-permute-start(bf16[8,4,2,16,256]{4,3,2,1,0:T(8,128)(2,1)} %get-tuple-element.86), channel_id=1, source_target_pairs={{0,8},{1,9},{2,10},{3,11},{4,12},{5,13},{6,14},{7,15},{8,0},{9,1},... | collective-permute-start | bytes 1572872 | tf_op jit(solution)/shard_map/ppermute | solution.py:160
  140.8 19.7 %all-to-all-start.2 = ((bf16[8,2,4,2,16,256]{5,4,3,2,1,0:T(8,128)(2,1)}), bf16[8,2,4,2,16,256]{5,4,3,2,1,0:T(8,128)(2,1)}, u32[]{:S(2)}, u32[]{:S(2)}) async-start(bf16[8,2,4,2,16,256]{5,4,3,2,1,0:T(8,128)(2,1)} %get-tuple-element.44), calls=%async_computation.2 | async-start | bytes 2097152 | tf_op jit(solution)/shard_map/cond/branch_1_fun/all_to_all | solution.py:146
  145.0 3.4 %copy-start = (bf16[8,2,2,4,2,16,256]{6,5,4,3,2,1,0:T(8,128)(2,1)S(1)}, bf16[8,2,2,4,2,16,256]{6,5,4,3,2,1,0:T(8,128)(2,1)}, u32[]{:S(2)}) copy-start(bf16[8,2,2,4,2,16,256]{6,5,4,3,2,1,0:T(8,128)(2,1)} %get-tuple-element.135) | copy-start | bytes 6291460 | tf_op jit(solution)/shard_map/cond
  145.1 3.4 %copy-start.1 = (bf16[8,2,4,2,16,256]{5,4,3,2,1,0:T(8,128)(2,1)S(1)}, bf16[8,2,4,2,16,256]{5,4,3,2,1,0:T(8,128)(2,1)}, u32[]{:S(2)}) copy-start(bf16[8,2,4,2,16,256]{5,4,3,2,1,0:T(8,128)(2,1)} %all_to_all.22) | copy-start | bytes 3145732 | tf_op jit(solution)/shard_map/cond

commit v5 on v4

--- a/solution.py
+++ b/solution.py
@@ -82,20 +82,47 @@
     )(layer, x, g, *ws)
 
 
+def gather_kernel(layer_ref, same_ref, other_ref, out_ref):
+    def put(ref):
+        out_ref[...] = ref[...].reshape(out_ref.shape)
+
+    same = layer_ref[0] % 2 == pl.program_id(1)
+    pl.when(same)(lambda: put(same_ref))
+    pl.when(jnp.logical_not(same))(lambda: put(other_ref))
+
+
+def gather(layer, same, kind, other):
+    inner, _, modes, _, samples, channels = other.shape
+    block = (inner, 1, modes, 2, samples, channels)
+    if same.ndim == 7:
+        same_spec = pl.BlockSpec((inner, 1, *block[1:]), lambda h, p, layer: (0, kind, h, 0, 0, 0, 0))
+    else:
+        same_spec = pl.BlockSpec(block, lambda h, p, layer: (0, h, 0, 0, 0, 0))
+    return pl.pallas_call(
+        gather_kernel,
+        grid_spec=pltpu.PrefetchScalarGridSpec(
+            num_scalar_prefetch=1,
+            grid=(2, 2),
+            in_specs=[same_spec, pl.BlockSpec(block, lambda h, p, layer: (0, h, 0, 0, 0, 0))],
+            out_specs=pl.BlockSpec((1, inner, modes, 2, samples, channels), lambda h, p, layer: (2 * h + p, 0, 0, 0, 0, 0)),
+        ),
+        out_shape=jax.ShapeDtypeStruct((4, inner, modes, 2, samples, channels), other.dtype),
+        compiler_params=pltpu.CompilerParams(vmem_limit_bytes=32 * 1024 * 1024),
+        name="gather",
+    )(layer, same, other)
+
+
 def weight_grad_kernel(layer_ref, *refs):
     *pairs, mask_ref, out_ref = refs
 
     def rows(ref, c):
         return ref[..., c, :, :].reshape(-1, ref.shape[-1])
 
-    real = imag = 0.0
-    for x_ref, g_ref in zip(pairs[::2], pairs[1::2]):
-        x_real, x_imag, g_real, g_imag = rows(x_ref, 0), rows(x_ref, 1), rows(g_ref, 0), rows(g_ref, 1)
-        real = real + dot(x_real, g_real, TN) + dot(x_imag, g_imag, TN)
-        imag = imag + dot(x_real, g_imag, TN) - dot(x_imag, g_real, TN)
+    x = jnp.concatenate([rows(ref, c) for ref in pairs[::2] for c in range(2)])
+    g = [(rows(ref, 0), rows(ref, 1)) for ref in pairs[1::2]]
     mask = mask_ref[0].astype(F32)
-    out_ref[0, 0] = real * mask
-    out_ref[0, 1] = imag * mask
+    out_ref[0, 0] = dot(x, jnp.concatenate([part for real, imag in g for part in (real, imag)]), TN) * mask
+    out_ref[0, 1] = dot(x, jnp.concatenate([part for real, imag in g for part in (imag, -real)]), TN) * mask
 
 
 def weight_grad(layer, x, g, pairs, mask):
@@ -149,11 +176,9 @@
         turned = a.transpose(3, 1, 2, 0)
         return turned.reshape(outer, inner, modes, *turned.shape[1:]).swapaxes(0, 1)
 
-    def to_samples(same, other):
-        even = layer % 2 == 0
-        parts = jnp.where(even, same, other), jnp.where(even, other, same)
-        turned = jnp.stack(parts, axis=2).transpose(1, 2, 0, *range(3, 7))
-        turned = turned.reshape(ranks * modes, *turned.shape[4:]).transpose(3, 1, 2, 0)
+    def to_samples(same, kind, other):
+        turned = gather(place, same, kind, other)
+        turned = turned.reshape(ranks * modes, *turned.shape[3:]).transpose(3, 1, 2, 0)
         return with_layout_constraint(turned, Layout((0, 1, 2, 3)))
 
     def send(a, step):
@@ -170,9 +195,9 @@
 
     def outward(x, g, ws, same):
         y, d = mixed(1, False, x, g, ws)
-        spec_out = to_samples(same[0][:, 0] if chans == 1 else same[0], y)
+        spec_out = to_samples(same[0], 0, y)
         same, d, spec_out = lax.optimization_barrier((same, d, spec_out))
-        return spec_out, to_samples(same[0][:, 1] if chans == 1 else same[1], d)
+        return spec_out, to_samples(same[-1], 1, d)
 
     barrier = lax.optimization_barrier
     place = layer.astype(jnp.int32).reshape(1)

time: 175 us -> 172 us (0.983)
  local copies, waits for them, and re-layouts: 33.3 us -> 25.5 us
  Pallas kernels: 14.7 us -> 18.9 us
  waiting for transfers between devices: 46.4 us -> 49.9 us
  other arithmetic: 4.53 us -> 1.85 us
    pallas_call x0 -> x2, Pallas kernels: none -> 4.85 us  [gather(): pl.pallas_call(gather_kernel, grid_spec=pltpu.PrefetchScalarGridSpec(num_...]
    all_to_all x3, waiting for transfers between devices: 41.4 us -> 45.7 us  [exchange(): return lax.all_to_all(a, 'blk', 0, 0, tiled=True, axis_index_groups=layers)]
    another operation x3 -> x2, local copies, waits for them, and re-layouts: 11.2 us -> 7.37 us
    transpose x2 -> x0, local copies, waits for them, and re-layouts: 3.07 us -> none  [to_samples(): turned = jnp.stack(parts, axis=2).transpose(1, 2, 0, *range(3, 7))]
    reshape x2, local copies, waits for them, and re-layouts: 10.3 us -> 7.87 us  [to_samples(): turned.reshape(ranks * modes, *turned.shape[3:]).transpose(3, 1, 2, 0)]
    another operation x2 -> x0, other arithmetic: 2.29 us -> none  [to_samples(): turned = jnp.stack(parts, axis=2).transpose(1, 2, 0, *range(3, 7))]
  transfers between devices with their start and end apart: 12 -> 12, of which waited for: 5 -> 5; matrix products, arithmetic and copies ran while one was open for 20% -> 13% of each run, Pallas kernels for 5% -> 8%
where the time goes in v5:
time: 172 us; the launch traced here: 171 us
  waiting for transfers between devices  49.9 us (29%)
  blocking collectives  48.2 us (28%)
  starting transfers between devices  25.9 us (15%)
  local copies, waits for them, and re-layouts  25.5 us (15%)
  Pallas kernels  18.9 us (11%)
  other arithmetic  1.85 us (1%)
    all_to_all x2, blocking collectives, exchange(): return lax.all_to_all(a, 'blk', 0, 0, tiled=True, axis_index_groups=layers)  48.2 us
    all_to_all x3, waiting for transfers between devices, exchange(): return lax.all_to_all(a, 'blk', 0, 0, tiled=True, axis_index_groups=layers)  45.7 us
    ppermute x9, starting transfers between devices, send(): return lax.ppermute(a, 'blk', [(i, i ^ step * inner) for i in range(ranks)])  13.6 us
    all_to_all x3, starting transfers between devices, exchange(): return lax.all_to_all(a, 'blk', 0, 0, tiled=True, axis_index_groups=layers)  12.3 us
    pallas_call x2, Pallas kernels, mix(): pl.pallas_call(mix_kernel, grid_spec=pltpu.PrefetchScalarGridSpec(num_sca...  8.96 us
    reshape x2, local copies, waits for them, and re-layouts, to_samples(): turned.reshape(ranks * modes, *turned.shape[3:]).transpose(3, 1, 2, 0)  7.87 us
    another operation x2, local copies, waits for them, and re-layouts  7.37 us
    pallas_call x1, Pallas kernels, weight_grad(): pl.pallas_call(weight_grad_kernel, grid_spec=pltpu.PrefetchScalarGridSpec...  5.03 us
  transfers between devices with their start and end apart: 12, of which 5 were waited for; matrix products, arithmetic and copies ran while one was open for 13% of the time, Pallas kernels for 8%

profile of v5, /device:TPU:0, one launch (start us, length us, event | category | flops | bytes accessed | tf_op | source)
XLA Modules:
  0.0 171.0 jit_solution(12682271708043084638)
XLA Ops:
  0.6 0.0 copy-start.4
  0.6 0.8 convert_element_type.9
  1.4 0.1 copy.35
  1.6 0.1 broadcast_in_dim.7
  1.6 0.1 reshape.28
  1.8 0.2 copy.36.refs_8_
  2.0 0.0 copy-done.4
  2.0 1.1 broadcast_multiply_fusion
  3.1 3.0 %collective-permute-start.1 = (bf16[4,2,256,256]{3,2,1,0:T(8,128)(2,1)}, bf16[4,2,256,256]{3,2,1,0:T(8,128)(2,1)}, u32[]{:S(2)}, u32[]{:S(2)}) collective-permute-start(bf16[4,2,256,256]{3,2,1,0:T(8,128)(2,1)} %broadcast_multiply_fusion), channel_id=1, source_target_pairs={{0,8},{1,9},{2,10},{3,11},{4,12},{5,13},{6,14},{7,15},{8,0},{9,1},... | collective-permute-start | bytes 3145736 | tf_op jit(solution)/shard_map/ppermute | solution.py:185
  6.1 2.6 %collective-permute-start = (bf16[4,2,256,256]{3,2,1,0:T(8,128)(2,1)}, bf16[4,2,256,256]{3,2,1,0:T(8,128)(2,1)}, u32[]{:S(2)}, u32[]{:S(2)}) collective-permute-start(bf16[4,2,256,256]{3,2,1,0:T(8,128)(2,1)} %broadcast_multiply_fusion), channel_id=1, source_target_pairs={{0,16},{1,17},{2,18},{3,19},{4,20},{5,21},{6,22},{7,23},{8,24},{9,... | collective-permute-start | bytes 3145736 | tf_op jit(solution)/shard_map/ppermute | solution.py:185
  8.7 36.7 %conditional.3 = (bf16[8,4,4,2,16,256]{5,4,3,2,1,0:T(8,128)(2,1)}, bf16[8,4,4,2,16,256]{5,4,3,2,1,0:T(8,128)(2,1)S(1)}) conditional(s32[]{:T(128)} %convert_element_type.8, () %tuple.36, (bf16[256,2,16,128]{3,2,1,0:T(8,128)(2,1)}, bf16[256,2,16,128]{3,2,1,0:T(8,128)(2,1)}) %tuple.37), branch_computations={%region_0.1_spmd, %region_1.2_spmd} | conditional | bytes 31457356 | solution.py:154
  8.7 3.9 %copy.33 = bf16[256,2,16,128]{0,2,1,3:T(8,128)(2,1)S(1)} copy(bf16[256,2,16,128]{3,2,1,0:T(8,128)(2,1)} %get-tuple-element.122) | data formatting | bytes 4194304 | tf_op jit(solution)/shard_map
  12.6 1.6 copy.30
  14.2 0.0 copy-start.3
  14.2 4.5 %all-to-all-start = ((bf16[8,4,4,2,16,256]{5,4,3,2,1,0:T(8,128)(2,1)}), bf16[8,4,4,2,16,256]{5,4,3,2,1,0:T(8,128)(2,1)}, u32[]{:S(2)}, u32[]{:S(2)}) async-start(bf16[8,4,4,2,16,256]{5,4,3,2,1,0:T(8,128)(2,1)} %copy.30), calls=%async_computation | async-start | bytes 4194304 | tf_op jit(solution)/shard_map/cond/branch_1_fun/all_to_all | solution.py:173
  18.7 0.0 copy-done.3
  18.7 3.5 %copy.34 = bf16[256,2,16,128]{0,2,1,3:T(8,128)(2,1)} copy(bf16[256,2,16,128]{3,2,1,0:T(8,128)(2,1)S(1)} %copy-done.3) | data formatting | bytes 4194304 | tf_op jit(solution)/shard_map
  22.2 1.9 %copy.40 = bf16[8,4,4,2,16,256]{5,4,3,2,1,0:T(8,128)(2,1)S(1)} copy(bf16[8,4,4,2,16,256]{5,4,3,2,0,1:T(8,128)(2,1)} %bitcast.33) | data formatting | bytes 4194304 | tf_op jit(solution)/shard_map/cond | solution.py:154
  24.0 21.3 %all-to-all-done = bf16[8,4,4,2,16,256]{5,4,3,2,1,0:T(8,128)(2,1)} async-done(((bf16[8,4,4,2,16,256]{5,4,3,2,1,0:T(8,128)(2,1)}), bf16[8,4,4,2,16,256]{5,4,3,2,1,0:T(8,128)(2,1)}, u32[]{:S(2)}, u32[]{:S(2)}) %all-to-all-start) | async-done | bytes 2097184 | tf_op jit(solution)/shard_map/cond/branch_1_fun/all_to_all | solution.py:173
  45.3 0.0 copy-start.2
  45.3 1.3 copy-done.2
  46.7 3.6 %all-to-all-start.4 = ((bf16[8,4,4,2,16,256]{5,4,3,2,1,0:T(8,128)(2,1)}), bf16[8,4,4,2,16,256]{5,4,3,2,1,0:T(8,128)(2,1)S(1)}, u32[]{:S(2)}, u32[]{:S(2)}) async-start(bf16[8,4,4,2,16,256]{5,4,3,2,1,0:T(8,128)(2,1)} %copy-done.2), calls=%async_computation.4 | async-start | bytes 4194304 | tf_op jit(solution)/shard_map/all_to_all | solution.py:173
  50.3 1.6 collective-permute-done.1
  51.9 2.6 %collective-permute-done = bf16[4,2,256,256]{3,2,1,0:T(8,128)(2,1)} collective-permute-done((bf16[4,2,256,256]{3,2,1,0:T(8,128)(2,1)}, bf16[4,2,256,256]{3,2,1,0:T(8,128)(2,1)}, u32[]{:S(2)}, u32[]{:S(2)}) %collective-permute-start) | collective-permute-done | bytes 1048608 | tf_op jit(solution)/shard_map/ppermute | solution.py:185
  54.5 0.4 collective-permute-start.2
  54.9 2.5 %dynamic-slice_bitcast_fusion.1 = (bf16[8,4,2,16,256]{4,3,2,1,0:T(8,128)(2,1)}, bf16[8,4,2,16,256]{4,3,2,1,0:T(8,128)(2,1)}, bf16[8,4,2,16,256]{4,3,2,1,0:T(8,128)(2,1)}) fusion(bf16[8,4,4,2,16,256]{5,4,3,2,1,0:T(8,128)(2,1)} %get-tuple-element.72.refs_0_, s32[]{:T(128)S(6)} %select_n.22, s32[]{:T(128)S(6)} %select_n.21, s32[]{:T(128)S(6)} %select_n.20), kind=kLoop, calls=%fused_computation.1 | loop fusion | bytes 3145740 | tf_op jit(solution)/shard_map/jit(dynamic_index_in_dim)/squeeze | solution.py:188
  57.4 2.1 %collective-permute-start.7 = (bf16[8,4,2,16,256]{4,3,2,1,0:T(8,128)(2,1)}, bf16[8,4,2,16,256]{4,3,2,1,0:T(8,128)(2,1)S(1)}, u32[]{:S(2)}, u32[]{:S(2)}) collective-permute-start(bf16[8,4,2,16,256]{4,3,2,1,0:T(8,128)(2,1)} %get-tuple-element.128), channel_id=1, source_target_pairs={{0,24},{1,25},{2,26},{3,27},{4,28},{5,29},{6,30},{7,31},{8,16},{9,... | collective-permute-start | bytes 1572872 | tf_op jit(solution)/shard_map/ppermute | solution.py:185
  59.5 1.0 collective-permute-start.5
  60.5 16.4 %all-to-all-done.4.refs_1_ = bf16[8,4,4,2,16,256]{5,4,3,2,1,0:T(8,128)(2,1)S(1)} async-done(((bf16[8,4,4,2,16,256]{5,4,3,2,1,0:T(8,128)(2,1)}), bf16[8,4,4,2,16,256]{5,4,3,2,1,0:T(8,128)(2,1)S(1)}, u32[]{:S(2)}, u32[]{:S(2)}) %all-to-all-start.4) | async-done | bytes 2097184 | tf_op jit(solution)/shard_map/all_to_all | solution.py:173
  76.8 0.0 copy-start.1
  76.9 1.2 dynamic-slice_bitcast_fusion
  78.1 0.0 collective-permute-start.8
  78.1 1.9 %collective-permute-start.6 = (bf16[8,4,2,16,256]{4,3,2,1,0:T(8,128)(2,1)}, bf16[8,4,2,16,256]{4,3,2,1,0:T(8,128)(2,1)}, u32[]{:S(2)}, u32[]{:S(2)}) collective-permute-start(bf16[8,4,2,16,256]{4,3,2,1,0:T(8,128)(2,1)} %get-tuple-element.126), channel_id=1, source_target_pairs={{0,16},{1,17},{2,18},{3,19},{4,20},{5,21},{6,22},{7,23},{8,24},{9,... | collective-permute-start | bytes 1572872 | tf_op jit(solution)/shard_map/ppermute | solution.py:185
  80.0 33.9 %conditional.4 = (bf16[8,2,2,4,2,16,256]{6,5,4,3,2,1,0:T(8,128)(2,1)}) conditional(s32[]{:T(128)} %convert_element_type.8, () %tuple.40, (s32[1]{0:T(128)}, bf16[8,4,4,2,16,256]{5,4,3,2,1,0:T(8,128)(2,1)}, bf16[8,4,4,2,16,256]{5,4,3,2,1,0:T(8,128)(2,1)S(1)}, bf16[4,2,256,256]{3,2,1,0:T(8,128)(2,1)}, bf16[4,2,256,256]{3,2,1,0:T(8,128)(2,1)}) %tuple.41), branch_computations={%region_2.3_spmd, %region_3.4_spmd} | conditional | bytes 4194312 | solution.py:154
  80.0 4.1 %mix.2 = bf16[8,2,2,4,2,16,256]{6,5,4,3,2,1,0:T(8,128)(2,1)S(1)} custom-call(s32[1]{0:T(128)} %get-tuple-element.31.layer_ref, bf16[8,4,4,2,16,256]{5,4,3,2,1,0:T(8,128)(2,1)} %get-tuple-element.32.x_ref, bf16[8,4,4,2,16,256]{5,4,3,2,1,0:T(8,128)(2,1)S(1)} %get-tuple-element.33.g_ref, bf16[4,2,256,256]{3,2,1,0:T(8,128)(2,1)} %get-tuple-element.34.same_ref, ...), custom_call_target="tpu_custom_call" | custom-call | tf_op jit(solution)/shard_map/cond/branch_1_fun/mix/pallas_call | solution.py:71
  84.1 29.8 %all_to_all.21 = bf16[8,2,2,4,2,16,256]{6,5,4,3,2,1,0:T(8,128)(2,1)} all-to-all(bf16[8,2,2,4,2,16,256]{6,5,4,3,2,1,0:T(8,128)(2,1)S(1)} %mix.2), channel_id=1, replica_groups={{0,1,2,3,4,5,6,7},{8,9,10,11,12,13,14,15},{16,17,18,19,20,21,22,23},{24..., dimensions={0} | all-to-all | bytes 4194304 | tf_op jit(solution)/shard_map/cond/branch_1_fun/all_to_all | solution.py:173
  113.9 0.0 collective-permute-done.2
  113.9 2.5 %collective-permute-start.3 = (bf16[8,4,2,16,256]{4,3,2,1,0:T(8,128)(2,1)}, bf16[8,4,2,16,256]{4,3,2,1,0:T(8,128)(2,1)}, u32[]{:S(2)}, u32[]{:S(2)}) collective-permute-start(bf16[8,4,2,16,256]{4,3,2,1,0:T(8,128)(2,1)} %get-tuple-element.82), channel_id=1, source_target_pairs={{0,8},{1,9},{2,10},{3,11},{4,12},{5,13},{6,14},{7,15},{8,0},{9,1},... | collective-permute-start | bytes 1572872 | tf_op jit(solution)/shard_map/ppermute | solution.py:185
  116.4 0.0 collective-permute-done.7.refs_6_
  116.4 0.1 collective-permute-start.4
  116.5 0.0 copy-done.1
  116.5 49.5 %conditional.5 = (bf16[256,2,16,128]{3,2,1,0:T(8,128)(2,1)}, bf16[256,2,16,128]{3,2,1,0:T(8,128)(2,1)}) conditional(s32[]{:T(128)} %convert_element_type.8, () %tuple.35, (s32[1]{0:T(128)}, bf16[8,4,4,2,16,256]{5,4,3,2,1,0:T(8,128)(2,1)}, bf16[8,4,4,2,16,256]{5,4,3,2,1,0:T(8,128)(2,1)S(1)}, bf16[4,2,256,256]{3,2,1,0:T(8,128)(2,1)}, ...), branch_computations={%region_4.5_spmd, %region_5.6_spmd} | conditional | bytes 17825868 | solution.py:154
  116.5 4.8 %mix.3 = (bf16[8,2,4,2,16,256]{5,4,3,2,1,0:T(8,128)(2,1)S(1)}, bf16[8,2,4,2,16,256]{5,4,3,2,1,0:T(8,128)(2,1)}) custom-call(s32[1]{0:T(128)} %get-tuple-element.37.layer_ref, bf16[8,4,4,2,16,256]{5,4,3,2,1,0:T(8,128)(2,1)} %get-tuple-element.38.x_ref, bf16[8,4,4,2,16,256]{5,4,3,2,1,0:T(8,128)(2,1)S(1)} %get-tuple-element.39.g_ref, ...), custom_call_target="tpu_custom_call" | custom-call | tf_op jit(solution)/shard_map/cond/branch_1_fun/mix/pallas_call | solution.py:71
  121.3 18.5 %all_to_all.22.other_ref = bf16[8,2,4,2,16,256]{5,4,3,2,1,0:T(8,128)(2,1)} all-to-all(bf16[8,2,4,2,16,256]{5,4,3,2,1,0:T(8,128)(2,1)S(1)} %get-tuple-element.43), channel_id=1, replica_groups={{0,1,2,3,4,5,6,7},{8,9,10,11,12,13,14,15},{16,17,18,19,20,21,22,23},{24..., dimensions={0} | all-to-all | bytes 2097152 | tf_op jit(solution)/shard_map/cond/branch_1_fun/all_to_all | solution.py:173
  139.8 4.3 %all-to-all-start.2 = ((bf16[8,2,4,2,16,256]{5,4,3,2,1,0:T(8,128)(2,1)}), bf16[8,2,4,2,16,256]{5,4,3,2,1,0:T(8,128)(2,1)}, u32[]{:S(2)}, u32[]{:S(2)}) async-start(bf16[8,2,4,2,16,256]{5,4,3,2,1,0:T(8,128)(2,1)} %get-tuple-element.42), calls=%async_computation.2 | async-start | bytes 2097152 | tf_op jit(solution)/shard_map/cond/branch_1_fun/all_to_all | solution.py:173
  144.0 0.0 copy-start
  144.0 1.2 copy-done
  145.2 2.3 %gather.2 = bf16[4,8,4,2,16,256]{5,4,3,2,1,0:T(8,128)(2,1)S(1)} custom-call(s32[1]{0:T(128)} %get-tuple-element.37.layer_ref, bf16[8,2,2,4,2,16,256]{6,5,4,3,2,1,0:T(8,128)(2,1)} %get-tuple-element.45.same_ref, bf16[8,2,4,2,16,256]{5,4,3,2,1,0:T(8,128)(2,1)S(1)} %copy-done), custom_call_target="tpu_custom_call" | custom-call | tf_op jit(solution)/shard_map/cond/branch_1_fun/gather/pallas_call | solution.py:101
  147.5 3.9 %copy.31 = bf16[128,2,16,256]{0,2,1,3:T(8,128)(2,1)} copy(bf16[128,2,16,256]{3,2,1,0:T(8,128)(2,1)S(1)} %bitcast.30) | data formatting | bytes 4194304 | tf_op jit(solution)/shard_map/cond/branch_1_fun/reshape | solution.py:181
  151.5 8.0 %all-to-all-done.2.other_ref = bf16[8,2,4,2,16,256]{5,4,3,2,1,0:T(8,128)(2,1)} async-done(((bf16[8,2,4,2,16,256]{5,4,3,2,1,0:T(8,128)(2,1)}), bf16[8,2,4,2,16,256]{5,4,3,2,1,0:T(8,128)(2,1)}, u32[]{:S(2)}, u32[]{:S(2)}) %all-to-all-start.2) | async-done | bytes 1048608 | tf_op jit(solution)/shard_map/cond/branch_1_fun/all_to_all | solution.py:173
  159.4 2.6 %gather.3 = bf16[4,8,4,2,16,256]{5,4,3,2,1,0:T(8,128)(2,1)S(1)} custom-call(s32[1]{0:T(128)} %get-tuple-element.37.layer_ref, bf16[8,2,2,4,2,16,256]{6,5,4,3,2,1,0:T(8,128)(2,1)} %get-tuple-element.45.same_ref, bf16[8,2,4,2,16,256]{5,4,3,2,1,0:T(8,128)(2,1)} %all-to-all-done.2.other_ref), custom_call_target="tpu_custom_call" | custom-call | tf_op jit(solution)/shard_map/cond/branch_1_fun/gather/pallas_call | solution.py:101
  162.0 3.9 %copy.32 = bf16[128,2,16,256]{0,2,1,3:T(8,128)(2,1)} copy(bf16[128,2,16,256]{3,2,1,0:T(8,128)(2,1)S(1)} %bitcast.31) | data formatting | bytes 4194304 | tf_op jit(solution)/shard_map/cond/branch_1_fun/reshape | solution.py:181
  166.0 0.0 collective-permute-done.5.refs_4_
  166.0 0.0 collective-permute-done.8.refs_7_
  166.0 0.0 collective-permute-done.6.refs_5_
  166.0 0.0 collective-permute-done.3.refs_2_
  166.0 0.0 collective-permute-done.4.refs_3_
  166.0 5.0 %weight_grad.1 = f32[4,2,256,256]{3,2,1,0:T(8,128)} custom-call(s32[1]{0:T(128)} %bitcast.14.layer_ref, bf16[8,4,4,2,16,256]{5,4,3,2,1,0:T(8,128)(2,1)} %get-tuple-element.72.refs_0_, bf16[8,4,4,2,16,256]{5,4,3,2,1,0:T(8,128)(2,1)} %copy-done.1, bf16[8,4,2,16,256]{4,3,2,1,0:T(8,128)(2,1)} %collective-permute-done.3.refs_2_, ...), custom_call_target="tpu_custom_call" | custom-call | tf_op jit(solution)/shard_map/weight_grad/pallas_call | solution.py:138
  (1 shorter events, 0.0 us)
Async XLA Ops:
  0.6 1.4 copy-start.4
  3.1 48.8 %collective-permute-start.1 = (bf16[4,2,256,256]{3,2,1,0:T(8,128)(2,1)}, bf16[4,2,256,256]{3,2,1,0:T(8,128)(2,1)}, u32[]{:S(2)}, u32[]{:S(2)}) collective-permute-start(bf16[4,2,256,256]{3,2,1,0:T(8,128)(2,1)} %broadcast_multiply_fusion), channel_id=1, source_target_pairs={{0,8},{1,9},{2,10},{3,11},{4,12},{5,13},{6,14},{7,15},{8,0},{9,1},... | collective-permute-start | bytes 3145736 | tf_op jit(solution)/shard_map/ppermute | solution.py:185
  6.1 48.4 %collective-permute-start = (bf16[4,2,256,256]{3,2,1,0:T(8,128)(2,1)}, bf16[4,2,256,256]{3,2,1,0:T(8,128)(2,1)}, u32[]{:S(2)}, u32[]{:S(2)}) collective-permute-start(bf16[4,2,256,256]{3,2,1,0:T(8,128)(2,1)} %broadcast_multiply_fusion), channel_id=1, source_target_pairs={{0,16},{1,17},{2,18},{3,19},{4,20},{5,21},{6,22},{7,23},{8,24},{9,... | collective-permute-start | bytes 3145736 | tf_op jit(solution)/shard_map/ppermute | solution.py:185
  14.2 4.5 %copy-start.3 = (bf16[256,2,16,128]{3,2,1,0:T(8,128)(2,1)S(1)}, bf16[256,2,16,128]{3,2,1,0:T(8,128)(2,1)}, u32[]{:S(2)}) copy-start(bf16[256,2,16,128]{3,2,1,0:T(8,128)(2,1)} %get-tuple-element.123) | copy-start | bytes 6291460 | tf_op jit(solution)/shard_map/cond
  14.2 31.1 %all-to-all-start = ((bf16[8,4,4,2,16,256]{5,4,3,2,1,0:T(8,128)(2,1)}), bf16[8,4,4,2,16,256]{5,4,3,2,1,0:T(8,128)(2,1)}, u32[]{:S(2)}, u32[]{:S(2)}) async-start(bf16[8,4,4,2,16,256]{5,4,3,2,1,0:T(8,128)(2,1)} %copy.30), calls=%async_computation | async-start | bytes 4194304 | tf_op jit(solution)/shard_map/cond/branch_1_fun/all_to_all | solution.py:173
  45.3 1.3 copy-start.2
  46.7 30.2 %all-to-all-start.4 = ((bf16[8,4,4,2,16,256]{5,4,3,2,1,0:T(8,128)(2,1)}), bf16[8,4,4,2,16,256]{5,4,3,2,1,0:T(8,128)(2,1)S(1)}, u32[]{:S(2)}, u32[]{:S(2)}) async-start(bf16[8,4,4,2,16,256]{5,4,3,2,1,0:T(8,128)(2,1)} %copy-done.2), calls=%async_computation.4 | async-start | bytes 4194304 | tf_op jit(solution)/shard_map/all_to_all | solution.py:173
  54.5 59.5 %collective-permute-start.2 = (bf16[4,2,256,256]{3,2,1,0:T(8,128)(2,1)}, bf16[4,2,256,256]{3,2,1,0:T(8,128)(2,1)}, u32[]{:S(2)}, u32[]{:S(2)}) collective-permute-start(bf16[4,2,256,256]{3,2,1,0:T(8,128)(2,1)} %collective-permute-done), channel_id=1, source_target_pairs={{0,8},{1,9},{2,10},{3,11},{4,12},{5,13},{6,14},{7,15},{8,0},{9,1},... | collective-permute-start | bytes 3145736 | tf_op jit(solution)/shard_map/ppermute | solution.py:185
  57.4 59.0 %collective-permute-start.7 = (bf16[8,4,2,16,256]{4,3,2,1,0:T(8,128)(2,1)}, bf16[8,4,2,16,256]{4,3,2,1,0:T(8,128)(2,1)S(1)}, u32[]{:S(2)}, u32[]{:S(2)}) collective-permute-start(bf16[8,4,2,16,256]{4,3,2,1,0:T(8,128)(2,1)} %get-tuple-element.128), channel_id=1, source_target_pairs={{0,24},{1,25},{2,26},{3,27},{4,28},{5,29},{6,30},{7,31},{8,16},{9,... | collective-permute-start | bytes 1572872 | tf_op jit(solution)/shard_map/ppermute | solution.py:185
  59.5 106.5 %collective-permute-start.5 = (bf16[8,4,2,16,256]{4,3,2,1,0:T(8,128)(2,1)}, bf16[8,4,2,16,256]{4,3,2,1,0:T(8,128)(2,1)}, u32[]{:S(2)}, u32[]{:S(2)}) collective-permute-start(bf16[8,4,2,16,256]{4,3,2,1,0:T(8,128)(2,1)} %get-tuple-element.129), channel_id=1, source_target_pairs={{0,16},{1,17},{2,18},{3,19},{4,20},{5,21},{6,22},{7,23},{8,24},{9,... | collective-permute-start | bytes 1572872 | tf_op jit(solution)/shard_map/ppermute | solution.py:185
  76.8 39.6 %copy-start.1 = (bf16[8,4,4,2,16,256]{5,4,3,2,1,0:T(8,128)(2,1)}, bf16[8,4,4,2,16,256]{5,4,3,2,1,0:T(8,128)(2,1)S(1)}, u32[]{:S(2)}) copy-start(bf16[8,4,4,2,16,256]{5,4,3,2,1,0:T(8,128)(2,1)S(1)} %all-to-all-done.4.refs_1_) | copy-start | bytes 6291460
  78.1 87.9 %collective-permute-start.8 = (bf16[8,4,2,16,256]{4,3,2,1,0:T(8,128)(2,1)}, bf16[8,4,2,16,256]{4,3,2,1,0:T(8,128)(2,1)}, u32[]{:S(2)}, u32[]{:S(2)}) collective-permute-start(bf16[8,4,2,16,256]{4,3,2,1,0:T(8,128)(2,1)} %get-tuple-element.125), channel_id=1, source_target_pairs={{0,24},{1,25},{2,26},{3,27},{4,28},{5,29},{6,30},{7,31},{8,16},{9,... | collective-permute-start | bytes 1572872 | tf_op jit(solution)/shard_map/ppermute | solution.py:185
  78.1 87.9 %collective-permute-start.6 = (bf16[8,4,2,16,256]{4,3,2,1,0:T(8,128)(2,1)}, bf16[8,4,2,16,256]{4,3,2,1,0:T(8,128)(2,1)}, u32[]{:S(2)}, u32[]{:S(2)}) collective-permute-start(bf16[8,4,2,16,256]{4,3,2,1,0:T(8,128)(2,1)} %get-tuple-element.126), channel_id=1, source_target_pairs={{0,16},{1,17},{2,18},{3,19},{4,20},{5,21},{6,22},{7,23},{8,24},{9,... | collective-permute-start | bytes 1572872 | tf_op jit(solution)/shard_map/ppermute | solution.py:185
  113.9 52.1 %collective-permute-start.3 = (bf16[8,4,2,16,256]{4,3,2,1,0:T(8,128)(2,1)}, bf16[8,4,2,16,256]{4,3,2,1,0:T(8,128)(2,1)}, u32[]{:S(2)}, u32[]{:S(2)}) collective-permute-start(bf16[8,4,2,16,256]{4,3,2,1,0:T(8,128)(2,1)} %get-tuple-element.82), channel_id=1, source_target_pairs={{0,8},{1,9},{2,10},{3,11},{4,12},{5,13},{6,14},{7,15},{8,0},{9,1},... | collective-permute-start | bytes 1572872 | tf_op jit(solution)/shard_map/ppermute | solution.py:185
  116.4 49.6 %collective-permute-start.4 = (bf16[8,4,2,16,256]{4,3,2,1,0:T(8,128)(2,1)}, bf16[8,4,2,16,256]{4,3,2,1,0:T(8,128)(2,1)}, u32[]{:S(2)}, u32[]{:S(2)}) collective-permute-start(bf16[8,4,2,16,256]{4,3,2,1,0:T(8,128)(2,1)} %get-tuple-element.83), channel_id=1, source_target_pairs={{0,8},{1,9},{2,10},{3,11},{4,12},{5,13},{6,14},{7,15},{8,0},{9,1},... | collective-permute-start | bytes 1572872 | tf_op jit(solution)/shard_map/ppermute | solution.py:185
  139.8 19.7 %all-to-all-start.2 = ((bf16[8,2,4,2,16,256]{5,4,3,2,1,0:T(8,128)(2,1)}), bf16[8,2,4,2,16,256]{5,4,3,2,1,0:T(8,128)(2,1)}, u32[]{:S(2)}, u32[]{:S(2)}) async-start(bf16[8,2,4,2,16,256]{5,4,3,2,1,0:T(8,128)(2,1)} %get-tuple-element.42), calls=%async_computation.2 | async-start | bytes 2097152 | tf_op jit(solution)/shard_map/cond/branch_1_fun/all_to_all | solution.py:173
  144.0 1.2 copy-start

commit v6 on v5

--- a/solution.py
+++ b/solution.py
@@ -92,18 +92,19 @@
 
 
 def gather(layer, same, kind, other):
-    inner, _, modes, _, samples, channels = other.shape
-    block = (inner, 1, modes, 2, samples, channels)
-    if same.ndim == 7:
-        same_spec = pl.BlockSpec((inner, 1, *block[1:]), lambda h, p, layer: (0, kind, h, 0, 0, 0, 0))
-    else:
-        same_spec = pl.BlockSpec(block, lambda h, p, layer: (0, h, 0, 0, 0, 0))
+    inner, modes, samples, channels = other.shape[0], other.shape[-4], *other.shape[-2:]
+
+    def half(a):
+        if a.ndim == 7:
+            return pl.BlockSpec((inner, 1, 1, modes, 2, samples, channels), lambda h, p, layer: (0, kind, h, 0, 0, 0, 0))
+        return pl.BlockSpec((inner, 1, modes, 2, samples, channels), lambda h, p, layer: (0, h, 0, 0, 0, 0))
+
     return pl.pallas_call(
         gather_kernel,
         grid_spec=pltpu.PrefetchScalarGridSpec(
             num_scalar_prefetch=1,
             grid=(2, 2),
-            in_specs=[same_spec, pl.BlockSpec(block, lambda h, p, layer: (0, h, 0, 0, 0, 0))],
+            in_specs=[half(same), half(other)],
             out_specs=pl.BlockSpec((1, inner, modes, 2, samples, channels), lambda h, p, layer: (2 * h + p, 0, 0, 0, 0, 0)),
         ),
         out_shape=jax.ShapeDtypeStruct((4, inner, modes, 2, samples, channels), other.dtype),
@@ -194,10 +195,8 @@
         return [exchange(a) for a in out]
 
     def outward(x, g, ws, same):
-        y, d = mixed(1, False, x, g, ws)
-        spec_out = to_samples(same[0], 0, y)
-        same, d, spec_out = lax.optimization_barrier((same, d, spec_out))
-        return spec_out, to_samples(same[-1], 1, d)
+        other = mixed(1, chans == 1, x, g, ws)
+        return to_samples(same[0], 0, other[0]), to_samples(same[-1], 1, other[-1])
 
     barrier = lax.optimization_barrier
     place = layer.astype(jnp.int32).reshape(1)

time: 172 us -> 171 us (level)
  blocking collectives: 48.2 us -> 58.9 us
  waiting for transfers between devices: 49.9 us -> 41.9 us
  starting transfers between devices: 25.9 us -> 21.6 us
  local copies, waits for them, and re-layouts: 25.5 us -> 29.5 us
  Pallas kernels: 18.9 us -> 16 us
    all_to_all x2, blocking collectives: 48.2 us -> 58.9 us  [exchange(): return lax.all_to_all(a, 'blk', 0, 0, tiled=True, axis_index_groups=layers)]
    all_to_all x3 -> x2, waiting for transfers between devices: 45.7 us -> 37.7 us  [exchange(): return lax.all_to_all(a, 'blk', 0, 0, tiled=True, axis_index_groups=layers)]
    all_to_all x3 -> x2, starting transfers between devices: 12.3 us -> 8.08 us  [exchange(): return lax.all_to_all(a, 'blk', 0, 0, tiled=True, axis_index_groups=layers)]
    reshape x2, local copies, waits for them, and re-layouts: 7.87 us -> 10.3 us  [to_samples(): turned.reshape(ranks * modes, *turned.shape[3:]).transpose(3, 1, 2, 0)]
    pallas_call x2, Pallas kernels: 4.85 us -> 2.7 us  [gather(): pl.pallas_call(gather_kernel, grid_spec=pltpu.PrefetchScalarGridSpec(num_...]
  transfers between devices with their start and end apart: 12 -> 11, of which waited for: 5 -> 4; matrix products, arithmetic and copies ran while one was open for 13% -> 15% of each run, Pallas kernels for 8% -> 6%
where the time goes in v6:
time: 171 us
  blocking collectives  58.9 us (34%)
  waiting for transfers between devices  41.9 us (25%)
  local copies, waits for them, and re-layouts  29.5 us (17%)
  starting transfers between devices  21.6 us (13%)
  Pallas kernels  16 us (9%)
  other arithmetic  1.85 us (1%)
    all_to_all x2, blocking collectives, exchange(): return lax.all_to_all(a, 'blk', 0, 0, tiled=True, axis_index_groups=layers)  58.9 us
    all_to_all x2, waiting for transfers between devices, exchange(): return lax.all_to_all(a, 'blk', 0, 0, tiled=True, axis_index_groups=layers)  37.7 us
    ppermute x9, starting transfers between devices, send(): return lax.ppermute(a, 'blk', [(i, i ^ step * inner) for i in range(ranks)])  13.6 us
    reshape x2, local copies, waits for them, and re-layouts, to_samples(): turned.reshape(ranks * modes, *turned.shape[3:]).transpose(3, 1, 2, 0)  10.3 us
    pallas_call x2, Pallas kernels, mix(): pl.pallas_call(mix_kernel, grid_spec=pltpu.PrefetchScalarGridSpec(num_sca...  8.27 us
    all_to_all x2, starting transfers between devices, exchange(): return lax.all_to_all(a, 'blk', 0, 0, tiled=True, axis_index_groups=layers)  8.08 us
    another operation x2, local copies, waits for them, and re-layouts  7.37 us
    pallas_call x1, Pallas kernels, weight_grad(): pl.pallas_call(weight_grad_kernel, grid_spec=pltpu.PrefetchScalarGridSpec...  5.04 us
  transfers between devices with their start and end apart: 11, of which 4 were waited for; matrix products, arithmetic and copies ran while one was open for 15% of the time, Pallas kernels for 6%

profile of v6, /device:TPU:0, one launch (start us, length us, event | category | flops | bytes accessed | tf_op | source)
XLA Modules:
  0.0 170.6 jit_solution(15527886131968897003)
XLA Ops:
  0.6 0.0 copy-start.6
  0.6 0.8 convert_element_type.9
  1.4 0.1 copy.35
  1.6 0.1 broadcast_in_dim.7
  1.6 0.1 reshape.28
  1.8 0.2 copy.36.refs_8_
  2.0 0.0 copy-done.6
  2.0 1.1 broadcast_multiply_fusion
  3.1 3.0 %collective-permute-start.1 = (bf16[4,2,256,256]{3,2,1,0:T(8,128)(2,1)}, bf16[4,2,256,256]{3,2,1,0:T(8,128)(2,1)}, u32[]{:S(2)}, u32[]{:S(2)}) collective-permute-start(bf16[4,2,256,256]{3,2,1,0:T(8,128)(2,1)} %broadcast_multiply_fusion), channel_id=1, source_target_pairs={{0,8},{1,9},{2,10},{3,11},{4,12},{5,13},{6,14},{7,15},{8,0},{9,1},... | collective-permute-start | bytes 3145736 | tf_op jit(solution)/shard_map/ppermute | solution.py:186
  6.1 2.6 %collective-permute-start = (bf16[4,2,256,256]{3,2,1,0:T(8,128)(2,1)}, bf16[4,2,256,256]{3,2,1,0:T(8,128)(2,1)}, u32[]{:S(2)}, u32[]{:S(2)}) collective-permute-start(bf16[4,2,256,256]{3,2,1,0:T(8,128)(2,1)} %broadcast_multiply_fusion), channel_id=1, source_target_pairs={{0,16},{1,17},{2,18},{3,19},{4,20},{5,21},{6,22},{7,23},{8,24},{9,... | collective-permute-start | bytes 3145736 | tf_op jit(solution)/shard_map/ppermute | solution.py:186
  8.7 36.7 %conditional.3 = (bf16[8,4,4,2,16,256]{5,4,3,2,1,0:T(8,128)(2,1)}, bf16[8,4,4,2,16,256]{5,4,3,2,1,0:T(8,128)(2,1)S(1)}) conditional(s32[]{:T(128)} %convert_element_type.8, () %tuple.35, (bf16[256,2,16,128]{3,2,1,0:T(8,128)(2,1)}, bf16[256,2,16,128]{3,2,1,0:T(8,128)(2,1)}) %tuple.36), branch_computations={%region_0.1_spmd, %region_1.2_spmd} | conditional | bytes 31457356 | solution.py:155
  8.7 3.9 %copy.33 = bf16[256,2,16,128]{0,2,1,3:T(8,128)(2,1)S(1)} copy(bf16[256,2,16,128]{3,2,1,0:T(8,128)(2,1)} %get-tuple-element.117) | data formatting | bytes 4194304 | tf_op jit(solution)/shard_map
  12.6 1.6 copy.30
  14.2 0.0 copy-start.5
  14.2 4.5 %all-to-all-start = ((bf16[8,4,4,2,16,256]{5,4,3,2,1,0:T(8,128)(2,1)}), bf16[8,4,4,2,16,256]{5,4,3,2,1,0:T(8,128)(2,1)}, u32[]{:S(2)}, u32[]{:S(2)}) async-start(bf16[8,4,4,2,16,256]{5,4,3,2,1,0:T(8,128)(2,1)} %copy.30), calls=%async_computation | async-start | bytes 4194304 | tf_op jit(solution)/shard_map/cond/branch_1_fun/all_to_all | solution.py:174
  18.7 0.0 copy-done.5
  18.7 3.5 %copy.34 = bf16[256,2,16,128]{0,2,1,3:T(8,128)(2,1)} copy(bf16[256,2,16,128]{3,2,1,0:T(8,128)(2,1)S(1)} %copy-done.5) | data formatting | bytes 4194304 | tf_op jit(solution)/shard_map
  22.1 1.9 %copy.40 = bf16[8,4,4,2,16,256]{5,4,3,2,1,0:T(8,128)(2,1)S(1)} copy(bf16[8,4,4,2,16,256]{5,4,3,2,0,1:T(8,128)(2,1)} %bitcast.33) | data formatting | bytes 4194304 | tf_op jit(solution)/shard_map/cond | solution.py:155
  24.0 21.3 %all-to-all-done = bf16[8,4,4,2,16,256]{5,4,3,2,1,0:T(8,128)(2,1)} async-done(((bf16[8,4,4,2,16,256]{5,4,3,2,1,0:T(8,128)(2,1)}), bf16[8,4,4,2,16,256]{5,4,3,2,1,0:T(8,128)(2,1)}, u32[]{:S(2)}, u32[]{:S(2)}) %all-to-all-start) | async-done | bytes 2097184 | tf_op jit(solution)/shard_map/cond/branch_1_fun/all_to_all | solution.py:174
  45.3 0.0 copy-start.4
  45.3 1.3 copy-done.4
  46.7 3.6 %all-to-all-start.3 = ((bf16[8,4,4,2,16,256]{5,4,3,2,1,0:T(8,128)(2,1)}), bf16[8,4,4,2,16,256]{5,4,3,2,1,0:T(8,128)(2,1)S(1)}, u32[]{:S(2)}, u32[]{:S(2)}) async-start(bf16[8,4,4,2,16,256]{5,4,3,2,1,0:T(8,128)(2,1)} %copy-done.4), calls=%async_computation.3 | async-start | bytes 4194304 | tf_op jit(solution)/shard_map/all_to_all | solution.py:174
  50.3 1.6 collective-permute-done.1
  51.9 2.6 %collective-permute-done = bf16[4,2,256,256]{3,2,1,0:T(8,128)(2,1)} collective-permute-done((bf16[4,2,256,256]{3,2,1,0:T(8,128)(2,1)}, bf16[4,2,256,256]{3,2,1,0:T(8,128)(2,1)}, u32[]{:S(2)}, u32[]{:S(2)}) %collective-permute-start) | collective-permute-done | bytes 1048608 | tf_op jit(solution)/shard_map/ppermute | solution.py:186
  54.5 0.4 collective-permute-start.2
  54.9 2.6 %dynamic-slice_bitcast_fusion.1 = (bf16[8,4,2,16,256]{4,3,2,1,0:T(8,128)(2,1)}, bf16[8,4,2,16,256]{4,3,2,1,0:T(8,128)(2,1)}, bf16[8,4,2,16,256]{4,3,2,1,0:T(8,128)(2,1)}) fusion(bf16[8,4,4,2,16,256]{5,4,3,2,1,0:T(8,128)(2,1)} %get-tuple-element.67.refs_0_, s32[]{:T(128)S(6)} %select_n.22, s32[]{:T(128)S(6)} %select_n.21, s32[]{:T(128)S(6)} %select_n.20), kind=kLoop, calls=%fused_computation.1 | loop fusion | bytes 3145740 | tf_op jit(solution)/shard_map/jit(dynamic_index_in_dim)/squeeze | solution.py:189
  57.4 2.1 %collective-permute-start.7 = (bf16[8,4,2,16,256]{4,3,2,1,0:T(8,128)(2,1)}, bf16[8,4,2,16,256]{4,3,2,1,0:T(8,128)(2,1)S(1)}, u32[]{:S(2)}, u32[]{:S(2)}) collective-permute-start(bf16[8,4,2,16,256]{4,3,2,1,0:T(8,128)(2,1)} %get-tuple-element.123), channel_id=1, source_target_pairs={{0,24},{1,25},{2,26},{3,27},{4,28},{5,29},{6,30},{7,31},{8,16},{9,... | collective-permute-start | bytes 1572872 | tf_op jit(solution)/shard_map/ppermute | solution.py:186
  59.5 1.0 collective-permute-start.5
  60.5 16.3 %all-to-all-done.3.refs_1_ = bf16[8,4,4,2,16,256]{5,4,3,2,1,0:T(8,128)(2,1)S(1)} async-done(((bf16[8,4,4,2,16,256]{5,4,3,2,1,0:T(8,128)(2,1)}), bf16[8,4,4,2,16,256]{5,4,3,2,1,0:T(8,128)(2,1)S(1)}, u32[]{:S(2)}, u32[]{:S(2)}) %all-to-all-start.3) | async-done | bytes 2097184 | tf_op jit(solution)/shard_map/all_to_all | solution.py:174
  76.8 0.0 copy-start.2
  76.8 1.3 dynamic-slice_bitcast_fusion
  78.2 0.0 collective-permute-start.8
  78.2 1.9 %collective-permute-start.6 = (bf16[8,4,2,16,256]{4,3,2,1,0:T(8,128)(2,1)}, bf16[8,4,2,16,256]{4,3,2,1,0:T(8,128)(2,1)}, u32[]{:S(2)}, u32[]{:S(2)}) collective-permute-start(bf16[8,4,2,16,256]{4,3,2,1,0:T(8,128)(2,1)} %get-tuple-element.121), channel_id=1, source_target_pairs={{0,16},{1,17},{2,18},{3,19},{4,20},{5,21},{6,22},{7,23},{8,24},{9,... | collective-permute-start | bytes 1572872 | tf_op jit(solution)/shard_map/ppermute | solution.py:186
  80.1 33.9 %conditional.4 = (bf16[8,2,2,4,2,16,256]{6,5,4,3,2,1,0:T(8,128)(2,1)}) conditional(s32[]{:T(128)} %convert_element_type.8, () %tuple.39, (s32[1]{0:T(128)}, bf16[8,4,4,2,16,256]{5,4,3,2,1,0:T(8,128)(2,1)}, bf16[8,4,4,2,16,256]{5,4,3,2,1,0:T(8,128)(2,1)S(1)}, bf16[4,2,256,256]{3,2,1,0:T(8,128)(2,1)}, bf16[4,2,256,256]{3,2,1,0:T(8,128)(2,1)}) %tuple.40), branch_computations={%region_2.3_spmd, %region_3.4_spmd} | conditional | bytes 4194312 | solution.py:155
  80.1 4.1 %mix.2 = bf16[8,2,2,4,2,16,256]{6,5,4,3,2,1,0:T(8,128)(2,1)S(1)} custom-call(s32[1]{0:T(128)} %get-tuple-element.31.layer_ref, bf16[8,4,4,2,16,256]{5,4,3,2,1,0:T(8,128)(2,1)} %get-tuple-element.32.x_ref, bf16[8,4,4,2,16,256]{5,4,3,2,1,0:T(8,128)(2,1)S(1)} %get-tuple-element.33.g_ref, bf16[4,2,256,256]{3,2,1,0:T(8,128)(2,1)} %get-tuple-element.34.same_ref, ...), custom_call_target="tpu_custom_call" | custom-call | tf_op jit(solution)/shard_map/cond/branch_1_fun/mix/pallas_call | solution.py:71
  84.2 29.8 %all_to_all.17 = bf16[8,2,2,4,2,16,256]{6,5,4,3,2,1,0:T(8,128)(2,1)} all-to-all(bf16[8,2,2,4,2,16,256]{6,5,4,3,2,1,0:T(8,128)(2,1)S(1)} %mix.2), channel_id=1, replica_groups={{0,1,2,3,4,5,6,7},{8,9,10,11,12,13,14,15},{16,17,18,19,20,21,22,23},{24..., dimensions={0} | all-to-all | bytes 4194304 | tf_op jit(solution)/shard_map/cond/branch_1_fun/all_to_all | solution.py:174
  114.0 0.0 collective-permute-done.2
  114.0 2.5 %collective-permute-start.3 = (bf16[8,4,2,16,256]{4,3,2,1,0:T(8,128)(2,1)}, bf16[8,4,2,16,256]{4,3,2,1,0:T(8,128)(2,1)}, u32[]{:S(2)}, u32[]{:S(2)}) collective-permute-start(bf16[8,4,2,16,256]{4,3,2,1,0:T(8,128)(2,1)} %get-tuple-element.77), channel_id=1, source_target_pairs={{0,8},{1,9},{2,10},{3,11},{4,12},{5,13},{6,14},{7,15},{8,0},{9,1},... | collective-permute-start | bytes 1572872 | tf_op jit(solution)/shard_map/ppermute | solution.py:186
  116.5 0.0 collective-permute-done.7.refs_6_
  116.5 0.1 collective-permute-start.4
  116.5 0.0 copy-done.2
  116.5 49.0 %conditional.5 = (bf16[256,2,16,128]{3,2,1,0:T(8,128)(2,1)}, bf16[256,2,16,128]{3,2,1,0:T(8,128)(2,1)}) conditional(s32[]{:T(128)} %convert_element_type.8, () %tuple.34, (s32[1]{0:T(128)}, bf16[8,4,4,2,16,256]{5,4,3,2,1,0:T(8,128)(2,1)}, bf16[8,4,4,2,16,256]{5,4,3,2,1,0:T(8,128)(2,1)S(1)}, bf16[4,2,256,256]{3,2,1,0:T(8,128)(2,1)}, ...), branch_computations={%region_4.5_spmd, %region_5.6_spmd} | conditional | bytes 37748836 | solution.py:155
  116.5 4.1 %mix.3 = bf16[8,2,2,4,2,16,256]{6,5,4,3,2,1,0:T(8,128)(2,1)S(1)} custom-call(s32[1]{0:T(128)} %get-tuple-element.36.layer_ref, bf16[8,4,4,2,16,256]{5,4,3,2,1,0:T(8,128)(2,1)} %get-tuple-element.38.x_ref, bf16[8,4,4,2,16,256]{5,4,3,2,1,0:T(8,128)(2,1)S(1)} %get-tuple-element.39.g_ref, bf16[4,2,256,256]{3,2,1,0:T(8,128)(2,1)} %get-tuple-element.40.same_ref, ...), custom_call_target="tpu_custom_call" | custom-call | tf_op jit(solution)/shard_map/cond/branch_1_fun/mix/pallas_call | solution.py:71
  120.7 0.0 copy-start.3
  120.7 29.2 %all_to_all.18.other_ref = bf16[8,2,2,4,2,16,256]{6,5,4,3,2,1,0:T(8,128)(2,1)S(1)} all-to-all(bf16[8,2,2,4,2,16,256]{6,5,4,3,2,1,0:T(8,128)(2,1)S(1)} %mix.3), channel_id=1, replica_groups={{0,1,2,3,4,5,6,7},{8,9,10,11,12,13,14,15},{16,17,18,19,20,21,22,23},{24..., dimensions={0} | all-to-all | bytes 4194304 | tf_op jit(solution)/shard_map/cond/branch_1_fun/all_to_all | solution.py:174
  149.9 0.0 copy-done.3
  149.9 0.4 gather.2
  150.3 0.0 copy-start.1
  150.3 1.3 copy-done.1
  151.6 5.1 %copy.31 = bf16[128,2,16,256]{0,2,1,3:T(8,128)(2,1)} copy(bf16[128,2,16,256]{3,2,1,0:T(8,128)(2,1)} %bitcast.31) | data formatting | bytes 4194304 | tf_op jit(solution)/shard_map/cond/branch_1_fun/reshape | solution.py:182
  156.8 2.3 %gather.3 = bf16[4,8,4,2,16,256]{5,4,3,2,1,0:T(8,128)(2,1)S(1)} custom-call(s32[1]{0:T(128)} %get-tuple-element.36.layer_ref, bf16[8,2,2,4,2,16,256]{6,5,4,3,2,1,0:T(8,128)(2,1)} %get-tuple-element.37.same_ref, bf16[8,2,2,4,2,16,256]{6,5,4,3,2,1,0:T(8,128)(2,1)S(1)} %all_to_all.18.other_ref), custom_call_target="tpu_custom_call" | custom-call | tf_op jit(solution)/shard_map/cond/branch_1_fun/gather/pallas_call | solution.py:102
  159.0 0.0 copy-start
  159.1 1.3 copy-done
  160.4 5.1 %copy.32 = bf16[128,2,16,256]{0,2,1,3:T(8,128)(2,1)} copy(bf16[128,2,16,256]{3,2,1,0:T(8,128)(2,1)} %bitcast.30) | data formatting | bytes 4194304 | tf_op jit(solution)/shard_map/cond/branch_1_fun/reshape | solution.py:182
  165.5 0.0 collective-permute-done.5.refs_4_
  165.5 0.0 collective-permute-done.8.refs_7_
  165.5 0.0 collective-permute-done.6.refs_5_
  165.5 0.0 collective-permute-done.3.refs_2_
  165.5 0.0 collective-permute-done.4.refs_3_
  165.5 5.0 %weight_grad.1 = f32[4,2,256,256]{3,2,1,0:T(8,128)} custom-call(s32[1]{0:T(128)} %bitcast.14.layer_ref, bf16[8,4,4,2,16,256]{5,4,3,2,1,0:T(8,128)(2,1)} %get-tuple-element.67.refs_0_, bf16[8,4,4,2,16,256]{5,4,3,2,1,0:T(8,128)(2,1)} %copy-done.2, bf16[8,4,2,16,256]{4,3,2,1,0:T(8,128)(2,1)} %collective-permute-done.3.refs_2_, ...), custom_call_target="tpu_custom_call" | custom-call | tf_op jit(solution)/shard_map/weight_grad/pallas_call | solution.py:139
  (1 shorter events, 0.0 us)
Async XLA Ops:
  0.6 1.4 copy-start.6
  3.1 48.8 %collective-permute-start.1 = (bf16[4,2,256,256]{3,2,1,0:T(8,128)(2,1)}, bf16[4,2,256,256]{3,2,1,0:T(8,128)(2,1)}, u32[]{:S(2)}, u32[]{:S(2)}) collective-permute-start(bf16[4,2,256,256]{3,2,1,0:T(8,128)(2,1)} %broadcast_multiply_fusion), channel_id=1, source_target_pairs={{0,8},{1,9},{2,10},{3,11},{4,12},{5,13},{6,14},{7,15},{8,0},{9,1},... | collective-permute-start | bytes 3145736 | tf_op jit(solution)/shard_map/ppermute | solution.py:186
  6.1 48.4 %collective-permute-start = (bf16[4,2,256,256]{3,2,1,0:T(8,128)(2,1)}, bf16[4,2,256,256]{3,2,1,0:T(8,128)(2,1)}, u32[]{:S(2)}, u32[]{:S(2)}) collective-permute-start(bf16[4,2,256,256]{3,2,1,0:T(8,128)(2,1)} %broadcast_multiply_fusion), channel_id=1, source_target_pairs={{0,16},{1,17},{2,18},{3,19},{4,20},{5,21},{6,22},{7,23},{8,24},{9,... | collective-permute-start | bytes 3145736 | tf_op jit(solution)/shard_map/ppermute | solution.py:186
  14.2 4.5 %copy-start.5 = (bf16[256,2,16,128]{3,2,1,0:T(8,128)(2,1)S(1)}, bf16[256,2,16,128]{3,2,1,0:T(8,128)(2,1)}, u32[]{:S(2)}) copy-start(bf16[256,2,16,128]{3,2,1,0:T(8,128)(2,1)} %get-tuple-element.118) | copy-start | bytes 6291460 | tf_op jit(solution)/shard_map/cond
  14.2 31.1 %all-to-all-start = ((bf16[8,4,4,2,16,256]{5,4,3,2,1,0:T(8,128)(2,1)}), bf16[8,4,4,2,16,256]{5,4,3,2,1,0:T(8,128)(2,1)}, u32[]{:S(2)}, u32[]{:S(2)}) async-start(bf16[8,4,4,2,16,256]{5,4,3,2,1,0:T(8,128)(2,1)} %copy.30), calls=%async_computation | async-start | bytes 4194304 | tf_op jit(solution)/shard_map/cond/branch_1_fun/all_to_all | solution.py:174
  45.3 1.3 copy-start.4
  46.7 30.2 %all-to-all-start.3 = ((bf16[8,4,4,2,16,256]{5,4,3,2,1,0:T(8,128)(2,1)}), bf16[8,4,4,2,16,256]{5,4,3,2,1,0:T(8,128)(2,1)S(1)}, u32[]{:S(2)}, u32[]{:S(2)}) async-start(bf16[8,4,4,2,16,256]{5,4,3,2,1,0:T(8,128)(2,1)} %copy-done.4), calls=%async_computation.3 | async-start | bytes 4194304 | tf_op jit(solution)/shard_map/all_to_all | solution.py:174
  54.5 59.5 %collective-permute-start.2 = (bf16[4,2,256,256]{3,2,1,0:T(8,128)(2,1)}, bf16[4,2,256,256]{3,2,1,0:T(8,128)(2,1)}, u32[]{:S(2)}, u32[]{:S(2)}) collective-permute-start(bf16[4,2,256,256]{3,2,1,0:T(8,128)(2,1)} %collective-permute-done), channel_id=1, source_target_pairs={{0,8},{1,9},{2,10},{3,11},{4,12},{5,13},{6,14},{7,15},{8,0},{9,1},... | collective-permute-start | bytes 3145736 | tf_op jit(solution)/shard_map/ppermute | solution.py:186
  57.4 59.0 %collective-permute-start.7 = (bf16[8,4,2,16,256]{4,3,2,1,0:T(8,128)(2,1)}, bf16[8,4,2,16,256]{4,3,2,1,0:T(8,128)(2,1)S(1)}, u32[]{:S(2)}, u32[]{:S(2)}) collective-permute-start(bf16[8,4,2,16,256]{4,3,2,1,0:T(8,128)(2,1)} %get-tuple-element.123), channel_id=1, source_target_pairs={{0,24},{1,25},{2,26},{3,27},{4,28},{5,29},{6,30},{7,31},{8,16},{9,... | collective-permute-start | bytes 1572872 | tf_op jit(solution)/shard_map/ppermute | solution.py:186
  59.5 106.0 %collective-permute-start.5 = (bf16[8,4,2,16,256]{4,3,2,1,0:T(8,128)(2,1)}, bf16[8,4,2,16,256]{4,3,2,1,0:T(8,128)(2,1)}, u32[]{:S(2)}, u32[]{:S(2)}) collective-permute-start(bf16[8,4,2,16,256]{4,3,2,1,0:T(8,128)(2,1)} %get-tuple-element.124), channel_id=1, source_target_pairs={{0,16},{1,17},{2,18},{3,19},{4,20},{5,21},{6,22},{7,23},{8,24},{9,... | collective-permute-start | bytes 1572872 | tf_op jit(solution)/shard_map/ppermute | solution.py:186
  76.8 39.7 %copy-start.2 = (bf16[8,4,4,2,16,256]{5,4,3,2,1,0:T(8,128)(2,1)}, bf16[8,4,4,2,16,256]{5,4,3,2,1,0:T(8,128)(2,1)S(1)}, u32[]{:S(2)}) copy-start(bf16[8,4,4,2,16,256]{5,4,3,2,1,0:T(8,128)(2,1)S(1)} %all-to-all-done.3.refs_1_) | copy-start | bytes 6291460
  78.2 87.3 %collective-permute-start.8 = (bf16[8,4,2,16,256]{4,3,2,1,0:T(8,128)(2,1)}, bf16[8,4,2,16,256]{4,3,2,1,0:T(8,128)(2,1)}, u32[]{:S(2)}, u32[]{:S(2)}) collective-permute-start(bf16[8,4,2,16,256]{4,3,2,1,0:T(8,128)(2,1)} %get-tuple-element.120), channel_id=1, source_target_pairs={{0,24},{1,25},{2,26},{3,27},{4,28},{5,29},{6,30},{7,31},{8,16},{9,... | collective-permute-start | bytes 1572872 | tf_op jit(solution)/shard_map/ppermute | solution.py:186
  78.2 87.3 %collective-permute-start.6 = (bf16[8,4,2,16,256]{4,3,2,1,0:T(8,128)(2,1)}, bf16[8,4,2,16,256]{4,3,2,1,0:T(8,128)(2,1)}, u32[]{:S(2)}, u32[]{:S(2)}) collective-permute-start(bf16[8,4,2,16,256]{4,3,2,1,0:T(8,128)(2,1)} %get-tuple-element.121), channel_id=1, source_target_pairs={{0,16},{1,17},{2,18},{3,19},{4,20},{5,21},{6,22},{7,23},{8,24},{9,... | collective-permute-start | bytes 1572872 | tf_op jit(solution)/shard_map/ppermute | solution.py:186
  114.0 51.5 %collective-permute-start.3 = (bf16[8,4,2,16,256]{4,3,2,1,0:T(8,128)(2,1)}, bf16[8,4,2,16,256]{4,3,2,1,0:T(8,128)(2,1)}, u32[]{:S(2)}, u32[]{:S(2)}) collective-permute-start(bf16[8,4,2,16,256]{4,3,2,1,0:T(8,128)(2,1)} %get-tuple-element.77), channel_id=1, source_target_pairs={{0,8},{1,9},{2,10},{3,11},{4,12},{5,13},{6,14},{7,15},{8,0},{9,1},... | collective-permute-start | bytes 1572872 | tf_op jit(solution)/shard_map/ppermute | solution.py:186
  116.5 49.1 %collective-permute-start.4 = (bf16[8,4,2,16,256]{4,3,2,1,0:T(8,128)(2,1)}, bf16[8,4,2,16,256]{4,3,2,1,0:T(8,128)(2,1)}, u32[]{:S(2)}, u32[]{:S(2)}) collective-permute-start(bf16[8,4,2,16,256]{4,3,2,1,0:T(8,128)(2,1)} %get-tuple-element.78), channel_id=1, source_target_pairs={{0,8},{1,9},{2,10},{3,11},{4,12},{5,13},{6,14},{7,15},{8,0},{9,1},... | collective-permute-start | bytes 1572872 | tf_op jit(solution)/shard_map/ppermute | solution.py:186
  120.7 29.2 %copy-start.3 = (bf16[8,2,2,4,2,16,256]{6,5,4,3,2,1,0:T(8,128)(2,1)S(1)}, bf16[8,2,2,4,2,16,256]{6,5,4,3,2,1,0:T(8,128)(2,1)}, u32[]{:S(2)}) copy-start(bf16[8,2,2,4,2,16,256]{6,5,4,3,2,1,0:T(8,128)(2,1)} %get-tuple-element.37.same_ref) | copy-start | bytes 6291460 | tf_op jit(solution)/shard_map/cond
  150.3 1.3 copy-start.1
  159.0 1.3 copy-start

commit v7 on v6

--- a/solution.py
+++ b/solution.py
@@ -43,7 +43,7 @@
 def mix(layer, odd, x, g, ws, y_type, joint):
     inner, outer, modes, _, samples, _ = x.shape
     ci, co = ws[0].shape[2:]
-    some = 2 if modes % 2 == 0 else 1
+    some = modes
 
     def block(channels):
         return pl.BlockSpec(
@@ -77,7 +77,7 @@
             out_specs=out_specs,
         ),
         out_shape=out_shape,
-        compiler_params=pltpu.CompilerParams(vmem_limit_bytes=40 * 1024 * 1024),
+        compiler_params=pltpu.CompilerParams(vmem_limit_bytes=48 * 1024 * 1024),
         name="mix",
     )(layer, x, g, *ws)
 

time: 171 us -> 170 us (level)
  no operation moved by 1% of the time
where the time goes in v7:
time: 170 us; the launch traced here: 169 us
  blocking collectives  58.9 us (35%)
  waiting for transfers between devices  41.9 us (25%)
  local copies, waits for them, and re-layouts  29.5 us (17%)
  starting transfers between devices  21.6 us (13%)
  Pallas kernels  14.5 us (9%)
  other arithmetic  1.85 us (1%)
    all_to_all x2, blocking collectives, exchange(): return lax.all_to_all(a, 'blk', 0, 0, tiled=True, axis_index_groups=layers)  58.9 us
    all_to_all x2, waiting for transfers between devices, exchange(): return lax.all_to_all(a, 'blk', 0, 0, tiled=True, axis_index_groups=layers)  37.7 us
    ppermute x9, starting transfers between devices, send(): return lax.ppermute(a, 'blk', [(i, i ^ step * inner) for i in range(ranks)])  13.6 us
    reshape x2, local copies, waits for them, and re-layouts, to_samples(): turned.reshape(ranks * modes, *turned.shape[3:]).transpose(3, 1, 2, 0)  10.3 us
    all_to_all x2, starting transfers between devices, exchange(): return lax.all_to_all(a, 'blk', 0, 0, tiled=True, axis_index_groups=layers)  8.08 us
    another operation x2, local copies, waits for them, and re-layouts  7.37 us
    pallas_call x2, Pallas kernels, mix(): pl.pallas_call(mix_kernel, grid_spec=pltpu.PrefetchScalarGridSpec(num_sca...  6.77 us
    pallas_call x1, Pallas kernels, weight_grad(): pl.pallas_call(weight_grad_kernel, grid_spec=pltpu.PrefetchScalarGridSpec...  5.03 us
  transfers between devices with their start and end apart: 11, of which 4 were waited for; matrix products, arithmetic and copies ran while one was open for 15% of the time, Pallas kernels for 6%

profile of v7, /device:TPU:0, one launch (start us, length us, event | category | flops | bytes accessed | tf_op | source)
XLA Modules:
  0.0 169.1 jit_solution(14861169685597474440)
XLA Ops:
  0.6 0.0 copy-start.6
  0.6 0.8 convert_element_type.9
  1.4 0.1 copy.35
  1.6 0.1 broadcast_in_dim.7
  1.6 0.1 reshape.28
  1.8 0.2 copy.36.refs_8_
  2.0 0.0 copy-done.6
  2.0 1.1 broadcast_multiply_fusion
  3.1 3.0 %collective-permute-start.1 = (bf16[4,2,256,256]{3,2,1,0:T(8,128)(2,1)}, bf16[4,2,256,256]{3,2,1,0:T(8,128)(2,1)}, u32[]{:S(2)}, u32[]{:S(2)}) collective-permute-start(bf16[4,2,256,256]{3,2,1,0:T(8,128)(2,1)} %broadcast_multiply_fusion), channel_id=1, source_target_pairs={{0,8},{1,9},{2,10},{3,11},{4,12},{5,13},{6,14},{7,15},{8,0},{9,1},... | collective-permute-start | bytes 3145736 | tf_op jit(solution)/shard_map/ppermute | solution.py:186
  6.1 2.6 %collective-permute-start = (bf16[4,2,256,256]{3,2,1,0:T(8,128)(2,1)}, bf16[4,2,256,256]{3,2,1,0:T(8,128)(2,1)}, u32[]{:S(2)}, u32[]{:S(2)}) collective-permute-start(bf16[4,2,256,256]{3,2,1,0:T(8,128)(2,1)} %broadcast_multiply_fusion), channel_id=1, source_target_pairs={{0,16},{1,17},{2,18},{3,19},{4,20},{5,21},{6,22},{7,23},{8,24},{9,... | collective-permute-start | bytes 3145736 | tf_op jit(solution)/shard_map/ppermute | solution.py:186
  8.7 36.7 %conditional.3 = (bf16[8,4,4,2,16,256]{5,4,3,2,1,0:T(8,128)(2,1)}, bf16[8,4,4,2,16,256]{5,4,3,2,1,0:T(8,128)(2,1)S(1)}) conditional(s32[]{:T(128)} %convert_element_type.8, () %tuple.35, (bf16[256,2,16,128]{3,2,1,0:T(8,128)(2,1)}, bf16[256,2,16,128]{3,2,1,0:T(8,128)(2,1)}) %tuple.36), branch_computations={%region_0.1_spmd, %region_1.2_spmd} | conditional | bytes 31457356 | solution.py:155
  8.7 3.9 %copy.33 = bf16[256,2,16,128]{0,2,1,3:T(8,128)(2,1)S(1)} copy(bf16[256,2,16,128]{3,2,1,0:T(8,128)(2,1)} %get-tuple-element.117) | data formatting | bytes 4194304 | tf_op jit(solution)/shard_map
  12.6 1.6 copy.30
  14.2 0.0 copy-start.5
  14.2 4.5 %all-to-all-start = ((bf16[8,4,4,2,16,256]{5,4,3,2,1,0:T(8,128)(2,1)}), bf16[8,4,4,2,16,256]{5,4,3,2,1,0:T(8,128)(2,1)}, u32[]{:S(2)}, u32[]{:S(2)}) async-start(bf16[8,4,4,2,16,256]{5,4,3,2,1,0:T(8,128)(2,1)} %copy.30), calls=%async_computation | async-start | bytes 4194304 | tf_op jit(solution)/shard_map/cond/branch_1_fun/all_to_all | solution.py:174
  18.7 0.0 copy-done.5
  18.7 3.5 %copy.34 = bf16[256,2,16,128]{0,2,1,3:T(8,128)(2,1)} copy(bf16[256,2,16,128]{3,2,1,0:T(8,128)(2,1)S(1)} %copy-done.5) | data formatting | bytes 4194304 | tf_op jit(solution)/shard_map
  22.1 1.9 %copy.40 = bf16[8,4,4,2,16,256]{5,4,3,2,1,0:T(8,128)(2,1)S(1)} copy(bf16[8,4,4,2,16,256]{5,4,3,2,0,1:T(8,128)(2,1)} %bitcast.33) | data formatting | bytes 4194304 | tf_op jit(solution)/shard_map/cond | solution.py:155
  24.0 21.3 %all-to-all-done = bf16[8,4,4,2,16,256]{5,4,3,2,1,0:T(8,128)(2,1)} async-done(((bf16[8,4,4,2,16,256]{5,4,3,2,1,0:T(8,128)(2,1)}), bf16[8,4,4,2,16,256]{5,4,3,2,1,0:T(8,128)(2,1)}, u32[]{:S(2)}, u32[]{:S(2)}) %all-to-all-start) | async-done | bytes 2097184 | tf_op jit(solution)/shard_map/cond/branch_1_fun/all_to_all | solution.py:174
  45.3 0.0 copy-start.4
  45.3 1.3 copy-done.4
  46.7 3.6 %all-to-all-start.3 = ((bf16[8,4,4,2,16,256]{5,4,3,2,1,0:T(8,128)(2,1)}), bf16[8,4,4,2,16,256]{5,4,3,2,1,0:T(8,128)(2,1)S(1)}, u32[]{:S(2)}, u32[]{:S(2)}) async-start(bf16[8,4,4,2,16,256]{5,4,3,2,1,0:T(8,128)(2,1)} %copy-done.4), calls=%async_computation.3 | async-start | bytes 4194304 | tf_op jit(solution)/shard_map/all_to_all | solution.py:174
  50.3 1.6 collective-permute-done.1
  51.9 2.6 %collective-permute-done = bf16[4,2,256,256]{3,2,1,0:T(8,128)(2,1)} collective-permute-done((bf16[4,2,256,256]{3,2,1,0:T(8,128)(2,1)}, bf16[4,2,256,256]{3,2,1,0:T(8,128)(2,1)}, u32[]{:S(2)}, u32[]{:S(2)}) %collective-permute-start) | collective-permute-done | bytes 1048608 | tf_op jit(solution)/shard_map/ppermute | solution.py:186
  54.5 0.4 collective-permute-start.2
  54.9 2.6 %dynamic-slice_bitcast_fusion.1 = (bf16[8,4,2,16,256]{4,3,2,1,0:T(8,128)(2,1)}, bf16[8,4,2,16,256]{4,3,2,1,0:T(8,128)(2,1)}, bf16[8,4,2,16,256]{4,3,2,1,0:T(8,128)(2,1)}) fusion(bf16[8,4,4,2,16,256]{5,4,3,2,1,0:T(8,128)(2,1)} %get-tuple-element.67.refs_0_, s32[]{:T(128)S(6)} %select_n.22, s32[]{:T(128)S(6)} %select_n.21, s32[]{:T(128)S(6)} %select_n.20), kind=kLoop, calls=%fused_computation.1 | loop fusion | bytes 3145740 | tf_op jit(solution)/shard_map/jit(dynamic_index_in_dim)/squeeze | solution.py:189
  57.4 2.1 %collective-permute-start.7 = (bf16[8,4,2,16,256]{4,3,2,1,0:T(8,128)(2,1)}, bf16[8,4,2,16,256]{4,3,2,1,0:T(8,128)(2,1)S(1)}, u32[]{:S(2)}, u32[]{:S(2)}) collective-permute-start(bf16[8,4,2,16,256]{4,3,2,1,0:T(8,128)(2,1)} %get-tuple-element.123), channel_id=1, source_target_pairs={{0,24},{1,25},{2,26},{3,27},{4,28},{5,29},{6,30},{7,31},{8,16},{9,... | collective-permute-start | bytes 1572872 | tf_op jit(solution)/shard_map/ppermute | solution.py:186
  59.5 1.0 collective-permute-start.5
  60.5 16.3 %all-to-all-done.3.refs_1_ = bf16[8,4,4,2,16,256]{5,4,3,2,1,0:T(8,128)(2,1)S(1)} async-done(((bf16[8,4,4,2,16,256]{5,4,3,2,1,0:T(8,128)(2,1)}), bf16[8,4,4,2,16,256]{5,4,3,2,1,0:T(8,128)(2,1)S(1)}, u32[]{:S(2)}, u32[]{:S(2)}) %all-to-all-start.3) | async-done | bytes 2097184 | tf_op jit(solution)/shard_map/all_to_all | solution.py:174
  76.8 0.0 copy-start.2
  76.8 1.3 dynamic-slice_bitcast_fusion
  78.2 0.0 collective-permute-start.8
  78.2 1.9 %collective-permute-start.6 = (bf16[8,4,2,16,256]{4,3,2,1,0:T(8,128)(2,1)}, bf16[8,4,2,16,256]{4,3,2,1,0:T(8,128)(2,1)}, u32[]{:S(2)}, u32[]{:S(2)}) collective-permute-start(bf16[8,4,2,16,256]{4,3,2,1,0:T(8,128)(2,1)} %get-tuple-element.121), channel_id=1, source_target_pairs={{0,16},{1,17},{2,18},{3,19},{4,20},{5,21},{6,22},{7,23},{8,24},{9,... | collective-permute-start | bytes 1572872 | tf_op jit(solution)/shard_map/ppermute | solution.py:186
  80.1 33.2 %conditional.4 = (bf16[8,2,2,4,2,16,256]{6,5,4,3,2,1,0:T(8,128)(2,1)}) conditional(s32[]{:T(128)} %convert_element_type.8, () %tuple.39, (s32[1]{0:T(128)}, bf16[8,4,4,2,16,256]{5,4,3,2,1,0:T(8,128)(2,1)}, bf16[8,4,4,2,16,256]{5,4,3,2,1,0:T(8,128)(2,1)S(1)}, bf16[4,2,256,256]{3,2,1,0:T(8,128)(2,1)}, bf16[4,2,256,256]{3,2,1,0:T(8,128)(2,1)}) %tuple.40), branch_computations={%region_2.3_spmd, %region_3.4_spmd} | conditional | bytes 4194312 | solution.py:155
  80.1 3.4 %mix.2 = bf16[8,2,2,4,2,16,256]{6,5,4,3,2,1,0:T(8,128)(2,1)S(1)} custom-call(s32[1]{0:T(128)} %get-tuple-element.31.layer_ref, bf16[8,4,4,2,16,256]{5,4,3,2,1,0:T(8,128)(2,1)} %get-tuple-element.32.x_ref, bf16[8,4,4,2,16,256]{5,4,3,2,1,0:T(8,128)(2,1)S(1)} %get-tuple-element.33.g_ref, bf16[4,2,256,256]{3,2,1,0:T(8,128)(2,1)} %get-tuple-element.34.same_ref, ...), custom_call_target="tpu_custom_call" | custom-call | tf_op jit(solution)/shard_map/cond/branch_1_fun/mix/pallas_call | solution.py:71
  83.5 29.8 %all_to_all.17 = bf16[8,2,2,4,2,16,256]{6,5,4,3,2,1,0:T(8,128)(2,1)} all-to-all(bf16[8,2,2,4,2,16,256]{6,5,4,3,2,1,0:T(8,128)(2,1)S(1)} %mix.2), channel_id=1, replica_groups={{0,1,2,3,4,5,6,7},{8,9,10,11,12,13,14,15},{16,17,18,19,20,21,22,23},{24..., dimensions={0} | all-to-all | bytes 4194304 | tf_op jit(solution)/shard_map/cond/branch_1_fun/all_to_all | solution.py:174
  113.2 0.0 collective-permute-done.2
  113.2 2.5 %collective-permute-start.3 = (bf16[8,4,2,16,256]{4,3,2,1,0:T(8,128)(2,1)}, bf16[8,4,2,16,256]{4,3,2,1,0:T(8,128)(2,1)}, u32[]{:S(2)}, u32[]{:S(2)}) collective-permute-start(bf16[8,4,2,16,256]{4,3,2,1,0:T(8,128)(2,1)} %get-tuple-element.77), channel_id=1, source_target_pairs={{0,8},{1,9},{2,10},{3,11},{4,12},{5,13},{6,14},{7,15},{8,0},{9,1},... | collective-permute-start | bytes 1572872 | tf_op jit(solution)/shard_map/ppermute | solution.py:186
  115.7 0.0 collective-permute-done.7.refs_6_
  115.7 0.1 collective-permute-start.4
  115.8 0.0 copy-done.2
  115.8 48.2 %conditional.5 = (bf16[256,2,16,128]{3,2,1,0:T(8,128)(2,1)}, bf16[256,2,16,128]{3,2,1,0:T(8,128)(2,1)}) conditional(s32[]{:T(128)} %convert_element_type.8, () %tuple.34, (s32[1]{0:T(128)}, bf16[8,4,4,2,16,256]{5,4,3,2,1,0:T(8,128)(2,1)}, bf16[8,4,4,2,16,256]{5,4,3,2,1,0:T(8,128)(2,1)S(1)}, bf16[4,2,256,256]{3,2,1,0:T(8,128)(2,1)}, ...), branch_computations={%region_4.5_spmd, %region_5.6_spmd} | conditional | bytes 37748836 | solution.py:155
  115.8 3.4 %mix.3 = bf16[8,2,2,4,2,16,256]{6,5,4,3,2,1,0:T(8,128)(2,1)S(1)} custom-call(s32[1]{0:T(128)} %get-tuple-element.36.layer_ref, bf16[8,4,4,2,16,256]{5,4,3,2,1,0:T(8,128)(2,1)} %get-tuple-element.38.x_ref, bf16[8,4,4,2,16,256]{5,4,3,2,1,0:T(8,128)(2,1)S(1)} %get-tuple-element.39.g_ref, bf16[4,2,256,256]{3,2,1,0:T(8,128)(2,1)} %get-tuple-element.40.same_ref, ...), custom_call_target="tpu_custom_call" | custom-call | tf_op jit(solution)/shard_map/cond/branch_1_fun/mix/pallas_call | solution.py:71
  119.2 0.0 copy-start.3
  119.2 29.2 %all_to_all.18.other_ref = bf16[8,2,2,4,2,16,256]{6,5,4,3,2,1,0:T(8,128)(2,1)S(1)} all-to-all(bf16[8,2,2,4,2,16,256]{6,5,4,3,2,1,0:T(8,128)(2,1)S(1)} %mix.3), channel_id=1, replica_groups={{0,1,2,3,4,5,6,7},{8,9,10,11,12,13,14,15},{16,17,18,19,20,21,22,23},{24..., dimensions={0} | all-to-all | bytes 4194304 | tf_op jit(solution)/shard_map/cond/branch_1_fun/all_to_all | solution.py:174
  148.4 0.0 copy-done.3
  148.4 0.4 gather.2
  148.8 0.0 copy-start.1
  148.8 1.3 copy-done.1
  150.1 5.1 %copy.31 = bf16[128,2,16,256]{0,2,1,3:T(8,128)(2,1)} copy(bf16[128,2,16,256]{3,2,1,0:T(8,128)(2,1)} %bitcast.31) | data formatting | bytes 4194304 | tf_op jit(solution)/shard_map/cond/branch_1_fun/reshape | solution.py:182
  155.3 2.3 %gather.3 = bf16[4,8,4,2,16,256]{5,4,3,2,1,0:T(8,128)(2,1)S(1)} custom-call(s32[1]{0:T(128)} %get-tuple-element.36.layer_ref, bf16[8,2,2,4,2,16,256]{6,5,4,3,2,1,0:T(8,128)(2,1)} %get-tuple-element.37.same_ref, bf16[8,2,2,4,2,16,256]{6,5,4,3,2,1,0:T(8,128)(2,1)S(1)} %all_to_all.18.other_ref), custom_call_target="tpu_custom_call" | custom-call | tf_op jit(solution)/shard_map/cond/branch_1_fun/gather/pallas_call | solution.py:102
  157.6 0.0 copy-start
  157.6 1.3 copy-done
  158.9 5.1 %copy.32 = bf16[128,2,16,256]{0,2,1,3:T(8,128)(2,1)} copy(bf16[128,2,16,256]{3,2,1,0:T(8,128)(2,1)} %bitcast.30) | data formatting | bytes 4194304 | tf_op jit(solution)/shard_map/cond/branch_1_fun/reshape | solution.py:182
  164.0 0.0 collective-permute-done.5.refs_4_
  164.0 0.0 collective-permute-done.8.refs_7_
  164.0 0.0 collective-permute-done.6.refs_5_
  164.0 0.0 collective-permute-done.3.refs_2_
  164.0 0.0 collective-permute-done.4.refs_3_
  164.1 5.0 %weight_grad.1 = f32[4,2,256,256]{3,2,1,0:T(8,128)} custom-call(s32[1]{0:T(128)} %bitcast.14.layer_ref, bf16[8,4,4,2,16,256]{5,4,3,2,1,0:T(8,128)(2,1)} %get-tuple-element.67.refs_0_, bf16[8,4,4,2,16,256]{5,4,3,2,1,0:T(8,128)(2,1)} %copy-done.2, bf16[8,4,2,16,256]{4,3,2,1,0:T(8,128)(2,1)} %collective-permute-done.3.refs_2_, ...), custom_call_target="tpu_custom_call" | custom-call | tf_op jit(solution)/shard_map/weight_grad/pallas_call | solution.py:139
  (1 shorter events, 0.0 us)
Async XLA Ops:
  0.6 1.4 copy-start.6
  3.1 48.8 %collective-permute-start.1 = (bf16[4,2,256,256]{3,2,1,0:T(8,128)(2,1)}, bf16[4,2,256,256]{3,2,1,0:T(8,128)(2,1)}, u32[]{:S(2)}, u32[]{:S(2)}) collective-permute-start(bf16[4,2,256,256]{3,2,1,0:T(8,128)(2,1)} %broadcast_multiply_fusion), channel_id=1, source_target_pairs={{0,8},{1,9},{2,10},{3,11},{4,12},{5,13},{6,14},{7,15},{8,0},{9,1},... | collective-permute-start | bytes 3145736 | tf_op jit(solution)/shard_map/ppermute | solution.py:186
  6.1 48.4 %collective-permute-start = (bf16[4,2,256,256]{3,2,1,0:T(8,128)(2,1)}, bf16[4,2,256,256]{3,2,1,0:T(8,128)(2,1)}, u32[]{:S(2)}, u32[]{:S(2)}) collective-permute-start(bf16[4,2,256,256]{3,2,1,0:T(8,128)(2,1)} %broadcast_multiply_fusion), channel_id=1, source_target_pairs={{0,16},{1,17},{2,18},{3,19},{4,20},{5,21},{6,22},{7,23},{8,24},{9,... | collective-permute-start | bytes 3145736 | tf_op jit(solution)/shard_map/ppermute | solution.py:186
  14.2 4.5 %copy-start.5 = (bf16[256,2,16,128]{3,2,1,0:T(8,128)(2,1)S(1)}, bf16[256,2,16,128]{3,2,1,0:T(8,128)(2,1)}, u32[]{:S(2)}) copy-start(bf16[256,2,16,128]{3,2,1,0:T(8,128)(2,1)} %get-tuple-element.118) | copy-start | bytes 6291460 | tf_op jit(solution)/shard_map/cond
  14.2 31.1 %all-to-all-start = ((bf16[8,4,4,2,16,256]{5,4,3,2,1,0:T(8,128)(2,1)}), bf16[8,4,4,2,16,256]{5,4,3,2,1,0:T(8,128)(2,1)}, u32[]{:S(2)}, u32[]{:S(2)}) async-start(bf16[8,4,4,2,16,256]{5,4,3,2,1,0:T(8,128)(2,1)} %copy.30), calls=%async_computation | async-start | bytes 4194304 | tf_op jit(solution)/shard_map/cond/branch_1_fun/all_to_all | solution.py:174
  45.3 1.3 copy-start.4
  46.7 30.2 %all-to-all-start.3 = ((bf16[8,4,4,2,16,256]{5,4,3,2,1,0:T(8,128)(2,1)}), bf16[8,4,4,2,16,256]{5,4,3,2,1,0:T(8,128)(2,1)S(1)}, u32[]{:S(2)}, u32[]{:S(2)}) async-start(bf16[8,4,4,2,16,256]{5,4,3,2,1,0:T(8,128)(2,1)} %copy-done.4), calls=%async_computation.3 | async-start | bytes 4194304 | tf_op jit(solution)/shard_map/all_to_all | solution.py:174
  54.5 58.8 %collective-permute-start.2 = (bf16[4,2,256,256]{3,2,1,0:T(8,128)(2,1)}, bf16[4,2,256,256]{3,2,1,0:T(8,128)(2,1)}, u32[]{:S(2)}, u32[]{:S(2)}) collective-permute-start(bf16[4,2,256,256]{3,2,1,0:T(8,128)(2,1)} %collective-permute-done), channel_id=1, source_target_pairs={{0,8},{1,9},{2,10},{3,11},{4,12},{5,13},{6,14},{7,15},{8,0},{9,1},... | collective-permute-start | bytes 3145736 | tf_op jit(solution)/shard_map/ppermute | solution.py:186
  57.4 58.3 %collective-permute-start.7 = (bf16[8,4,2,16,256]{4,3,2,1,0:T(8,128)(2,1)}, bf16[8,4,2,16,256]{4,3,2,1,0:T(8,128)(2,1)S(1)}, u32[]{:S(2)}, u32[]{:S(2)}) collective-permute-start(bf16[8,4,2,16,256]{4,3,2,1,0:T(8,128)(2,1)} %get-tuple-element.123), channel_id=1, source_target_pairs={{0,24},{1,25},{2,26},{3,27},{4,28},{5,29},{6,30},{7,31},{8,16},{9,... | collective-permute-start | bytes 1572872 | tf_op jit(solution)/shard_map/ppermute | solution.py:186
  59.5 104.5 %collective-permute-start.5 = (bf16[8,4,2,16,256]{4,3,2,1,0:T(8,128)(2,1)}, bf16[8,4,2,16,256]{4,3,2,1,0:T(8,128)(2,1)}, u32[]{:S(2)}, u32[]{:S(2)}) collective-permute-start(bf16[8,4,2,16,256]{4,3,2,1,0:T(8,128)(2,1)} %get-tuple-element.124), channel_id=1, source_target_pairs={{0,16},{1,17},{2,18},{3,19},{4,20},{5,21},{6,22},{7,23},{8,24},{9,... | collective-permute-start | bytes 1572872 | tf_op jit(solution)/shard_map/ppermute | solution.py:186
  76.8 39.0 %copy-start.2 = (bf16[8,4,4,2,16,256]{5,4,3,2,1,0:T(8,128)(2,1)}, bf16[8,4,4,2,16,256]{5,4,3,2,1,0:T(8,128)(2,1)S(1)}, u32[]{:S(2)}) copy-start(bf16[8,4,4,2,16,256]{5,4,3,2,1,0:T(8,128)(2,1)S(1)} %all-to-all-done.3.refs_1_) | copy-start | bytes 6291460
  78.2 85.9 %collective-permute-start.8 = (bf16[8,4,2,16,256]{4,3,2,1,0:T(8,128)(2,1)}, bf16[8,4,2,16,256]{4,3,2,1,0:T(8,128)(2,1)}, u32[]{:S(2)}, u32[]{:S(2)}) collective-permute-start(bf16[8,4,2,16,256]{4,3,2,1,0:T(8,128)(2,1)} %get-tuple-element.120), channel_id=1, source_target_pairs={{0,24},{1,25},{2,26},{3,27},{4,28},{5,29},{6,30},{7,31},{8,16},{9,... | collective-permute-start | bytes 1572872 | tf_op jit(solution)/shard_map/ppermute | solution.py:186
  78.2 85.9 %collective-permute-start.6 = (bf16[8,4,2,16,256]{4,3,2,1,0:T(8,128)(2,1)}, bf16[8,4,2,16,256]{4,3,2,1,0:T(8,128)(2,1)}, u32[]{:S(2)}, u32[]{:S(2)}) collective-permute-start(bf16[8,4,2,16,256]{4,3,2,1,0:T(8,128)(2,1)} %get-tuple-element.121), channel_id=1, source_target_pairs={{0,16},{1,17},{2,18},{3,19},{4,20},{5,21},{6,22},{7,23},{8,24},{9,... | collective-permute-start | bytes 1572872 | tf_op jit(solution)/shard_map/ppermute | solution.py:186
  113.2 50.8 %collective-permute-start.3 = (bf16[8,4,2,16,256]{4,3,2,1,0:T(8,128)(2,1)}, bf16[8,4,2,16,256]{4,3,2,1,0:T(8,128)(2,1)}, u32[]{:S(2)}, u32[]{:S(2)}) collective-permute-start(bf16[8,4,2,16,256]{4,3,2,1,0:T(8,128)(2,1)} %get-tuple-element.77), channel_id=1, source_target_pairs={{0,8},{1,9},{2,10},{3,11},{4,12},{5,13},{6,14},{7,15},{8,0},{9,1},... | collective-permute-start | bytes 1572872 | tf_op jit(solution)/shard_map/ppermute | solution.py:186
  115.7 48.3 %collective-permute-start.4 = (bf16[8,4,2,16,256]{4,3,2,1,0:T(8,128)(2,1)}, bf16[8,4,2,16,256]{4,3,2,1,0:T(8,128)(2,1)}, u32[]{:S(2)}, u32[]{:S(2)}) collective-permute-start(bf16[8,4,2,16,256]{4,3,2,1,0:T(8,128)(2,1)} %get-tuple-element.78), channel_id=1, source_target_pairs={{0,8},{1,9},{2,10},{3,11},{4,12},{5,13},{6,14},{7,15},{8,0},{9,1},... | collective-permute-start | bytes 1572872 | tf_op jit(solution)/shard_map/ppermute | solution.py:186
  119.2 29.2 %copy-start.3 = (bf16[8,2,2,4,2,16,256]{6,5,4,3,2,1,0:T(8,128)(2,1)S(1)}, bf16[8,2,2,4,2,16,256]{6,5,4,3,2,1,0:T(8,128)(2,1)}, u32[]{:S(2)}) copy-start(bf16[8,2,2,4,2,16,256]{6,5,4,3,2,1,0:T(8,128)(2,1)} %get-tuple-element.37.same_ref) | copy-start | bytes 6291460 | tf_op jit(solution)/shard_map/cond
  148.8 1.3 copy-start.1
  157.6 1.3 copy-start

commit v8 on v7

--- a/solution.py
+++ b/solution.py
@@ -116,33 +116,35 @@
 def weight_grad_kernel(layer_ref, *refs):
     *pairs, mask_ref, out_ref = refs
 
-    def rows(ref, c):
-        return ref[..., c, :, :].reshape(-1, ref.shape[-1])
-
-    x = jnp.concatenate([rows(ref, c) for ref in pairs[::2] for c in range(2)])
-    g = [(rows(ref, 0), rows(ref, 1)) for ref in pairs[1::2]]
-    mask = mask_ref[0].astype(F32)
-    out_ref[0, 0] = dot(x, jnp.concatenate([part for real, imag in g for part in (real, imag)]), TN) * mask
-    out_ref[0, 1] = dot(x, jnp.concatenate([part for real, imag in g for part in (imag, -real)]), TN) * mask
+    def rows(ref, j, c):
+        return ref[..., j, c, :, :].reshape(-1, ref.shape[-1])
+
+    for j in range(out_ref.shape[0]):
+        x = jnp.concatenate([rows(ref, j, c) for ref in pairs[::2] for c in range(2)])
+        g = [(rows(ref, j, 0), rows(ref, j, 1)) for ref in pairs[1::2]]
+        mask = mask_ref[j].astype(F32)
+        out_ref[j, 0] = dot(x, jnp.concatenate([part for real, imag in g for part in (real, imag)]), TN) * mask
+        out_ref[j, 1] = dot(x, jnp.concatenate([part for real, imag in g for part in (imag, -real)]), TN) * mask
 
 
 def weight_grad(layer, x, g, pairs, mask):
     inner, _, modes, _, samples, ci = x.shape
     co = g.shape[-1]
+    some = 2 if modes % 2 == 0 else 1
 
     def own(channels):
-        return pl.BlockSpec((inner, 1, 1, 2, samples, channels), lambda j, layer: (0, layer[0], j, 0, 0, 0))
+        return pl.BlockSpec((inner, 1, some, 2, samples, channels), lambda j, layer: (0, layer[0], j, 0, 0, 0))
 
     def block(channels):
-        return pl.BlockSpec((inner, 1, 2, samples, channels), lambda j, layer: (0, j, 0, 0, 0))
+        return pl.BlockSpec((inner, some, 2, samples, channels), lambda j, layer: (0, j, 0, 0, 0))
 
     return pl.pallas_call(
         weight_grad_kernel,
         grid_spec=pltpu.PrefetchScalarGridSpec(
             num_scalar_prefetch=1,
-            grid=(modes,),
-            in_specs=[own(ci), own(co), *[block(ci), block(co)] * len(pairs), pl.BlockSpec((1, ci, co), lambda j, layer: (j, 0, 0))],
-            out_specs=pl.BlockSpec((1, 2, ci, co), lambda j, layer: (j, 0, 0, 0)),
+            grid=(modes // some,),
+            in_specs=[own(ci), own(co), *[block(ci), block(co)] * len(pairs), pl.BlockSpec((some, ci, co), lambda j, layer: (j, 0, 0))],
+            out_specs=pl.BlockSpec((some, 2, ci, co), lambda j, layer: (j, 0, 0, 0)),
         ),
         out_shape=jax.ShapeDtypeStruct((modes, 2, ci, co), F32),
         compiler_params=pltpu.CompilerParams(vmem_limit_bytes=40 * 1024 * 1024),

time: 170 us -> 169 us (level)
  no operation moved by 1% of the time
where the time goes in v8:
time: 169 us; the launch traced here: 168 us
  blocking collectives  58.9 us (35%)
  waiting for transfers between devices  41.9 us (25%)
  local copies, waits for them, and re-layouts  29.5 us (17%)
  starting transfers between devices  21.6 us (13%)
  Pallas kernels  13.4 us (8%)
  other arithmetic  1.85 us (1%)
    all_to_all x2, blocking collectives, exchange(): return lax.all_to_all(a, 'blk', 0, 0, tiled=True, axis_index_groups=layers)  58.9 us
    all_to_all x2, waiting for transfers between devices, exchange(): return lax.all_to_all(a, 'blk', 0, 0, tiled=True, axis_index_groups=layers)  37.7 us
    ppermute x9, starting transfers between devices, send(): return lax.ppermute(a, 'blk', [(i, i ^ step * inner) for i in range(ranks)])  13.6 us
    reshape x2, local copies, waits for them, and re-layouts, to_samples(): turned.reshape(ranks * modes, *turned.shape[3:]).transpose(3, 1, 2, 0)  10.3 us
    all_to_all x2, starting transfers between devices, exchange(): return lax.all_to_all(a, 'blk', 0, 0, tiled=True, axis_index_groups=layers)  8.08 us
    another operation x2, local copies, waits for them, and re-layouts  7.37 us
    pallas_call x2, Pallas kernels, mix(): pl.pallas_call(mix_kernel, grid_spec=pltpu.PrefetchScalarGridSpec(num_sca...  6.77 us
    ppermute x9, waiting for transfers between devices, send(): return lax.ppermute(a, 'blk', [(i, i ^ step * inner) for i in range(ranks)])  4.21 us
  transfers between devices with their start and end apart: 11, of which 4 were waited for; matrix products, arithmetic and copies ran while one was open for 15% of the time, Pallas kernels for 6%

profile of v8, /device:TPU:0, one launch (start us, length us, event | category | flops | bytes accessed | tf_op | source)
XLA Modules:
  0.0 168.0 jit_solution(1458303352047528422)
XLA Ops:
  0.6 0.0 copy-start.6
  0.6 0.8 convert_element_type.9
  1.4 0.1 copy.35
  1.6 0.1 broadcast_in_dim.7
  1.6 0.1 reshape.28
  1.8 0.2 copy.36.refs_8_
  2.0 0.0 copy-done.6
  2.0 1.1 broadcast_multiply_fusion
  3.1 3.0 %collective-permute-start.1 = (bf16[4,2,256,256]{3,2,1,0:T(8,128)(2,1)}, bf16[4,2,256,256]{3,2,1,0:T(8,128)(2,1)}, u32[]{:S(2)}, u32[]{:S(2)}) collective-permute-start(bf16[4,2,256,256]{3,2,1,0:T(8,128)(2,1)} %broadcast_multiply_fusion), channel_id=1, source_target_pairs={{0,8},{1,9},{2,10},{3,11},{4,12},{5,13},{6,14},{7,15},{8,0},{9,1},... | collective-permute-start | bytes 3145736 | tf_op jit(solution)/shard_map/ppermute | solution.py:188
  6.1 2.6 %collective-permute-start = (bf16[4,2,256,256]{3,2,1,0:T(8,128)(2,1)}, bf16[4,2,256,256]{3,2,1,0:T(8,128)(2,1)}, u32[]{:S(2)}, u32[]{:S(2)}) collective-permute-start(bf16[4,2,256,256]{3,2,1,0:T(8,128)(2,1)} %broadcast_multiply_fusion), channel_id=1, source_target_pairs={{0,16},{1,17},{2,18},{3,19},{4,20},{5,21},{6,22},{7,23},{8,24},{9,... | collective-permute-start | bytes 3145736 | tf_op jit(solution)/shard_map/ppermute | solution.py:188
  8.7 36.7 %conditional.3 = (bf16[8,4,4,2,16,256]{5,4,3,2,1,0:T(8,128)(2,1)}, bf16[8,4,4,2,16,256]{5,4,3,2,1,0:T(8,128)(2,1)S(1)}) conditional(s32[]{:T(128)} %convert_element_type.8, () %tuple.35, (bf16[256,2,16,128]{3,2,1,0:T(8,128)(2,1)}, bf16[256,2,16,128]{3,2,1,0:T(8,128)(2,1)}) %tuple.36), branch_computations={%region_0.1_spmd, %region_1.2_spmd} | conditional | bytes 31457356 | solution.py:157
  8.7 3.9 %copy.33 = bf16[256,2,16,128]{0,2,1,3:T(8,128)(2,1)S(1)} copy(bf16[256,2,16,128]{3,2,1,0:T(8,128)(2,1)} %get-tuple-element.117) | data formatting | bytes 4194304 | tf_op jit(solution)/shard_map
  12.6 1.6 copy.30
  14.2 0.0 copy-start.5
  14.2 4.5 %all-to-all-start = ((bf16[8,4,4,2,16,256]{5,4,3,2,1,0:T(8,128)(2,1)}), bf16[8,4,4,2,16,256]{5,4,3,2,1,0:T(8,128)(2,1)}, u32[]{:S(2)}, u32[]{:S(2)}) async-start(bf16[8,4,4,2,16,256]{5,4,3,2,1,0:T(8,128)(2,1)} %copy.30), calls=%async_computation | async-start | bytes 4194304 | tf_op jit(solution)/shard_map/cond/branch_1_fun/all_to_all | solution.py:176
  18.7 0.0 copy-done.5
  18.7 3.5 %copy.34 = bf16[256,2,16,128]{0,2,1,3:T(8,128)(2,1)} copy(bf16[256,2,16,128]{3,2,1,0:T(8,128)(2,1)S(1)} %copy-done.5) | data formatting | bytes 4194304 | tf_op jit(solution)/shard_map
  22.1 1.9 %copy.40 = bf16[8,4,4,2,16,256]{5,4,3,2,1,0:T(8,128)(2,1)S(1)} copy(bf16[8,4,4,2,16,256]{5,4,3,2,0,1:T(8,128)(2,1)} %bitcast.33) | data formatting | bytes 4194304 | tf_op jit(solution)/shard_map/cond | solution.py:157
  24.0 21.3 %all-to-all-done = bf16[8,4,4,2,16,256]{5,4,3,2,1,0:T(8,128)(2,1)} async-done(((bf16[8,4,4,2,16,256]{5,4,3,2,1,0:T(8,128)(2,1)}), bf16[8,4,4,2,16,256]{5,4,3,2,1,0:T(8,128)(2,1)}, u32[]{:S(2)}, u32[]{:S(2)}) %all-to-all-start) | async-done | bytes 2097184 | tf_op jit(solution)/shard_map/cond/branch_1_fun/all_to_all | solution.py:176
  45.3 0.0 copy-start.4
  45.3 1.3 copy-done.4
  46.7 3.6 %all-to-all-start.3 = ((bf16[8,4,4,2,16,256]{5,4,3,2,1,0:T(8,128)(2,1)}), bf16[8,4,4,2,16,256]{5,4,3,2,1,0:T(8,128)(2,1)S(1)}, u32[]{:S(2)}, u32[]{:S(2)}) async-start(bf16[8,4,4,2,16,256]{5,4,3,2,1,0:T(8,128)(2,1)} %copy-done.4), calls=%async_computation.3 | async-start | bytes 4194304 | tf_op jit(solution)/shard_map/all_to_all | solution.py:176
  50.3 1.6 collective-permute-done.1
  51.9 2.6 %collective-permute-done = bf16[4,2,256,256]{3,2,1,0:T(8,128)(2,1)} collective-permute-done((bf16[4,2,256,256]{3,2,1,0:T(8,128)(2,1)}, bf16[4,2,256,256]{3,2,1,0:T(8,128)(2,1)}, u32[]{:S(2)}, u32[]{:S(2)}) %collective-permute-start) | collective-permute-done | bytes 1048608 | tf_op jit(solution)/shard_map/ppermute | solution.py:188
  54.5 0.4 collective-permute-start.2
  54.9 2.6 %dynamic-slice_bitcast_fusion.1 = (bf16[8,4,2,16,256]{4,3,2,1,0:T(8,128)(2,1)}, bf16[8,4,2,16,256]{4,3,2,1,0:T(8,128)(2,1)}, bf16[8,4,2,16,256]{4,3,2,1,0:T(8,128)(2,1)}) fusion(bf16[8,4,4,2,16,256]{5,4,3,2,1,0:T(8,128)(2,1)} %get-tuple-element.67.refs_0_, s32[]{:T(128)S(6)} %select_n.22, s32[]{:T(128)S(6)} %select_n.21, s32[]{:T(128)S(6)} %select_n.20), kind=kLoop, calls=%fused_computation.1 | loop fusion | bytes 3145740 | tf_op jit(solution)/shard_map/jit(dynamic_index_in_dim)/squeeze | solution.py:191
  57.4 2.1 %collective-permute-start.7 = (bf16[8,4,2,16,256]{4,3,2,1,0:T(8,128)(2,1)}, bf16[8,4,2,16,256]{4,3,2,1,0:T(8,128)(2,1)S(1)}, u32[]{:S(2)}, u32[]{:S(2)}) collective-permute-start(bf16[8,4,2,16,256]{4,3,2,1,0:T(8,128)(2,1)} %get-tuple-element.123), channel_id=1, source_target_pairs={{0,24},{1,25},{2,26},{3,27},{4,28},{5,29},{6,30},{7,31},{8,16},{9,... | collective-permute-start | bytes 1572872 | tf_op jit(solution)/shard_map/ppermute | solution.py:188
  59.5 1.0 collective-permute-start.5
  60.5 16.3 %all-to-all-done.3.refs_1_ = bf16[8,4,4,2,16,256]{5,4,3,2,1,0:T(8,128)(2,1)S(1)} async-done(((bf16[8,4,4,2,16,256]{5,4,3,2,1,0:T(8,128)(2,1)}), bf16[8,4,4,2,16,256]{5,4,3,2,1,0:T(8,128)(2,1)S(1)}, u32[]{:S(2)}, u32[]{:S(2)}) %all-to-all-start.3) | async-done | bytes 2097184 | tf_op jit(solution)/shard_map/all_to_all | solution.py:176
  76.8 0.0 copy-start.2
  76.8 1.3 dynamic-slice_bitcast_fusion
  78.2 0.0 collective-permute-start.8
  78.2 1.9 %collective-permute-start.6 = (bf16[8,4,2,16,256]{4,3,2,1,0:T(8,128)(2,1)}, bf16[8,4,2,16,256]{4,3,2,1,0:T(8,128)(2,1)}, u32[]{:S(2)}, u32[]{:S(2)}) collective-permute-start(bf16[8,4,2,16,256]{4,3,2,1,0:T(8,128)(2,1)} %get-tuple-element.121), channel_id=1, source_target_pairs={{0,16},{1,17},{2,18},{3,19},{4,20},{5,21},{6,22},{7,23},{8,24},{9,... | collective-permute-start | bytes 1572872 | tf_op jit(solution)/shard_map/ppermute | solution.py:188
  80.1 33.2 %conditional.4 = (bf16[8,2,2,4,2,16,256]{6,5,4,3,2,1,0:T(8,128)(2,1)}) conditional(s32[]{:T(128)} %convert_element_type.8, () %tuple.39, (s32[1]{0:T(128)}, bf16[8,4,4,2,16,256]{5,4,3,2,1,0:T(8,128)(2,1)}, bf16[8,4,4,2,16,256]{5,4,3,2,1,0:T(8,128)(2,1)S(1)}, bf16[4,2,256,256]{3,2,1,0:T(8,128)(2,1)}, bf16[4,2,256,256]{3,2,1,0:T(8,128)(2,1)}) %tuple.40), branch_computations={%region_2.3_spmd, %region_3.4_spmd} | conditional | bytes 4194312 | solution.py:157
  80.1 3.4 %mix.2 = bf16[8,2,2,4,2,16,256]{6,5,4,3,2,1,0:T(8,128)(2,1)S(1)} custom-call(s32[1]{0:T(128)} %get-tuple-element.31.layer_ref, bf16[8,4,4,2,16,256]{5,4,3,2,1,0:T(8,128)(2,1)} %get-tuple-element.32.x_ref, bf16[8,4,4,2,16,256]{5,4,3,2,1,0:T(8,128)(2,1)S(1)} %get-tuple-element.33.g_ref, bf16[4,2,256,256]{3,2,1,0:T(8,128)(2,1)} %get-tuple-element.34.same_ref, ...), custom_call_target="tpu_custom_call" | custom-call | tf_op jit(solution)/shard_map/cond/branch_1_fun/mix/pallas_call | solution.py:71
  83.5 29.8 %all_to_all.17 = bf16[8,2,2,4,2,16,256]{6,5,4,3,2,1,0:T(8,128)(2,1)} all-to-all(bf16[8,2,2,4,2,16,256]{6,5,4,3,2,1,0:T(8,128)(2,1)S(1)} %mix.2), channel_id=1, replica_groups={{0,1,2,3,4,5,6,7},{8,9,10,11,12,13,14,15},{16,17,18,19,20,21,22,23},{24..., dimensions={0} | all-to-all | bytes 4194304 | tf_op jit(solution)/shard_map/cond/branch_1_fun/all_to_all | solution.py:176
  113.2 0.0 collective-permute-done.2
  113.2 2.5 %collective-permute-start.3 = (bf16[8,4,2,16,256]{4,3,2,1,0:T(8,128)(2,1)}, bf16[8,4,2,16,256]{4,3,2,1,0:T(8,128)(2,1)}, u32[]{:S(2)}, u32[]{:S(2)}) collective-permute-start(bf16[8,4,2,16,256]{4,3,2,1,0:T(8,128)(2,1)} %get-tuple-element.77), channel_id=1, source_target_pairs={{0,8},{1,9},{2,10},{3,11},{4,12},{5,13},{6,14},{7,15},{8,0},{9,1},... | collective-permute-start | bytes 1572872 | tf_op jit(solution)/shard_map/ppermute | solution.py:188
  115.7 0.0 collective-permute-done.7.refs_6_
  115.7 0.1 collective-permute-start.4
  115.8 0.0 copy-done.2
  115.8 48.2 %conditional.5 = (bf16[256,2,16,128]{3,2,1,0:T(8,128)(2,1)}, bf16[256,2,16,128]{3,2,1,0:T(8,128)(2,1)}) conditional(s32[]{:T(128)} %convert_element_type.8, () %tuple.34, (s32[1]{0:T(128)}, bf16[8,4,4,2,16,256]{5,4,3,2,1,0:T(8,128)(2,1)}, bf16[8,4,4,2,16,256]{5,4,3,2,1,0:T(8,128)(2,1)S(1)}, bf16[4,2,256,256]{3,2,1,0:T(8,128)(2,1)}, ...), branch_computations={%region_4.5_spmd, %region_5.6_spmd} | conditional | bytes 37748836 | solution.py:157
  115.8 3.4 %mix.3 = bf16[8,2,2,4,2,16,256]{6,5,4,3,2,1,0:T(8,128)(2,1)S(1)} custom-call(s32[1]{0:T(128)} %get-tuple-element.36.layer_ref, bf16[8,4,4,2,16,256]{5,4,3,2,1,0:T(8,128)(2,1)} %get-tuple-element.38.x_ref, bf16[8,4,4,2,16,256]{5,4,3,2,1,0:T(8,128)(2,1)S(1)} %get-tuple-element.39.g_ref, bf16[4,2,256,256]{3,2,1,0:T(8,128)(2,1)} %get-tuple-element.40.same_ref, ...), custom_call_target="tpu_custom_call" | custom-call | tf_op jit(solution)/shard_map/cond/branch_1_fun/mix/pallas_call | solution.py:71
  119.2 0.0 copy-start.3
  119.2 29.2 %all_to_all.18.other_ref = bf16[8,2,2,4,2,16,256]{6,5,4,3,2,1,0:T(8,128)(2,1)S(1)} all-to-all(bf16[8,2,2,4,2,16,256]{6,5,4,3,2,1,0:T(8,128)(2,1)S(1)} %mix.3), channel_id=1, replica_groups={{0,1,2,3,4,5,6,7},{8,9,10,11,12,13,14,15},{16,17,18,19,20,21,22,23},{24..., dimensions={0} | all-to-all | bytes 4194304 | tf_op jit(solution)/shard_map/cond/branch_1_fun/all_to_all | solution.py:176
  148.4 0.0 copy-done.3
  148.4 0.4 gather.2
  148.8 0.0 copy-start.1
  148.8 1.3 copy-done.1
  150.1 5.1 %copy.31 = bf16[128,2,16,256]{0,2,1,3:T(8,128)(2,1)} copy(bf16[128,2,16,256]{3,2,1,0:T(8,128)(2,1)} %bitcast.31) | data formatting | bytes 4194304 | tf_op jit(solution)/shard_map/cond/branch_1_fun/reshape | solution.py:184
  155.3 2.3 %gather.3 = bf16[4,8,4,2,16,256]{5,4,3,2,1,0:T(8,128)(2,1)S(1)} custom-call(s32[1]{0:T(128)} %get-tuple-element.36.layer_ref, bf16[8,2,2,4,2,16,256]{6,5,4,3,2,1,0:T(8,128)(2,1)} %get-tuple-element.37.same_ref, bf16[8,2,2,4,2,16,256]{6,5,4,3,2,1,0:T(8,128)(2,1)S(1)} %all_to_all.18.other_ref), custom_call_target="tpu_custom_call" | custom-call | tf_op jit(solution)/shard_map/cond/branch_1_fun/gather/pallas_call | solution.py:102
  157.6 0.0 copy-start
  157.6 1.3 copy-done
  158.9 5.1 %copy.32 = bf16[128,2,16,256]{0,2,1,3:T(8,128)(2,1)} copy(bf16[128,2,16,256]{3,2,1,0:T(8,128)(2,1)} %bitcast.30) | data formatting | bytes 4194304 | tf_op jit(solution)/shard_map/cond/branch_1_fun/reshape | solution.py:184
  164.0 0.0 collective-permute-done.5.refs_4_
  164.0 0.0 collective-permute-done.8.refs_7_
  164.0 0.0 collective-permute-done.6.refs_5_
  164.0 0.0 collective-permute-done.3.refs_2_
  164.0 0.0 collective-permute-done.4.refs_3_
  164.1 4.0 %weight_grad.1 = f32[4,2,256,256]{3,2,1,0:T(8,128)} custom-call(s32[1]{0:T(128)} %bitcast.14.layer_ref, bf16[8,4,4,2,16,256]{5,4,3,2,1,0:T(8,128)(2,1)} %get-tuple-element.67.refs_0_, bf16[8,4,4,2,16,256]{5,4,3,2,1,0:T(8,128)(2,1)} %copy-done.2, bf16[8,4,2,16,256]{4,3,2,1,0:T(8,128)(2,1)} %collective-permute-done.3.refs_2_, ...), custom_call_target="tpu_custom_call" | custom-call | tf_op jit(solution)/shard_map/weight_grad/pallas_call | solution.py:141
  (1 shorter events, 0.0 us)
Async XLA Ops:
  0.6 1.4 copy-start.6
  3.1 48.8 %collective-permute-start.1 = (bf16[4,2,256,256]{3,2,1,0:T(8,128)(2,1)}, bf16[4,2,256,256]{3,2,1,0:T(8,128)(2,1)}, u32[]{:S(2)}, u32[]{:S(2)}) collective-permute-start(bf16[4,2,256,256]{3,2,1,0:T(8,128)(2,1)} %broadcast_multiply_fusion), channel_id=1, source_target_pairs={{0,8},{1,9},{2,10},{3,11},{4,12},{5,13},{6,14},{7,15},{8,0},{9,1},... | collective-permute-start | bytes 3145736 | tf_op jit(solution)/shard_map/ppermute | solution.py:188
  6.1 48.4 %collective-permute-start = (bf16[4,2,256,256]{3,2,1,0:T(8,128)(2,1)}, bf16[4,2,256,256]{3,2,1,0:T(8,128)(2,1)}, u32[]{:S(2)}, u32[]{:S(2)}) collective-permute-start(bf16[4,2,256,256]{3,2,1,0:T(8,128)(2,1)} %broadcast_multiply_fusion), channel_id=1, source_target_pairs={{0,16},{1,17},{2,18},{3,19},{4,20},{5,21},{6,22},{7,23},{8,24},{9,... | collective-permute-start | bytes 3145736 | tf_op jit(solution)/shard_map/ppermute | solution.py:188
  14.2 4.5 %copy-start.5 = (bf16[256,2,16,128]{3,2,1,0:T(8,128)(2,1)S(1)}, bf16[256,2,16,128]{3,2,1,0:T(8,128)(2,1)}, u32[]{:S(2)}) copy-start(bf16[256,2,16,128]{3,2,1,0:T(8,128)(2,1)} %get-tuple-element.118) | copy-start | bytes 6291460 | tf_op jit(solution)/shard_map/cond
  14.2 31.1 %all-to-all-start = ((bf16[8,4,4,2,16,256]{5,4,3,2,1,0:T(8,128)(2,1)}), bf16[8,4,4,2,16,256]{5,4,3,2,1,0:T(8,128)(2,1)}, u32[]{:S(2)}, u32[]{:S(2)}) async-start(bf16[8,4,4,2,16,256]{5,4,3,2,1,0:T(8,128)(2,1)} %copy.30), calls=%async_computation | async-start | bytes 4194304 | tf_op jit(solution)/shard_map/cond/branch_1_fun/all_to_all | solution.py:176
  45.3 1.3 copy-start.4
  46.7 30.2 %all-to-all-start.3 = ((bf16[8,4,4,2,16,256]{5,4,3,2,1,0:T(8,128)(2,1)}), bf16[8,4,4,2,16,256]{5,4,3,2,1,0:T(8,128)(2,1)S(1)}, u32[]{:S(2)}, u32[]{:S(2)}) async-start(bf16[8,4,4,2,16,256]{5,4,3,2,1,0:T(8,128)(2,1)} %copy-done.4), calls=%async_computation.3 | async-start | bytes 4194304 | tf_op jit(solution)/shard_map/all_to_all | solution.py:176
  54.5 58.8 %collective-permute-start.2 = (bf16[4,2,256,256]{3,2,1,0:T(8,128)(2,1)}, bf16[4,2,256,256]{3,2,1,0:T(8,128)(2,1)}, u32[]{:S(2)}, u32[]{:S(2)}) collective-permute-start(bf16[4,2,256,256]{3,2,1,0:T(8,128)(2,1)} %collective-permute-done), channel_id=1, source_target_pairs={{0,8},{1,9},{2,10},{3,11},{4,12},{5,13},{6,14},{7,15},{8,0},{9,1},... | collective-permute-start | bytes 3145736 | tf_op jit(solution)/shard_map/ppermute | solution.py:188
  57.4 58.3 %collective-permute-start.7 = (bf16[8,4,2,16,256]{4,3,2,1,0:T(8,128)(2,1)}, bf16[8,4,2,16,256]{4,3,2,1,0:T(8,128)(2,1)S(1)}, u32[]{:S(2)}, u32[]{:S(2)}) collective-permute-start(bf16[8,4,2,16,256]{4,3,2,1,0:T(8,128)(2,1)} %get-tuple-element.123), channel_id=1, source_target_pairs={{0,24},{1,25},{2,26},{3,27},{4,28},{5,29},{6,30},{7,31},{8,16},{9,... | collective-permute-start | bytes 1572872 | tf_op jit(solution)/shard_map/ppermute | solution.py:188
  59.5 104.5 %collective-permute-start.5 = (bf16[8,4,2,16,256]{4,3,2,1,0:T(8,128)(2,1)}, bf16[8,4,2,16,256]{4,3,2,1,0:T(8,128)(2,1)}, u32[]{:S(2)}, u32[]{:S(2)}) collective-permute-start(bf16[8,4,2,16,256]{4,3,2,1,0:T(8,128)(2,1)} %get-tuple-element.124), channel_id=1, source_target_pairs={{0,16},{1,17},{2,18},{3,19},{4,20},{5,21},{6,22},{7,23},{8,24},{9,... | collective-permute-start | bytes 1572872 | tf_op jit(solution)/shard_map/ppermute | solution.py:188
  76.8 39.0 %copy-start.2 = (bf16[8,4,4,2,16,256]{5,4,3,2,1,0:T(8,128)(2,1)}, bf16[8,4,4,2,16,256]{5,4,3,2,1,0:T(8,128)(2,1)S(1)}, u32[]{:S(2)}) copy-start(bf16[8,4,4,2,16,256]{5,4,3,2,1,0:T(8,128)(2,1)S(1)} %all-to-all-done.3.refs_1_) | copy-start | bytes 6291460
  78.2 85.9 %collective-permute-start.8 = (bf16[8,4,2,16,256]{4,3,2,1,0:T(8,128)(2,1)}, bf16[8,4,2,16,256]{4,3,2,1,0:T(8,128)(2,1)}, u32[]{:S(2)}, u32[]{:S(2)}) collective-permute-start(bf16[8,4,2,16,256]{4,3,2,1,0:T(8,128)(2,1)} %get-tuple-element.120), channel_id=1, source_target_pairs={{0,24},{1,25},{2,26},{3,27},{4,28},{5,29},{6,30},{7,31},{8,16},{9,... | collective-permute-start | bytes 1572872 | tf_op jit(solution)/shard_map/ppermute | solution.py:188
  78.2 85.9 %collective-permute-start.6 = (bf16[8,4,2,16,256]{4,3,2,1,0:T(8,128)(2,1)}, bf16[8,4,2,16,256]{4,3,2,1,0:T(8,128)(2,1)}, u32[]{:S(2)}, u32[]{:S(2)}) collective-permute-start(bf16[8,4,2,16,256]{4,3,2,1,0:T(8,128)(2,1)} %get-tuple-element.121), channel_id=1, source_target_pairs={{0,16},{1,17},{2,18},{3,19},{4,20},{5,21},{6,22},{7,23},{8,24},{9,... | collective-permute-start | bytes 1572872 | tf_op jit(solution)/shard_map/ppermute | solution.py:188
  113.2 50.8 %collective-permute-start.3 = (bf16[8,4,2,16,256]{4,3,2,1,0:T(8,128)(2,1)}, bf16[8,4,2,16,256]{4,3,2,1,0:T(8,128)(2,1)}, u32[]{:S(2)}, u32[]{:S(2)}) collective-permute-start(bf16[8,4,2,16,256]{4,3,2,1,0:T(8,128)(2,1)} %get-tuple-element.77), channel_id=1, source_target_pairs={{0,8},{1,9},{2,10},{3,11},{4,12},{5,13},{6,14},{7,15},{8,0},{9,1},... | collective-permute-start | bytes 1572872 | tf_op jit(solution)/shard_map/ppermute | solution.py:188
  115.7 48.3 %collective-permute-start.4 = (bf16[8,4,2,16,256]{4,3,2,1,0:T(8,128)(2,1)}, bf16[8,4,2,16,256]{4,3,2,1,0:T(8,128)(2,1)}, u32[]{:S(2)}, u32[]{:S(2)}) collective-permute-start(bf16[8,4,2,16,256]{4,3,2,1,0:T(8,128)(2,1)} %get-tuple-element.78), channel_id=1, source_target_pairs={{0,8},{1,9},{2,10},{3,11},{4,12},{5,13},{6,14},{7,15},{8,0},{9,1},... | collective-permute-start | bytes 1572872 | tf_op jit(solution)/shard_map/ppermute | solution.py:188
  119.2 29.2 %copy-start.3 = (bf16[8,2,2,4,2,16,256]{6,5,4,3,2,1,0:T(8,128)(2,1)S(1)}, bf16[8,2,2,4,2,16,256]{6,5,4,3,2,1,0:T(8,128)(2,1)}, u32[]{:S(2)}) copy-start(bf16[8,2,2,4,2,16,256]{6,5,4,3,2,1,0:T(8,128)(2,1)} %get-tuple-element.37.same_ref) | copy-start | bytes 6291460 | tf_op jit(solution)/shard_map/cond
  148.8 1.3 copy-start.1
  157.6 1.3 copy-start
